TPU v7x, 128 devices: a whole 4x4x4 slice. The times are simulated.
128 devices in a mesh: row: 16 (over z, x), col: 8 (over y, core).
Axes of the slice: x: 4, y: 4, z: 4, core: 2. Of those that a mesh axis runs over, the one named last changes fastest.
Arguments:
- alignment_tensor: bfloat16 [1024, 32768], P('row', 'col'), may hold values from -20 to 20
- supplement_align_cover: int32 [1024, 512], P('row', 'col'), may hold values from 0 to 1, as said below
- couple_tensor: float32 [512, 512, 128], P('row', 'col'), may hold values from -6 to 6
- couple_cover_grid: int32 [512, 512], P('row', 'col'), may hold values 0 or 1
- amino_strand_label: int32 [512], replicated, may hold values from 0 to 3, never falling along the last dimension, each value on 1 to 256 neighbouring positions
- focus_scaling_vector: float32 [64], replicated, may hold values from 0.5 to 12
- focus_asking_factor: bfloat16 [64, 64], replicated, may hold values from -0.75 to 0.75
- focus_lookup_factor: bfloat16 [64, 8], replicated, may hold values from -0.75 to 0.75
- focus_content_factor: bfloat16 [64, 8], replicated, may hold values from -0.75 to 0.75
- focus_sigmoid_factor: bfloat16 [64, 64], replicated, may hold values from -0.75 to 0.75
- focus_final_factor: bfloat16 [64, 64], replicated, may hold values from -0.75 to 0.75
- dyadic_scaling_vector: float32 [64], replicated, may hold values from 0.5 to 1.5
- dyadic_first_factor: bfloat16 [64, 32], replicated, may hold values from -0.75 to 0.75
- dyadic_second_factor: bfloat16 [64, 32], replicated, may hold values from -0.75 to 0.75
- dyadic_final_factor: bfloat16 [1024, 128], replicated, may hold values from -1 to 1
- strand_couple_table: float32 [2, 128], replicated, may hold values from -4 to 4
- trio_source_scaling: float32 [128], replicated, may hold values from 0.5 to 1.5
- trio_mapping_factors: bfloat16 [128, 512], replicated, may hold values from -0.5 to 0.5
- trio_sigmoid_factor: bfloat16 [128, 128], replicated, may hold values from -0.5 to 0.5
- trio_middle_scaling: float32 [128], replicated, may hold values from 0.5 to 1.5
- trio_final_factor: bfloat16 [128, 128], replicated, may hold values from -0.5 to 0.5
Outputs:
- refreshed_supplement_align: bfloat16 [1024, 32768], P('row', 'col')
- refreshed_couple_tensor: float32 [512, 512, 128], P('row', 'col')
Inputs may be any that keep to these rules, and one draw needn't show every extreme that they name: `supplement_align_cover`: a trailing run of residues is 0 in every sequence.
All inputs are finite; a program needn't handle non-finite values. No bound on the sum of `couple_cover_grid` on one device may be relied on, other than what follows from the above.
Results may differ from a plain program's by a relative error of at most 0.0072.
Values may be sent and summed in bfloat16 or wider, within the bound.
No kernel may reach another device: no remote copies, remote signals or barrier semaphores. Data moves between devices by JAX's collectives and lax.ppermute only.
A program may use at most 128 MiB of HBM per device.

v0:
```python
import jax
import jax.numpy as jnp
from jax import lax
from jax.sharding import PartitionSpec as P


def broadcast(shard, axis, root):
    mine = lax.axis_index(axis) == root
    return lax.psum(jnp.where(mine, shard, jnp.zeros_like(shard)), axis)


def standardize_features(x, gain):
    mean = jnp.mean(x, -1, keepdims=True)
    centred = x - mean
    var = jnp.mean(centred * centred, -1, keepdims=True)
    return centred * lax.rsqrt(var + 1e-05) * gain


def contract_first(left, right):
    return lax.dot_general(
        left, right, (((0,), (0,)), ((), ())), preferred_element_type=jnp.float32
    )


def row_block(left_all, mask_all, ratio, block_rows, channels):
    row_pos = lax.axis_index("row")
    half = row_pos % ratio
    sub_left = lax.dynamic_slice_in_dim(
        left_all, half * block_rows * channels, block_rows * channels, 1
    )
    sub_mask = lax.dynamic_slice_in_dim(mask_all, half * block_rows, block_rows, 1)
    return (
        broadcast(sub_left, "col", row_pos // ratio),
        broadcast(sub_mask, "col", row_pos // ratio),
    )


def local(
    alignment_tensor,
    supplement_align_cover,
    couple_tensor,
    couple_cover_grid,
    amino_strand_label,
    focus_scaling_vector,
    focus_asking_factor,
    focus_lookup_factor,
    focus_content_factor,
    focus_sigmoid_factor,
    focus_final_factor,
    dyadic_scaling_vector,
    dyadic_first_factor,
    dyadic_second_factor,
    dyadic_final_factor,
    strand_couple_table,
    trio_source_scaling,
    trio_mapping_factors,
    trio_sigmoid_factor,
    trio_middle_scaling,
    trio_final_factor,
):
    hi = lax.Precision.HIGHEST
    n_row = lax.axis_size("row")
    n_col = lax.axis_size("col")
    ratio = n_row // n_col
    alignments_each_device, vertical_aminos = supplement_align_cover.shape
    rows_res = couple_tensor.shape[0]
    align_feature_length = focus_scaling_vector.shape[0]
    head_dim = focus_lookup_factor.shape[1]
    heads = focus_asking_factor.shape[1] // head_dim
    width_o = dyadic_first_factor.shape[1]
    width_z = couple_tensor.shape[2]
    width_t = trio_final_factor.shape[0]
    split_cover_lines = supplement_align_cover.astype(jnp.bfloat16)
    dispatched, sent_mask = (
        lax.all_to_all(alignment_tensor, "row", split_axis=1, concat_axis=0, tiled=True),
        lax.all_to_all(split_cover_lines, "row", split_axis=1, concat_axis=0, tiled=True),
    )
    alignments_total, amino_swap = sent_mask.shape
    align_verticals = dispatched.reshape(alignments_total, amino_swap, align_feature_length).astype(
        jnp.float32
    )
    covered_contents = sent_mask.astype(jnp.float32)
    focus_source = standardize_features(align_verticals, focus_scaling_vector).astype(jnp.bfloat16)
    counts = jnp.maximum(jnp.sum(covered_contents, 0), 1.0)
    query_mean = (
        jnp.sum(covered_contents[:, :, None] * focus_source.astype(jnp.float32), 0)
        / counts[:, None]
    ).astype(jnp.bfloat16)
    query = (
        jnp.dot(query_mean, focus_asking_factor, preferred_element_type=jnp.float32)
        * head_dim ** (-0.5)
    ).reshape(amino_swap, heads, head_dim)
    flattened_source = focus_source.reshape(alignments_total * amino_swap, align_feature_length)
    keys = jnp.dot(
        flattened_source, focus_lookup_factor, preferred_element_type=jnp.float32
    ).reshape(alignments_total, amino_swap, head_dim)
    values = jnp.dot(
        flattened_source, focus_content_factor, preferred_element_type=jnp.float32
    ).reshape(alignments_total, amino_swap, head_dim)
    logits = jnp.einsum("rhd,srd->rhs", query, keys, precision=hi)
    logits = logits + jnp.where(covered_contents.T[:, None, :] > 0, 0.0, -1000000000.0).astype(
        jnp.float32
    )
    weights = jax.nn.softmax(logits, -1)
    mixed = jnp.einsum("rhs,srd->rhd", weights, values, precision=hi).reshape(
        amino_swap, heads * head_dim
    )
    gates = jax.nn.sigmoid(
        jnp.dot(flattened_source, focus_sigmoid_factor, preferred_element_type=jnp.float32)
    ).reshape(alignments_total, amino_swap, heads * head_dim)
    sigmoid_scaled_result = (
        (gates * mixed[None])
        .astype(jnp.bfloat16)
        .reshape(alignments_total * amino_swap, heads * head_dim)
    )
    refreshed = (
        align_verticals
        + jnp.dot(
            sigmoid_scaled_result, focus_final_factor, preferred_element_type=jnp.float32
        ).reshape(alignments_total, amino_swap, align_feature_length)
    ).astype(jnp.bfloat16)
    refreshed_supplement_align = lax.all_to_all(
        refreshed.reshape(alignments_total, amino_swap * align_feature_length),
        "row",
        split_axis=0,
        concat_axis=1,
        tiled=True,
    )
    device_align_slice = alignment_tensor.reshape(
        alignments_each_device, vertical_aminos, align_feature_length
    ).astype(jnp.float32)
    device_cover_slice = supplement_align_cover.astype(jnp.float32)
    product_source = (
        standardize_features(device_align_slice, dyadic_scaling_vector)
        .astype(jnp.bfloat16)
        .reshape(alignments_each_device * vertical_aminos, align_feature_length)
    )
    left = (
        (
            jnp.dot(
                product_source, dyadic_first_factor, preferred_element_type=jnp.float32
            ).reshape(alignments_each_device, vertical_aminos, width_o)
            * device_cover_slice[:, :, None]
        )
        .astype(jnp.bfloat16)
        .reshape(alignments_each_device, vertical_aminos * width_o)
    )
    right = (
        (
            jnp.dot(
                product_source, dyadic_second_factor, preferred_element_type=jnp.float32
            ).reshape(alignments_each_device, vertical_aminos, width_o)
            * device_cover_slice[:, :, None]
        )
        .astype(jnp.bfloat16)
        .reshape(alignments_each_device, vertical_aminos * width_o)
    )
    left_all, right_all, mask_all = (
        lax.all_gather(left, "row", axis=0, tiled=True),
        lax.all_gather(right, "row", axis=0, tiled=True),
        lax.all_gather(split_cover_lines, "row", axis=0, tiled=True),
    )
    left_rows, mask_rows = row_block(left_all, mask_all, ratio, rows_res, width_o)
    outer = contract_first(left_rows, right_all)
    pair_count = contract_first(mask_rows, mask_all)
    outer = (
        outer.reshape(rows_res, width_o, vertical_aminos, width_o)
        .transpose(0, 2, 1, 3)
        .astype(jnp.bfloat16)
        .reshape(rows_res * vertical_aminos, width_o * width_o)
    )
    update = (
        jnp.dot(outer, dyadic_final_factor, preferred_element_type=jnp.float32).reshape(
            rows_res, vertical_aminos, width_z
        )
        / jnp.maximum(pair_count, 1.0)[:, :, None]
    )
    chain_rows = lax.dynamic_slice_in_dim(
        amino_strand_label, lax.axis_index("row") * rows_res, rows_res, 0
    )
    chain_cols = lax.dynamic_slice_in_dim(
        amino_strand_label, lax.axis_index("col") * vertical_aminos, vertical_aminos, 0
    )
    same = chain_rows[:, None] == chain_cols[None, :]
    pair_mid = (
        couple_tensor
        + update
        + jnp.where(same[:, :, None], strand_couple_table[1], strand_couple_table[0])
    )
    tri_in = (
        standardize_features(pair_mid, trio_source_scaling)
        .astype(jnp.bfloat16)
        .reshape(rows_res * vertical_aminos, width_z)
    )
    proj = jnp.dot(tri_in, trio_mapping_factors, preferred_element_type=jnp.float32).reshape(
        rows_res, vertical_aminos, 4 * width_t
    )
    pmask = couple_cover_grid.astype(jnp.float32)[:, :, None]
    tri_left = (
        pmask * jax.nn.sigmoid(proj[..., :width_t]) * proj[..., width_t : 2 * width_t]
    ).astype(jnp.bfloat16)
    tri_right = (
        pmask * jax.nn.sigmoid(proj[..., 2 * width_t : 3 * width_t]) * proj[..., 3 * width_t :]
    ).astype(jnp.bfloat16)
    right_every = lax.all_gather(tri_right, "row", axis=0, tiled=True)
    swapped = lax.psum_scatter(
        jnp.einsum(
            "ikc,jkc->jic", tri_left, right_every, preferred_element_type=jnp.float32
        ).astype(jnp.bfloat16),
        "col",
        scatter_dimension=0,
        tiled=True,
    ).astype(jnp.float32)
    product = swapped.transpose(1, 0, 2)
    centered = (
        standardize_features(product, trio_middle_scaling)
        .astype(jnp.bfloat16)
        .reshape(rows_res * vertical_aminos, width_t)
    )
    out_gate = jax.nn.sigmoid(
        jnp.dot(tri_in, trio_sigmoid_factor, preferred_element_type=jnp.float32)
    )
    refreshed_couple_tensor = pair_mid + (
        out_gate * jnp.dot(centered, trio_final_factor, preferred_element_type=jnp.float32)
    ).reshape(rows_res, vertical_aminos, width_z)
    return (refreshed_supplement_align, refreshed_couple_tensor)


def solution(mesh):
    in_specs = (
        P("row", "col"),
        P("row", "col"),
        P("row", "col", None),
        P("row", "col"),
        P(),
        P(),
        P(),
        P(),
        P(),
        P(),
        P(),
        P(),
        P(),
        P(),
        P(),
        P(),
        P(),
        P(),
        P(),
        P(),
        P(),
    )
    out_specs = (P("row", "col"), P("row", "col", None))
    return jax.shard_map(local, mesh=mesh, in_specs=in_specs, out_specs=out_specs, check_vma=False)
```

profile of v0, /device:TPU:0, one launch (start us, length us, event | category | flops | bytes accessed | tf_op | source)
XLA Modules:
  0.0 461.7 jit_solution(16373111073245818870)
XLA Ops:
  7.2 2.0 reshape.258
  18.9 25.4 %all_gather.14 = bf16[1024,64]{1,0:T(8,128)(2,1)S(1)} all-gather(bf16[64,64]{1,0:T(8,128)(2,1)S(1)} %copy.115), channel_id=1, replica_groups=mesh['row'=16,'col'=8] {'row'}, dimensions={0}, use_global_device_ids=true | all-gather | bytes 139264 | tf_op jit(solution)/shard_map/all_gather | solution.py:161
  45.1 24.3 %all-gather.4.cloned.1.call-done = bf16[1024,2048]{1,0:T(8,128)(2,1)} async-done(((bf16[64,2048]{1,0:T(8,128)(2,1)}), bf16[1024,2048]{1,0:T(8,128)(2,1)}) %all-gather.4.cloned.1.call-update) | async-done | bytes 4194320 | tf_op jit(solution)/shard_map/all_gather | solution.py:159
  69.4 3.5 dynamic-slice_select_fusion
  73.8 49.0 %all-gather.6.cloned.1.call-done = bf16[1024,2048]{1,0:T(8,128)(2,1)} async-done(((bf16[64,2048]{1,0:T(8,128)(2,1)}), bf16[1024,2048]{1,0:T(8,128)(2,1)}) %all-gather.6.cloned.1.call-update) | async-done | bytes 4194320 | tf_op jit(solution)/shard_map/all_gather | solution.py:160
  122.9 69.4 %all-reduce.3.cloned.1.call-done = (bf16[1024,1024]{1,0:T(8,128)(2,1)}, bf16[1024,32]{1,0:T(8,128)(2,1)}) async-done(((bf16[1024,1024]{1,0:T(8,128)(2,1)}, bf16[1024,32]{1,0:T(8,128)(2,1)}), (bf16[1024,1024]{1,0:T(8,128)(2,1)}, bf16[1024,32]{1,0:T(8,128)(2,1)})) %all-reduce.3.cloned.1.call-update) | async-done | bytes 2162704 | tf_op jit(solution)/shard_map/psum | solution.py:9
  192.3 9.3 %convolution_convert_fusion = bf16[1024,2048]{1,0:T(8,128)(2,1)} fusion(bf16[1024,1024]{1,0:T(8,128)(2,1)} %get-tuple-element.2, bf16[1024,2048]{1,0:T(8,128)(2,1)} %all-gather.6.cloned.1.call-done), kind=kOutput, calls=%fused_computation.7 | convolution fusion | flops 4297064448 | bytes 10485760 | tf_op jit(solution)/shard_map/dot_general | solution.py:20
  201.6 19.5 %convert_element_type.147 = bf16[32,32,64,32]{3,2,1,0:T(8,128)(2,1)} reshape(bf16[1024,2048]{1,0:T(8,128)(2,1)} %convolution_convert_fusion) | data formatting | bytes 8388608 | tf_op jit(solution)/shard_map/convert_element_type | solution.py:169
  221.1 16.1 %copy.113 = bf16[32,64,32,32]{1,3,2,0:T(8,128)(2,1)} copy(bf16[32,64,32,32]{3,1,2,0:T(8,128)(2,1)} %bitcast.102) | data formatting | bytes 8388608 | tf_op jit(solution)/shard_map/convert_element_type | solution.py:169
  237.4 5.4 %fusion.49 = (f32[32,64]{1,0:T(8,128)S(1)}, f32[32,64,128]{2,1,0:T(8,128)S(1)}) fusion(f32[128]{0:T(128)S(1)} %get-tuple-element.7, f32[128]{0:T(128)S(1)} %get-tuple-element.6, pred[32,64]{1,0:T(8,128)(4,1)S(1)} %broadcast_compare_fusion, f32[32,64,128]{2,1,0:T(8,128)S(1)} %copy-done.22, f32[32,64]{1,0:T(8,128)S(1)} %convolution_maximum_fusion, ...), kind=kOutput, calls=%fused_computation.97 | convolution fusion | flops 538179584 | bytes 6573056 | tf_op jit(solution)/shard_map/dot_general | solution.py:173
  249.0 68.7 %all-gather.8.cloned.1.call-done = bf16[512,64,128]{2,1,0:T(8,128)(2,1)} async-done(((bf16[32,64,128]{2,1,0:T(8,128)(2,1)}), bf16[512,64,128]{2,1,0:T(8,128)(2,1)}) %all-gather.8.cloned.1.call-update) | async-done | bytes 8388624 | tf_op jit(solution)/shard_map/all_gather | solution.py:205
  317.7 23.7 %copy.116 = bf16[512,64,128]{1,0,2:T(8,128)(2,1)} copy(bf16[512,64,128]{2,1,0:T(8,128)(2,1)} %all-gather.8.cloned.1.call-done) | data formatting | bytes 16777216 | tf_op jit(solution)/shard_map/all_gather | solution.py:205
  341.5 10.7 %convert_bitcast_fusion = bf16[512,32,128]{0,1,2:T(8,128)(2,1)} fusion(bf16[512,64,128]{1,0,2:T(8,128)(2,1)} %copy.116, bf16[32,64,128]{1,0,2:T(8,128)(2,1)S(1)} %copy.117), kind=kOutput, calls=%fused_computation.6 | convolution fusion | flops 270532608 | bytes 13107200 | tf_op jit(solution)/shard_map/ikc,jkc->jic/dot_general | solution.py:207
  352.2 9.1 %copy.118 = bf16[512,32,128]{2,1,0:T(8,128)(2,1)} copy(bf16[512,32,128]{0,1,2:T(8,128)(2,1)} %convert_bitcast_fusion) | data formatting | bytes 8388608 | tf_op jit(solution)/shard_map/convert_element_type | solution.py:209
  362.0 5.3 %all-to-all-start.1 = ((bf16[16,2,128]{2,1,0:T(2,128)(2,1)}), bf16[16,2,128]{2,1,0:T(2,128)(2,1)S(1)}, u32[]{:S(2)}, u32[]{:S(2)}) async-start(bf16[16,2,128]{2,1,0:T(2,128)(2,1)} %reshape.266), calls=%async_computation.1 | async-start | bytes 16384 | tf_op jit(solution)/shard_map/all_to_all | solution.py:76
  368.2 6.5 %all-to-all-done.1 = bf16[16,2,128]{2,1,0:T(2,128)(2,1)S(1)} async-done(((bf16[16,2,128]{2,1,0:T(2,128)(2,1)}), bf16[16,2,128]{2,1,0:T(2,128)(2,1)S(1)}, u32[]{:S(2)}, u32[]{:S(2)}) %all-to-all-start.1) | async-done | bytes 8224 | tf_op jit(solution)/shard_map/all_to_all | solution.py:76
  374.8 4.3 all-to-all-start
  380.4 1.7 mul.196
  382.1 2.3 copy.102
  384.4 5.0 %all-to-all-done = bf16[64,16,256]{2,0,1:T(8,128)(2,1)} async-done(((bf16[64,16,256]{2,0,1:T(8,128)(2,1)}), bf16[64,16,256]{2,0,1:T(8,128)(2,1)}, u32[]{:S(2)}, u32[]{:S(2)}) %all-to-all-start) | async-done | bytes 524320 | tf_op jit(solution)/shard_map/all_to_all | solution.py:75
  390.8 2.8 copy.94
  395.2 2.0 reshape.255
  399.6 1.9 mul.198
  401.5 3.8 copy.101
  405.5 1.9 sub.64
  407.4 4.0 copy.100
  411.3 2.1 multiply_reduce_fusion.2
  417.1 3.2 copy.103
  424.7 4.0 fusion.4
  431.5 1.8 all_to_all.38
  434.1 13.1 %all_to_all.45 = bf16[16,64,256]{2,1,0:T(8,128)(2,1)S(1)} all-to-all(bf16[16,64,256]{2,1,0:T(8,128)(2,1)S(1)} %copy.107), channel_id=1, replica_groups=mesh['row'=16,'col'=8] {'row'}, dimensions={0} | all-to-all | bytes 1048576 | tf_op jit(solution)/shard_map/all_to_all | solution.py:122
  449.9 1.7 fusion.25
  (140 shorter events, 43.5 us)
Async XLA Ops:
  7.2 230.2 %copy-start = (bf16[1024,128]{1,0:T(8,128)(2,1)S(1)}, bf16[1024,128]{1,0:T(8,128)(2,1)}, u32[]{:S(2)}) copy-start(bf16[1024,128]{1,0:T(8,128)(2,1)} %param.35) | copy-start | bytes 786436
  7.2 62.3 %all-gather.4.cloned.1.call-start = ((), (), s32[]{:S(2)}) async-start(), calls=%async_computation.4 | async-start | bytes 4456448 | tf_op jit(solution)/shard_map/all_gather | solution.py:159
  9.2 2.0 copy-start.9
  9.2 2.0 copy-start.13
  9.2 2.0 copy-start.17
  11.2 3.7 copy-start.14
  14.9 107.9 %all-gather.6.cloned.1.call-start = ((), (), s32[]{:S(2)}) async-start(), calls=%async_computation.5 | async-start | bytes 4456448 | tf_op jit(solution)/shard_map/all_gather | solution.py:160
  18.6 173.6 %all-reduce.3.cloned.1.call-start = ((), (), s32[]{:S(2)}) async-start(), calls=%async_computation.8 | async-start | bytes 4718592 | tf_op jit(solution)/shard_map/psum | solution.py:9
  72.9 0.8 copy-start.19
  72.9 244.8 %all-gather.8.cloned.1.call-start = ((), (), s32[]{:S(2)}) async-start(), calls=%async_computation.6 | async-start | bytes 8912896 | tf_op jit(solution)/shard_map/all_gather | solution.py:205
  221.1 16.1 %copy-start.7 = (bf16[1024,32]{1,0:T(8,128)(2,1)S(1)}, bf16[1024,32]{1,0:T(8,128)(2,1)}, u32[]{:S(2)}) copy-start(bf16[1024,32]{1,0:T(8,128)(2,1)} %get-tuple-element.3) | copy-start | bytes 196612
  221.1 16.3 %copy-start.22 = (f32[32,64,128]{2,1,0:T(8,128)S(1)}, f32[32,64,128]{2,1,0:T(8,128)}, u32[]{:S(2)}) copy-start(f32[32,64,128]{2,1,0:T(8,128)} %param.23) | copy-start | bytes 3145732
  237.4 6.1 %copy-start.20 = (f32[128]{0:T(128)S(1)}, f32[128]{0:T(128)}, u32[]{:S(2)}) copy-start(f32[128]{0:T(128)} %param.37) | copy-start | bytes 1540
  242.8 2.1 copy-start.8
  244.1 0.8 copy-start.5
  247.1 201.4 %reduce-scatter.2.cloned.1.call-start = ((), (), s32[]{:S(2)}) async-start(), calls=%async_computation.7 | async-start | bytes 4718592 | tf_op jit(solution)/shard_map/reduce_scatter | solution.py:206
  361.3 6.0 %copy-start.4 = (bf16[64,4096]{1,0:T(8,128)(2,1)S(1)}, bf16[64,4096]{1,0:T(8,128)(2,1)}, u32[]{:S(2)}) copy-start(bf16[64,4096]{1,0:T(8,128)(2,1)} %param.21) | copy-start | bytes 1572868
  361.3 6.8 %copy-start.18 = (f32[64]{0:T(128)S(1)}, f32[64]{0:T(128)}, u32[]{:S(2)}) copy-start(f32[64]{0:T(128)} %param.26) | copy-start | bytes 772
  362.0 12.7 %all-to-all-start.1 = ((bf16[16,2,128]{2,1,0:T(2,128)(2,1)}), bf16[16,2,128]{2,1,0:T(2,128)(2,1)S(1)}, u32[]{:S(2)}, u32[]{:S(2)}) async-start(bf16[16,2,128]{2,1,0:T(2,128)(2,1)} %reshape.266), calls=%async_computation.1 | async-start | bytes 16384 | tf_op jit(solution)/shard_map/all_to_all | solution.py:76
  374.8 14.7 %all-to-all-start = ((bf16[64,16,256]{2,0,1:T(8,128)(2,1)}), bf16[64,16,256]{2,0,1:T(8,128)(2,1)}, u32[]{:S(2)}, u32[]{:S(2)}) async-start(bf16[64,16,256]{2,0,1:T(8,128)(2,1)} %bitcast.101), calls=%async_computation | async-start | bytes 1048576 | tf_op jit(solution)/shard_map/all_to_all | solution.py:75
  407.4 4.0 copy-start.2
  411.3 2.2 copy-start.24
  411.3 2.7 copy-start.15
  413.5 1.3 copy-start.16
  417.1 5.9 %copy-start.3 = (f32[16,64,256]{2,1,0:T(8,128)S(1)}, f32[16,64,256]{2,1,0:T(8,128)}, u32[]{:S(2)}) copy-start(f32[16,64,256]{2,1,0:T(8,128)} %copy.95) | copy-start | bytes 3145732
  420.3 4.3 copy-start.25
  424.7 5.5 %copy-start.11 = (bf16[64,64]{1,0:T(8,128)(2,1)S(1)}, bf16[64,64]{1,0:T(8,128)(2,1)}, u32[]{:S(2)}) copy-start(bf16[64,64]{1,0:T(8,128)(2,1)} %param.31) | copy-start | bytes 24580
  433.2 14.8 %copy-start.6 = (bf16[32,64,128]{2,1,0:T(8,128)(2,1)S(1)}, bf16[32,64,128]{2,1,0:T(8,128)(2,1)}, u32[]{:S(2)}) copy-start(bf16[32,64,128]{2,1,0:T(8,128)(2,1)} %copy-done.5) | copy-start | bytes 1572868
  433.3 14.8 %copy-start.23 = (bf16[128,128]{1,0:T(8,128)(2,1)S(1)}, bf16[128,128]{1,0:T(8,128)(2,1)}, u32[]{:S(2)}) copy-start(bf16[128,128]{1,0:T(8,128)(2,1)} %param.39) | copy-start | bytes 98308
  448.1 3.6 copy-start.21
  448.5 4.8 %copy-start.10 = (bf16[128,128]{1,0:T(8,128)(2,1)S(1)}, bf16[128,128]{1,0:T(8,128)(2,1)}, u32[]{:S(2)}) copy-start(bf16[128,128]{1,0:T(8,128)(2,1)} %param.41) | copy-start | bytes 98308
  453.3 1.4 copy-start.1
  (2 other events, 1.5 us)
Sparse Core Ops, SparseCore 0:
  15.0 54.3 all-gather.3
  71.6 51.2 all-gather.5
  126.0 66.2 all-reduce.2
  247.2 70.4 all-gather.7
  361.4 37.7 reduce-scatter.1
where the time goes:
time: 469 us; the launch traced here: 462 us
  waiting for transfers between devices  223 us (48%)
  local copies, waits for them, and re-layouts  119 us (25%)
  blocking collectives  38.5 us (8%)
  matrix products  37 us (8%)
  other arithmetic  19.2 us (4%)
  between operations  14.8 us (3%)
  starting transfers between devices  10.1 us (2%)
    psum x1, waiting for transfers between devices, broadcast(): return lax.psum(jnp.where(mine, shard, jnp.zeros_like(shard)), axis)  69.4 us
    all_gather x1, waiting for transfers between devices, local(): right_every = lax.all_gather(tri_right, 'row', axis=0, tiled=True)  68.7 us
    all_gather x1, waiting for transfers between devices, local(): lax.all_gather(right, 'row', axis=0, tiled=True)  49 us
    convert_element_type x2, local copies, waits for them, and re-layouts, local(): outer = outer.reshape(rows_res, width_o, vertical_aminos, width_o).transp...  35.6 us
    all_gather x1, blocking collectives, local(): lax.all_gather(split_cover_lines, 'row', axis=0, tiled=True)  25.4 us
    all_gather x1, waiting for transfers between devices, local(): lax.all_gather(left, 'row', axis=0, tiled=True)  24.3 us
    all_gather x1, local copies, waits for them, and re-layouts, local(): right_every = lax.all_gather(tri_right, 'row', axis=0, tiled=True)  23.7 us
    all_to_all x1, blocking collectives, local(): lax.all_to_all(refreshed.reshape(alignments_total, amino_swap * align_fea...  13.1 us
  transfers between devices with their start and end apart: 7, of which 6 were waited for; matrix products, arithmetic and copies ran while one was open for 13% of the time, Pallas kernels for 0%

commit v1 on v0

--- a/solution.py
+++ b/solution.py
@@ -1,12 +1,13 @@
 import jax
 import jax.numpy as jnp
 from jax import lax
+from jax.experimental import pallas as pl
+from jax.experimental.pallas import tpu as pltpu
 from jax.sharding import PartitionSpec as P
 
-
-def broadcast(shard, axis, root):
-    mine = lax.axis_index(axis) == root
-    return lax.psum(jnp.where(mine, shard, jnp.zeros_like(shard)), axis)
+LANES = 128
+HALF = 64
+VMEM_LIMIT = 50 * 1024 * 1024
 
 
 def standardize_features(x, gain):
@@ -16,23 +17,284 @@
     return centred * lax.rsqrt(var + 1e-05) * gain
 
 
-def contract_first(left, right):
-    return lax.dot_general(
-        left, right, (((0,), (0,)), ((), ())), preferred_element_type=jnp.float32
-    )
-
-
-def row_block(left_all, mask_all, ratio, block_rows, channels):
-    row_pos = lax.axis_index("row")
-    half = row_pos % ratio
-    sub_left = lax.dynamic_slice_in_dim(
-        left_all, half * block_rows * channels, block_rows * channels, 1
-    )
-    sub_mask = lax.dynamic_slice_in_dim(mask_all, half * block_rows, block_rows, 1)
-    return (
-        broadcast(sub_left, "col", row_pos // ratio),
-        broadcast(sub_mask, "col", row_pos // ratio),
-    )
+def lane_index(shape):
+    return lax.broadcasted_iota(jnp.int32, shape, len(shape) - 1)
+
+
+def pair_kernel(
+    left_a_ref,
+    left_b_ref,
+    left_mask_ref,
+    right_ref,
+    final_ref,
+    couple_ref,
+    cover_ref,
+    same_ref,
+    table_ref,
+    gain_ref,
+    mapping_ref,
+    mid_ref,
+    source_ref,
+    sent_ref,
+    outer_ref,
+    count_ref,
+    sides_ref,
+):
+    step = pl.program_id(0)
+    steps = pl.num_programs(0)
+    rows = 4
+    low = lane_index((LANES, LANES)) < HALF
+
+    @pl.when(step == 0)
+    def _():
+        both = lax.dot_general(
+            left_mask_ref[...],
+            right_ref[:, 2048:2176],
+            (((0,), (0,)), ((), ())),
+            preferred_element_type=jnp.float32,
+        )
+        both = jnp.maximum(both[:32], 1.0)
+        count_ref[...] = jnp.where(lane_index((16, LANES)) < HALF, both[:16], both[16:])
+
+    left = jnp.concatenate([left_a_ref[...], left_b_ref[...]], axis=1).T
+    for n in range(8):
+        outer_ref[:, n * 256 : (n + 1) * 256] = jnp.dot(
+            left, right_ref[:, n * 256 : (n + 1) * 256], preferred_element_type=jnp.float32
+        ).astype(jnp.bfloat16)
+
+    sources = []
+    for p in range(rows):
+        halves = []
+        for top in (p * 32, 128 + p * 32):
+            halves.append(
+                jnp.concatenate(
+                    [outer_ref[top : top + 32, d * LANES : (d + 1) * LANES] for d in range(16)],
+                    axis=0,
+                )
+            )
+        update = jnp.dot(
+            final_ref[...],
+            jnp.concatenate(halves, axis=1),
+            preferred_element_type=jnp.float32,
+        )
+        a0, a1 = update[:LANES, :LANES], update[LANES:, :LANES]
+        b0, b1 = update[:LANES, LANES:], update[LANES:, LANES:]
+        update = jnp.where(low, a0, b1) + pltpu.roll(jnp.where(low, b0, a1), HALF, 1)
+        here = pl.ds(step * rows + p, 1)
+        update = update / count_ref[here, :]
+        update = update + jnp.where(same_ref[here, :] > 0, table_ref[:, 1:2], table_ref[:, 0:1])
+        mid = couple_ref[:, p].reshape(LANES, LANES) + update.T
+        mid_ref[:, p] = mid.reshape(2, HALF, LANES)
+        mean = jnp.mean(mid, -1, keepdims=True)
+        centred = mid - mean
+        var = jnp.mean(centred * centred, -1, keepdims=True)
+        source = (centred * lax.rsqrt(var + 1e-05) * gain_ref[...]).astype(jnp.bfloat16)
+        source_ref[:, p] = source.reshape(2, HALF, LANES)
+        sources.append(source)
+    for half in range(2):
+        proj = lax.dot_general(
+            mapping_ref[half * 256 : (half + 1) * 256, :],
+            jnp.concatenate(sources, axis=0),
+            (((1,), (1,)), ((), ())),
+            preferred_element_type=jnp.float32,
+        )
+        for p in range(rows):
+            cover = cover_ref[pl.ds(step * rows + p, 1), :]
+            gate = proj[:LANES, p * LANES : (p + 1) * LANES]
+            value = proj[LANES:, p * LANES : (p + 1) * LANES]
+            sides_ref[pl.ds(pl.multiple_of((half * 16 + step * rows + p) * LANES, LANES), LANES), :] = (
+                cover * jax.nn.sigmoid(gate) * value
+            )
+
+    @pl.when(step == steps - 1)
+    def _():
+        def one(c, carry):
+            sent_ref[c] = sides_ref[pl.ds(c, 32, stride=LANES), :].astype(jnp.bfloat16)
+            return carry
+
+        lax.fori_loop(0, LANES, one, 0, unroll=8)
+
+
+def triangle_kernel(taken_ref, product_ref):
+    low = lane_index((256, LANES)) < HALF
+    sides = []
+    for top in (0, 16):
+        columns = []
+        for q in range(4):
+            even = taken_ref[:, 2 * q, top : top + 16, :].reshape(256, LANES).astype(jnp.float32)
+            odd = taken_ref[:, 2 * q + 1, top : top + 16, :].reshape(256, LANES).astype(jnp.float32)
+            first = jnp.where(low, even, pltpu.roll(odd, HALF, 1)).astype(jnp.bfloat16)
+            second = jnp.where(low, pltpu.roll(even, HALF, 1), odd).astype(jnp.bfloat16)
+            columns.append(
+                jnp.concatenate(
+                    [first.reshape(16, 1, 16, LANES), second.reshape(16, 1, 16, LANES)], axis=1
+                ).reshape(512, LANES)
+            )
+        sides.append(jnp.concatenate(columns, axis=1))
+    product = lax.dot_general(
+        sides[0], sides[1], (((1,), (1,)), ((), ())), preferred_element_type=jnp.float32
+    )
+    product = product.reshape(16, 2, 16, 512)
+    for q in range(4):
+        first = product[:, 0, :, q * LANES : (q + 1) * LANES].reshape(256, LANES)
+        second = product[:, 1, :, q * LANES : (q + 1) * LANES].reshape(256, LANES)
+        product_ref[:, 2 * q] = (
+            jnp.where(low, first, pltpu.roll(second, HALF, 1))
+            .astype(jnp.bfloat16)
+            .reshape(16, 16, LANES)
+        )
+        product_ref[:, 2 * q + 1] = (
+            jnp.where(low, pltpu.roll(first, HALF, 1), second)
+            .astype(jnp.bfloat16)
+            .reshape(16, 16, LANES)
+        )
+
+
+def finish_kernel(
+    product_ref, mid_ref, source_ref, gate_ref, final_ref, gain_ref, out_ref, normal_ref
+):
+    step = pl.program_id(0)
+    rows = 4
+
+    @pl.when(step == 0)
+    def _():
+        total = product_ref[0].astype(jnp.float32)
+        for c in range(1, LANES):
+            total = total + product_ref[c].astype(jnp.float32)
+        mean = total / LANES
+        square = jnp.zeros_like(mean)
+        for c in range(LANES):
+            centred = product_ref[c].astype(jnp.float32) - mean
+            square = square + centred * centred
+        scale = lax.rsqrt(square / LANES + 1e-05)
+        for c in range(LANES):
+            normal_ref[c * 16 : (c + 1) * 16, :] = (
+                product_ref[c].astype(jnp.float32) - mean
+            ) * scale
+
+    for p in range(rows):
+        centred = (
+            normal_ref[pl.ds(step * rows + p, LANES, stride=16), :] * gain_ref[...]
+        ).astype(jnp.bfloat16)
+        result = lax.dot_general(
+            centred, final_ref[...], (((0,), (0,)), ((), ())), preferred_element_type=jnp.float32
+        )
+        gate = jax.nn.sigmoid(
+            jnp.dot(
+                source_ref[:, p].reshape(LANES, LANES),
+                gate_ref[...],
+                preferred_element_type=jnp.float32,
+            )
+        )
+        out_ref[:, p] = mid_ref[:, p] + (gate * result).reshape(2, HALF, LANES)
+
+
+def whole(shape):
+    return pl.BlockSpec(shape, lambda t: (0,) * len(shape), pipeline_mode=pl.Buffered(1))
+
+
+def by_rows(dtype_rows=4):
+    return pl.BlockSpec((2, dtype_rows, HALF, LANES), lambda t: (0, t, 0, 0))
+
+
+PARAMS = pltpu.CompilerParams(
+    vmem_limit_bytes=VMEM_LIMIT, dimension_semantics=("arbitrary",)
+)
+
+
+def pair_call(left, right, final, couple, cover, same, table, gain, mapping):
+    return pl.pallas_call(
+        pair_kernel,
+        grid=(4,),
+        in_specs=[
+            pl.BlockSpec((1024, LANES), lambda t: (0, t)),
+            pl.BlockSpec((1024, LANES), lambda t: (0, t + 4)),
+            pl.BlockSpec((1024, LANES), lambda t: (0, 8), pipeline_mode=pl.Buffered(1)),
+            whole((1024, 2176)),
+            whole((256, 512)),
+            by_rows(),
+            whole((16, LANES)),
+            whole((16, LANES)),
+            whole((LANES, 2)),
+            whole((1, LANES)),
+            whole((512, LANES)),
+        ],
+        out_specs=[by_rows(), by_rows(), whole((LANES, 32, LANES))],
+        out_shape=[
+            jax.ShapeDtypeStruct((2, 16, HALF, LANES), jnp.float32),
+            jax.ShapeDtypeStruct((2, 16, HALF, LANES), jnp.bfloat16),
+            jax.ShapeDtypeStruct((LANES, 32, LANES), jnp.bfloat16),
+        ],
+        scratch_shapes=[
+            pltpu.VMEM((256, 2048), jnp.bfloat16),
+            pltpu.VMEM((16, LANES), jnp.float32),
+            pltpu.VMEM((32 * LANES, LANES), jnp.float32),
+        ],
+        compiler_params=PARAMS,
+        name="pair",
+    )(left, left, left, right, final, couple, cover, same, table, gain, mapping)
+
+
+def triangle_call(taken):
+    return pl.pallas_call(
+        triangle_kernel,
+        out_shape=jax.ShapeDtypeStruct((16, 8, 16, LANES), jnp.bfloat16),
+        compiler_params=pltpu.CompilerParams(vmem_limit_bytes=VMEM_LIMIT),
+        name="triangle",
+    )(taken)
+
+
+def finish_call(product, mid, source, gate, final, gain):
+    return pl.pallas_call(
+        finish_kernel,
+        grid=(4,),
+        in_specs=[
+            whole((LANES, 16, LANES)),
+            by_rows(),
+            by_rows(),
+            whole((LANES, LANES)),
+            whole((LANES, LANES)),
+            whole((LANES, 1)),
+        ],
+        out_specs=by_rows(),
+        out_shape=jax.ShapeDtypeStruct((2, 16, HALF, LANES), jnp.float32),
+        scratch_shapes=[pltpu.VMEM((LANES * 16, LANES), jnp.float32)],
+        compiler_params=PARAMS,
+        name="finish",
+    )(product, mid, source, gate, final, gain)
+
+
+def spread_left(left, cover):
+    row, n_row, n_col = lax.axis_index("row"), lax.axis_size("row"), lax.axis_size("col")
+    halves = [
+        jnp.concatenate(
+            [
+                left[:, h * 1024 : (h + 1) * 1024],
+                jnp.pad(cover[:, h * 32 : (h + 1) * 32], ((0, 0), (0, LANES - 32))),
+            ],
+            axis=1,
+        )
+        for h in range(2)
+    ]
+    odd = row % 2 == 1
+    own = jnp.where(odd, halves[1], halves[0])
+    other = jnp.where(odd, halves[0], halves[1])
+
+    def route(flip):
+        return [
+            (r * n_col + c, (2 * c + (r + flip) % 2) * n_col + r // 2)
+            for r in range(n_row)
+            for c in range(n_col)
+        ]
+
+    own = lax.ppermute(own, ("row", "col"), route(0))
+    other = lax.ppermute(other, ("row", "col"), route(1))
+    both = jnp.concatenate([jnp.where(odd, other, own), jnp.where(odd, own, other)], axis=0)
+    return lax.all_gather(both, "col", axis=0, tiled=True)
+
+
+def halves_on_lanes(grid):
+    return jnp.concatenate([grid[:16], grid[16:]], axis=1)
 
 
 def local(
@@ -61,7 +323,6 @@
     hi = lax.Precision.HIGHEST
     n_row = lax.axis_size("row")
     n_col = lax.axis_size("col")
-    ratio = n_row // n_col
     alignments_each_device, vertical_aminos = supplement_align_cover.shape
     rows_res = couple_tensor.shape[0]
     align_feature_length = focus_scaling_vector.shape[0]
@@ -153,75 +414,47 @@
             * device_cover_slice[:, :, None]
         )
         .astype(jnp.bfloat16)
+        .transpose(0, 2, 1)
         .reshape(alignments_each_device, vertical_aminos * width_o)
     )
-    left_all, right_all, mask_all = (
-        lax.all_gather(left, "row", axis=0, tiled=True),
-        lax.all_gather(right, "row", axis=0, tiled=True),
-        lax.all_gather(split_cover_lines, "row", axis=0, tiled=True),
-    )
-    left_rows, mask_rows = row_block(left_all, mask_all, ratio, rows_res, width_o)
-    outer = contract_first(left_rows, right_all)
-    pair_count = contract_first(mask_rows, mask_all)
-    outer = (
-        outer.reshape(rows_res, width_o, vertical_aminos, width_o)
-        .transpose(0, 2, 1, 3)
-        .astype(jnp.bfloat16)
-        .reshape(rows_res * vertical_aminos, width_o * width_o)
-    )
-    update = (
-        jnp.dot(outer, dyadic_final_factor, preferred_element_type=jnp.float32).reshape(
-            rows_res, vertical_aminos, width_z
-        )
-        / jnp.maximum(pair_count, 1.0)[:, :, None]
-    )
+    right = jnp.concatenate([right, split_cover_lines, split_cover_lines], axis=1)
+    left_rows = spread_left(left, split_cover_lines)
+    right_all = lax.all_gather(right, "row", axis=0, tiled=True)
     chain_rows = lax.dynamic_slice_in_dim(
         amino_strand_label, lax.axis_index("row") * rows_res, rows_res, 0
     )
     chain_cols = lax.dynamic_slice_in_dim(
         amino_strand_label, lax.axis_index("col") * vertical_aminos, vertical_aminos, 0
     )
-    same = chain_rows[:, None] == chain_cols[None, :]
-    pair_mid = (
-        couple_tensor
-        + update
-        + jnp.where(same[:, :, None], strand_couple_table[1], strand_couple_table[0])
-    )
-    tri_in = (
-        standardize_features(pair_mid, trio_source_scaling)
-        .astype(jnp.bfloat16)
-        .reshape(rows_res * vertical_aminos, width_z)
-    )
-    proj = jnp.dot(tri_in, trio_mapping_factors, preferred_element_type=jnp.float32).reshape(
-        rows_res, vertical_aminos, 4 * width_t
-    )
-    pmask = couple_cover_grid.astype(jnp.float32)[:, :, None]
-    tri_left = (
-        pmask * jax.nn.sigmoid(proj[..., :width_t]) * proj[..., width_t : 2 * width_t]
-    ).astype(jnp.bfloat16)
-    tri_right = (
-        pmask * jax.nn.sigmoid(proj[..., 2 * width_t : 3 * width_t]) * proj[..., 3 * width_t :]
-    ).astype(jnp.bfloat16)
-    right_every = lax.all_gather(tri_right, "row", axis=0, tiled=True)
-    swapped = lax.psum_scatter(
-        jnp.einsum(
-            "ikc,jkc->jic", tri_left, right_every, preferred_element_type=jnp.float32
-        ).astype(jnp.bfloat16),
-        "col",
-        scatter_dimension=0,
-        tiled=True,
-    ).astype(jnp.float32)
-    product = swapped.transpose(1, 0, 2)
-    centered = (
-        standardize_features(product, trio_middle_scaling)
-        .astype(jnp.bfloat16)
-        .reshape(rows_res * vertical_aminos, width_t)
-    )
-    out_gate = jax.nn.sigmoid(
-        jnp.dot(tri_in, trio_sigmoid_factor, preferred_element_type=jnp.float32)
-    )
-    refreshed_couple_tensor = pair_mid + (
-        out_gate * jnp.dot(centered, trio_final_factor, preferred_element_type=jnp.float32)
+    same = (chain_rows[:, None] == chain_cols[None, :]).astype(jnp.float32)
+    final = (
+        dyadic_final_factor.reshape(width_o, 16, 2, width_z)
+        .transpose(2, 3, 1, 0)
+        .reshape(2 * width_z, 16 * width_o)
+    )
+    pair_mid, tri_in, sides = pair_call(
+        left_rows,
+        right_all,
+        final,
+        couple_tensor.reshape(2, 16, vertical_aminos, width_z),
+        halves_on_lanes(couple_cover_grid.astype(jnp.float32)),
+        halves_on_lanes(same),
+        strand_couple_table.T,
+        trio_source_scaling.reshape(1, width_z),
+        trio_mapping_factors.T,
+    )
+    taken = lax.all_to_all(sides, ("row", "col"), 0, 0, tiled=True)
+    product = triangle_call(taken.reshape(n_row, n_col, 32, LANES))
+    product = lax.all_to_all(
+        product.reshape(n_row * n_col, 16, LANES), ("row", "col"), 0, 0, tiled=True
+    )
+    refreshed_couple_tensor = finish_call(
+        product,
+        pair_mid,
+        tri_in,
+        trio_sigmoid_factor,
+        trio_final_factor,
+        trio_middle_scaling.reshape(width_t, 1),
     ).reshape(rows_res, vertical_aminos, width_z)
     return (refreshed_supplement_align, refreshed_couple_tensor)
 

time: 469 us -> 220 us (0.47); the launches traced: 462 us -> 218 us
  waiting for transfers between devices: 223 us -> 62.4 us
  local copies, waits for them, and re-layouts: 119 us -> 55.1 us
  blocking collectives: 38.5 us -> 0 us
  starting transfers between devices: 10.1 us -> 48.6 us
  matrix products: 37 us -> 11.2 us
  Pallas kernels: 0 us -> 20.6 us
  other arithmetic: 19.2 us -> 6.02 us
    all_gather x3 -> x2, waiting for transfers between devices: 142 us -> 26.5 us  [the longest x1 26.4 us: local(): right_all = lax.all_gather(right, 'row', axis=0, tiled=True)]
    psum x1 -> x0, waiting for transfers between devices: 69.4 us -> none  [broadcast(): return lax.psum(jnp.where(mine, shard, jnp.zeros_like(shard)), axis)]
    convert_element_type x5 -> x0, local copies, waits for them, and re-layouts: 47.4 us -> none  [the longest x2 35.6 us: local(): outer = outer.reshape(rows_res, width_o, vertical_aminos, width_o).transp...]
    dot_general x7 -> x0, matrix products: 27.1 us -> none  [the longest x1 10.7 us: local(): jnp.einsum('ikc,jkc->jic', tri_left, right_every, preferred_element_type=...]
    all_gather x1 -> x0, blocking collectives: 25.4 us -> none  [local(): lax.all_gather(split_cover_lines, 'row', axis=0, tiled=True)]
    all_gather x1 -> x0, local copies, waits for them, and re-layouts: 23.7 us -> none  [local(): right_every = lax.all_gather(tri_right, 'row', axis=0, tiled=True)]
    all_to_all x0 -> x3, waiting for transfers between devices: none -> 21.8 us  [the longest x1 11.5 us: local(): lax.all_to_all(product.reshape(n_row * n_col, 16, LANES), ('row', 'col'),...]
    all_to_all x0 -> x3, starting transfers between devices: none -> 21.3 us  [the longest x1 8.47 us: local(): taken = lax.all_to_all(sides, ('row', 'col'), 0, 0, tiled=True)]
  transfers between devices with their start and end apart: 7 -> 9, of which waited for: 6 -> 6; matrix products, arithmetic and copies ran while one was open for 13% -> 28% of each run, Pallas kernels for 0% -> 1%
where the time goes in v1:
time: 220 us; the launch traced here: 218 us
  waiting for transfers between devices  62.4 us (28%)
  local copies, waits for them, and re-layouts  55.1 us (25%)
  starting transfers between devices  48.6 us (22%)
  Pallas kernels  20.6 us (9%)
  between operations  14.6 us (7%)
  matrix products  11.2 us (5%)
  other arithmetic  6.02 us (3%)
    all_gather x1, waiting for transfers between devices, local(): right_all = lax.all_gather(right, 'row', axis=0, tiled=True)  26.4 us
    all_to_all x1, starting transfers between devices, local(): lax.all_to_all(split_cover_lines, 'row', split_axis=1, concat_axis=0, til...  21.1 us
    pallas_call x1, Pallas kernels, pair_call(): pl.pallas_call(pair_kernel, grid=(4,), in_specs=[pl.BlockSpec((1024, LANE...  15.9 us
    all_to_all x1, waiting for transfers between devices, local(): lax.all_to_all(product.reshape(n_row * n_col, 16, LANES), ('row', 'col'),...  11.5 us
    convert_element_type x4, local copies, waits for them, and re-layouts, local(): dispatched.reshape(alignments_total, amino_swap, align_feature_length)  10.5 us
    all_to_all x1, waiting for transfers between devices, local(): lax.all_to_all(refreshed.reshape(alignments_total, amino_swap * align_fea...  10.3 us
    all_to_all x1, starting transfers between devices, local(): taken = lax.all_to_all(sides, ('row', 'col'), 0, 0, tiled=True)  8.47 us
    all_to_all x3, local copies, waits for them, and re-layouts, local(): lax.all_to_all(refreshed.reshape(alignments_total, amino_swap * align_fea...  7.1 us
  transfers between devices with their start and end apart: 9, of which 6 were waited for; matrix products, arithmetic and copies ran while one was open for 28% of the time, Pallas kernels for 1%

profile of v1, /device:TPU:0, one launch (start us, length us, event | category | flops | bytes accessed | tf_op | source)
XLA Modules:
  0.0 218.4 jit_solution(14496801729249971439)
XLA Ops:
  7.2 1.9 reshape.216
  16.7 2.9 %collective-permute-done = bf16[64,1152]{1,0:T(8,128)(2,1)S(1)} collective-permute-done((bf16[64,1152]{1,0:T(8,128)(2,1)S(1)}, bf16[64,1152]{1,0:T(8,128)(2,1)S(1)}, u32[]{:S(2)}, u32[]{:S(2)}) %collective-permute-start) | collective-permute-done | bytes 147488 | tf_op jit(solution)/shard_map/ppermute | solution.py:291
  24.3 21.1 %all-to-all-start.1 = ((bf16[16,2,128]{2,1,0:T(2,128)(2,1)}), bf16[16,2,128]{2,1,0:T(2,128)(2,1)S(1)}, u32[]{:S(2)}, u32[]{:S(2)}) async-start(bf16[16,2,128]{2,1,0:T(2,128)(2,1)} %reshape.222), calls=%async_computation.1 | async-start | bytes 16384 | tf_op jit(solution)/shard_map/all_to_all | solution.py:337
  47.4 5.5 %all-to-all-done.1 = bf16[16,2,128]{2,1,0:T(2,128)(2,1)S(1)} async-done(((bf16[16,2,128]{2,1,0:T(2,128)(2,1)}), bf16[16,2,128]{2,1,0:T(2,128)(2,1)S(1)}, u32[]{:S(2)}, u32[]{:S(2)}) %all-to-all-start.1) | async-done | bytes 8224 | tf_op jit(solution)/shard_map/all_to_all | solution.py:337
  52.9 3.8 %all-to-all-start = ((bf16[64,16,256]{2,0,1:T(8,128)(2,1)}), bf16[64,16,256]{2,0,1:T(8,128)(2,1)S(1)}, u32[]{:S(2)}, u32[]{:S(2)}) async-start(bf16[64,16,256]{2,0,1:T(8,128)(2,1)} %bitcast.74), calls=%async_computation | async-start | bytes 1048576 | tf_op jit(solution)/shard_map/all_to_all | solution.py:336
  58.1 1.7 mul.130
  59.8 2.3 %copy.103 = f32[16,64,256]{2,0,1:T(8,128)} copy(f32[16,64,256]{1,0,2:T(8,128)S(1)} %mul.130) | data formatting | bytes 2097152 | tf_op jit(solution)/shard_map/mul | solution.py:347
  62.1 5.7 %all-to-all-done = bf16[64,16,256]{2,0,1:T(8,128)(2,1)S(1)} async-done(((bf16[64,16,256]{2,0,1:T(8,128)(2,1)}), bf16[64,16,256]{2,0,1:T(8,128)(2,1)S(1)}, u32[]{:S(2)}, u32[]{:S(2)}) %all-to-all-start) | async-done | bytes 524320 | tf_op jit(solution)/shard_map/all_to_all | solution.py:336
  69.1 2.8 %copy.95 = f32[16,64,256]{1,0,2:T(8,128)} copy(f32[16,64,256]{2,0,1:T(8,128)S(1)} %convert_bitcast_fusion) | data formatting | bytes 2097152 | tf_op jit(solution)/shard_map/convert_element_type | solution.py:340
  71.9 2.1 reshape.213
  74.4 1.9 mul.132
  76.3 3.8 %copy.102 = f32[16,64,256]{2,0,1:T(8,128)} copy(f32[16,64,256]{1,0,2:T(8,128)} %mul.132) | data formatting | bytes 2097152 | tf_op jit(solution)/shard_map/mul | solution.py:17
  80.2 1.9 sub.43
  82.1 3.9 %copy.101 = f32[16,64,256]{2,0,1:T(8,128)} copy(f32[16,64,256]{1,0,2:T(8,128)} %sub.43) | data formatting | bytes 2097152 | tf_op jit(solution)/shard_map/sub | solution.py:15
  86.1 2.0 multiply_reduce_fusion.1
  89.1 26.4 %all-gather.5.cloned.1.call-done.right_ref = bf16[1024,2176]{1,0:T(8,128)(2,1)} async-done(((bf16[64,2176]{1,0:T(8,128)(2,1)}), bf16[1024,2176]{1,0:T(8,128)(2,1)}) %all-gather.5.cloned.1.call-update) | async-done | bytes 4456464 | tf_op jit(solution)/shard_map/all_gather | solution.py:422
  115.5 15.9 %pair.1 = (f32[2,16,64,128]{3,2,1,0:T(8,128)S(1)}, bf16[2,16,64,128]{3,2,1,0:T(8,128)(2,1)S(1)}, bf16[128,32,128]{2,1,0:T(8,128)(2,1)}) custom-call(bf16[1024,1152]{1,0:T(8,128)(2,1)} %all-gather.3.cloned.1.call-done.left_a_ref.left_b_ref.left_mask_ref, bf16[1024,1152]{1,0:T(8,128)(2,1)} %all-gather.3.cloned.1.call-done.left_a_ref.left_b_ref.left_mask_ref, ...), custom_call_target="tpu_custom_call" | custom-call | tf_op jit(solution)/shard_map/pair/pallas_call | solution.py:206
  131.5 8.5 %all-to-all-start.3 = ((bf16[128,32,128]{2,1,0:T(8,128)(2,1)}), bf16[128,32,128]{2,1,0:T(8,128)(2,1)S(1)}, u32[]{:S(2)}, u32[]{:S(2)}) async-start(bf16[128,32,128]{2,1,0:T(8,128)(2,1)} %get-tuple-element.5), calls=%async_computation.3 | async-start | bytes 2097152 | tf_op jit(solution)/shard_map/all_to_all | solution.py:446
  142.3 2.9 %copy.96 = f32[16,64,256]{2,1,0:T(8,128)} copy(f32[16,64,256]{2,0,1:T(8,128)} %copy-done.5) | data formatting | bytes 2097152 | tf_op jit(solution)/shard_map/convert_element_type | solution.py:340
  147.6 3.2 %copy.104 = f32[4096,64]{0,1:T(8,128)} copy(f32[4096,64]{1,0:T(8,128)} %bitcast.80) | data formatting | bytes 2097152 | tf_op jit(solution)/shard_map/mul | solution.py:373
  153.4 2.7 %reshape.214 = f32[4096,64]{1,0:T(8,128)} reshape(f32[16,64,256]{2,1,0:T(8,128)} %copy.96) | data formatting | bytes 2097152 | tf_op jit(solution)/shard_map/convert_element_type | solution.py:340
  156.1 3.7 %fusion.4 = bf16[4096,64]{0,1:T(8,128)(2,1)} fusion(f32[4096,64]{0,1:T(8,128)} %copy.104, bf16[64,64]{1,0:T(8,128)(2,1)S(1)} %copy-done, f32[4096,64]{1,0:T(8,128)} %reshape.214, f32[64]{0:T(128)S(1)} %copy-done.18, f32[4096]{0:T(1024)S(1)} %rsqrt.21, f32[4096]{0:T(1024)S(1)} %div.34), kind=kOutput, calls=%fused_computation.5 | convolution fusion | flops 35913728 | bytes 2662656 | tf_op jit(solution)/shard_map/dot_general | solution.py:370
  159.8 2.4 %copy.105 = bf16[4096,64]{1,0:T(8,128)(2,1)} copy(bf16[4096,64]{0,1:T(8,128)(2,1)} %fusion.4) | data formatting | bytes 1048576 | tf_op jit(solution)/shard_map/convert_element_type | solution.py:374
  162.2 2.9 %fusion.5 = bf16[1024,4,64]{0,2,1:T(8,128)(2,1)} fusion(f32[1024,4,64]{0,2,1:T(8,128)} %copy-done.4, bf16[1024,4,64]{2,1,0:T(4,128)(2,1)} %bitcast.81, bf16[64,64]{1,0:T(8,128)(2,1)S(1)} %copy-done.11), kind=kOutput, calls=%fused_computation.12 | convolution fusion | flops 34078720 | bytes 2105344 | tf_op jit(solution)/shard_map/dot_general | solution.py:379
  165.0 2.5 %all_to_all.44 = bf16[16,64,256]{1,0,2:T(8,128)(2,1)} reshape(bf16[1024,4,64]{0,2,1:T(8,128)(2,1)} %fusion.5) | data formatting | bytes 1048576 | tf_op jit(solution)/shard_map/all_to_all | solution.py:383
  167.5 2.8 %copy.108 = bf16[16,64,256]{2,1,0:T(8,128)(2,1)} copy(bf16[16,64,256]{1,0,2:T(8,128)(2,1)} %all_to_all.44) | data formatting | bytes 1048576 | tf_op jit(solution)/shard_map/all_to_all | solution.py:383
  170.3 6.6 %all-to-all-start.2 = ((bf16[16,64,256]{2,1,0:T(8,128)(2,1)}), bf16[16,64,256]{2,1,0:T(8,128)(2,1)}, u32[]{:S(2)}, u32[]{:S(2)}) async-start(bf16[16,64,256]{2,1,0:T(8,128)(2,1)} %copy.108), calls=%async_computation.2 | async-start | bytes 1048576 | tf_op jit(solution)/shard_map/all_to_all | solution.py:383
  178.6 10.3 %all-to-all-done.2 = bf16[16,64,256]{2,1,0:T(8,128)(2,1)} async-done(((bf16[16,64,256]{2,1,0:T(8,128)(2,1)}), bf16[16,64,256]{2,1,0:T(8,128)(2,1)}, u32[]{:S(2)}, u32[]{:S(2)}) %all-to-all-start.2) | async-done | bytes 524320 | tf_op jit(solution)/shard_map/all_to_all | solution.py:383
  188.8 6.2 %all-to-all-start.4 = ((bf16[128,16,128]{2,1,0:T(8,128)(2,1)}), bf16[128,16,128]{2,1,0:T(8,128)(2,1)S(1)}, u32[]{:S(2)}, u32[]{:S(2)}) async-start(bf16[128,16,128]{2,1,0:T(8,128)(2,1)} %bitcast.21), calls=%async_computation.4 | async-start | bytes 1048576 | tf_op jit(solution)/shard_map/all_to_all | solution.py:448
  195.2 1.9 copy.123
  197.1 11.5 %all-to-all-done.4.product_ref = bf16[128,16,128]{2,1,0:T(8,128)(2,1)S(1)} async-done(((bf16[128,16,128]{2,1,0:T(8,128)(2,1)}), bf16[128,16,128]{2,1,0:T(8,128)(2,1)S(1)}, u32[]{:S(2)}, u32[]{:S(2)}) %all-to-all-start.4) | async-done | bytes 524320 | tf_op jit(solution)/shard_map/all_to_all | solution.py:448
  208.6 3.0 %finish.1 = f32[2,16,64,128]{3,2,1,0:T(8,128)} custom-call(bf16[128,16,128]{2,1,0:T(8,128)(2,1)S(1)} %all-to-all-done.4.product_ref, f32[2,16,64,128]{3,2,1,0:T(8,128)S(1)} %get-tuple-element.6.mid_ref, bf16[2,16,64,128]{3,2,1,0:T(8,128)(2,1)S(1)} %get-tuple-element.7.source_ref, bf16[128,128]{1,0:T(8,128)(2,1)S(1)} %copy-done.1, ...), custom_call_target="tpu_custom_call" | custom-call | tf_op jit(solution)/shard_map/finish/pallas_call | solution.py:248
  (121 shorter events, 27.1 us)
Async XLA Ops:
  7.2 148.9 %copy-start = (bf16[64,64]{1,0:T(8,128)(2,1)S(1)}, bf16[64,64]{1,0:T(8,128)(2,1)}, u32[]{:S(2)}) copy-start(bf16[64,64]{1,0:T(8,128)(2,1)} %param.30) | copy-start | bytes 24580
  7.2 81.9 %all-gather.3.cloned.1.call-start = ((), (), s32[]{:S(2)}) async-start(), calls=%async_computation.5 | async-start | bytes 2654208 | tf_op jit(solution)/shard_map/all_gather | solution.py:293
  9.2 2.0 copy-start.10
  9.2 2.0 copy-start.13
  9.2 2.0 copy-start.17
  14.0 6.6 %copy-start.14 = (bf16[64,32]{0,1:T(8,128)(2,1)S(1)}, bf16[64,32]{0,1:T(8,128)(2,1)}, u32[]{:S(2)}) copy-start(bf16[64,32]{0,1:T(8,128)(2,1)} %param.34) | copy-start | bytes 12292
  14.4 5.2 %collective-permute-start = (bf16[64,1152]{1,0:T(8,128)(2,1)S(1)}, bf16[64,1152]{1,0:T(8,128)(2,1)S(1)}, u32[]{:S(2)}, u32[]{:S(2)}) collective-permute-start(bf16[64,1152]{1,0:T(8,128)(2,1)S(1)} %get-tuple-element.12), channel_id=1, source_target_pairs={{0,8},{1,24},{2,40},{3,56},{4,72},{5,88},{6,104},{7,120},{8,0},{9,... | collective-permute-start | bytes 442376 | tf_op jit(solution)/shard_map/ppermute | solution.py:291
  16.1 3.6 %collective-permute-start.1 = (bf16[64,1152]{1,0:T(8,128)(2,1)S(1)}, bf16[64,1152]{1,0:T(8,128)(2,1)S(1)}, u32[]{:S(2)}, u32[]{:S(2)}) collective-permute-start(bf16[64,1152]{1,0:T(8,128)(2,1)S(1)} %get-tuple-element.13), channel_id=1, source_target_pairs={{0,0},{1,16},{2,32},{3,48},{4,64},{5,80},{6,96},{7,112},{8,8},{9,2... | collective-permute-start | bytes 442376 | tf_op jit(solution)/shard_map/ppermute | solution.py:290
  20.5 25.0 %copy-start.22 = (s32[512]{0:T(512)S(1)}, s32[512]{0:T(512)}, u32[]{:S(2)}) copy-start(s32[512]{0:T(512)} %param.25) | copy-start | bytes 6148
  20.5 25.2 %copy-start.12 = (s32[32,64]{1,0:T(8,128)S(1)}, s32[32,64]{1,0:T(8,128)}, u32[]{:S(2)}) copy-start(s32[32,64]{1,0:T(8,128)} %param.24) | copy-start | bytes 24580
  20.5 25.3 %copy-start.8 = (bf16[1024,128]{1,0:T(8,128)(2,1)S(1)}, bf16[1024,128]{1,0:T(8,128)(2,1)}, u32[]{:S(2)}) copy-start(bf16[1024,128]{1,0:T(8,128)(2,1)} %param.35) | copy-start | bytes 786436
  20.5 95.0 %all-gather.5.cloned.1.call-start = ((), (), s32[]{:S(2)}) async-start(), calls=%async_computation.6 | async-start | bytes 4734976 | tf_op jit(solution)/shard_map/all_gather | solution.py:422
  22.2 24.0 %copy-start.9 = (bf16[128,512]{1,0:T(8,128)(2,1)S(1)}, bf16[128,512]{1,0:T(8,128)(2,1)}, u32[]{:S(2)}) copy-start(bf16[128,512]{1,0:T(8,128)(2,1)} %param.38) | copy-start | bytes 393220
  22.2 24.2 %copy-start.19 = (f32[2,128]{1,0:T(2,128)S(1)}, f32[2,128]{1,0:T(2,128)}, u32[]{:S(2)}) copy-start(f32[2,128]{1,0:T(2,128)} %param.36) | copy-start | bytes 3076
  22.2 24.3 %copy-start.7 = (bf16[64,4096]{1,0:T(8,128)(2,1)S(1)}, bf16[64,4096]{1,0:T(8,128)(2,1)}, u32[]{:S(2)}) copy-start(bf16[64,4096]{1,0:T(8,128)(2,1)} %param.21) | copy-start | bytes 1572868
  22.7 24.7 %copy-start.18 = (f32[64]{0:T(128)S(1)}, f32[64]{0:T(128)}, u32[]{:S(2)}) copy-start(f32[64]{0:T(128)} %param.26) | copy-start | bytes 772
  24.3 28.6 %all-to-all-start.1 = ((bf16[16,2,128]{2,1,0:T(2,128)(2,1)}), bf16[16,2,128]{2,1,0:T(2,128)(2,1)S(1)}, u32[]{:S(2)}, u32[]{:S(2)}) async-start(bf16[16,2,128]{2,1,0:T(2,128)(2,1)} %reshape.222), calls=%async_computation.1 | async-start | bytes 16384 | tf_op jit(solution)/shard_map/all_to_all | solution.py:337
  52.9 14.9 %all-to-all-start = ((bf16[64,16,256]{2,0,1:T(8,128)(2,1)}), bf16[64,16,256]{2,0,1:T(8,128)(2,1)S(1)}, u32[]{:S(2)}, u32[]{:S(2)}) async-start(bf16[64,16,256]{2,0,1:T(8,128)(2,1)} %bitcast.74), calls=%async_computation | async-start | bytes 1048576 | tf_op jit(solution)/shard_map/all_to_all | solution.py:336
  68.1 1.0 copy-start.5
  74.0 14.5 %copy-start.4 = (f32[1024,4,64]{0,2,1:T(8,128)}, f32[1024,4,64]{0,2,1:T(8,128)S(1)}, u32[]{:S(2)}) copy-start(f32[1024,4,64]{0,2,1:T(8,128)S(1)} %reshape.213) | copy-start | bytes 3145732
  82.1 3.9 %copy-start.6 = (f32[16,64,256]{2,0,1:T(8,128)S(1)}, f32[16,64,256]{2,0,1:T(8,128)}, u32[]{:S(2)}) copy-start(f32[16,64,256]{2,0,1:T(8,128)} %copy.103) | copy-start | bytes 3145732
  86.1 2.1 copy-start.21
  86.1 2.6 %copy-start.15 = (bf16[64,8]{0,1:T(8,128)(2,1)S(1)}, bf16[64,8]{0,1:T(8,128)(2,1)}, u32[]{:S(2)}) copy-start(bf16[64,8]{0,1:T(8,128)(2,1)} %param.28) | copy-start | bytes 3076
  86.1 2.8 %copy-start.16 = (bf16[64,8]{0,1:T(8,128)(2,1)S(1)}, bf16[64,8]{0,1:T(8,128)(2,1)}, u32[]{:S(2)}) copy-start(bf16[64,8]{0,1:T(8,128)(2,1)} %param.29) | copy-start | bytes 3076
  88.1 27.4 %copy-start.3 = (f32[128]{0:T(128)S(1)}, f32[128]{0:T(128)}, u32[]{:S(2)}) copy-start(f32[128]{0:T(128)} %param.37) | copy-start | bytes 1540
  131.5 38.8 %all-to-all-start.3 = ((bf16[128,32,128]{2,1,0:T(8,128)(2,1)}), bf16[128,32,128]{2,1,0:T(8,128)(2,1)S(1)}, u32[]{:S(2)}, u32[]{:S(2)}) async-start(bf16[128,32,128]{2,1,0:T(8,128)(2,1)} %get-tuple-element.5), calls=%async_computation.3 | async-start | bytes 2097152 | tf_op jit(solution)/shard_map/all_to_all | solution.py:446
  156.1 6.1 %copy-start.11 = (bf16[64,64]{1,0:T(8,128)(2,1)S(1)}, bf16[64,64]{1,0:T(8,128)(2,1)}, u32[]{:S(2)}) copy-start(bf16[64,64]{1,0:T(8,128)(2,1)} %param.31) | copy-start | bytes 24580
  170.3 24.8 %copy-start.20 = (f32[128]{0:T(128)S(1)}, f32[128]{0:T(128)}, u32[]{:S(2)}) copy-start(f32[128]{0:T(128)} %param.40) | copy-start | bytes 1540
  170.3 18.6 %all-to-all-start.2 = ((bf16[16,64,256]{2,1,0:T(8,128)(2,1)}), bf16[16,64,256]{2,1,0:T(8,128)(2,1)}, u32[]{:S(2)}, u32[]{:S(2)}) async-start(bf16[16,64,256]{2,1,0:T(8,128)(2,1)} %copy.108), calls=%async_computation.2 | async-start | bytes 1048576 | tf_op jit(solution)/shard_map/all_to_all | solution.py:383
  176.9 31.7 %copy-start.1 = (bf16[128,128]{1,0:T(8,128)(2,1)S(1)}, bf16[128,128]{1,0:T(8,128)(2,1)}, u32[]{:S(2)}) copy-start(bf16[128,128]{1,0:T(8,128)(2,1)} %gate_ref.1) | copy-start | bytes 98308
  176.9 31.7 %copy-start.2 = (bf16[128,128]{1,0:T(8,128)(2,1)S(1)}, bf16[128,128]{1,0:T(8,128)(2,1)}, u32[]{:S(2)}) copy-start(bf16[128,128]{1,0:T(8,128)(2,1)} %final_ref.1) | copy-start | bytes 98308
  188.8 19.8 %all-to-all-start.4 = ((bf16[128,16,128]{2,1,0:T(8,128)(2,1)}), bf16[128,16,128]{2,1,0:T(8,128)(2,1)S(1)}, u32[]{:S(2)}, u32[]{:S(2)}) async-start(bf16[128,16,128]{2,1,0:T(8,128)(2,1)} %bitcast.21), calls=%async_computation.4 | async-start | bytes 1048576 | tf_op jit(solution)/shard_map/all_to_all | solution.py:448
Sparse Core Ops, SparseCore 0:
  20.6 39.2 all-gather.2
  62.0 53.4 all-gather.4

commit v2 on v1

--- a/solution.py
+++ b/solution.py
@@ -7,14 +7,225 @@
 
 LANES = 128
 HALF = 64
+PART_ROWS = 40
 VMEM_LIMIT = 50 * 1024 * 1024
 
 
-def standardize_features(x, gain):
-    mean = jnp.mean(x, -1, keepdims=True)
-    centred = x - mean
-    var = jnp.mean(centred * centred, -1, keepdims=True)
-    return centred * lax.rsqrt(var + 1e-05) * gain
+def row_index(shape):
+    return lax.broadcasted_iota(jnp.int32, shape, 0)
+
+
+def ones_where(keep):
+    return jnp.where(keep, 1.0, 0.0).astype(jnp.bfloat16)
+
+
+def repeat_lanes(w, times):
+    b = w.shape[1]
+    shape = (b, times * b)
+    pick = ones_where(lane_index(shape) % b == row_index(shape))
+    return jnp.dot(w, pick, preferred_element_type=jnp.float32).astype(jnp.bfloat16)
+
+
+def block_diagonal(w, times):
+    a, b = w.shape
+    tall = jnp.concatenate([repeat_lanes(w, times)] * times, axis=0)
+    keep = row_index(tall.shape) // a == lane_index(tall.shape) // b
+    return jnp.where(keep, tall, jnp.zeros_like(tall))
+
+
+def parts_of(x, count):
+    out = []
+    for _ in range(count):
+        part = x.astype(jnp.bfloat16)
+        out.append(part)
+        x = x - part.astype(jnp.float32)
+    return out
+
+
+def project_kernel(
+    msa_ref,
+    cover_ref,
+    focus_gain_ref,
+    dyadic_gain_ref,
+    first_ref,
+    second_ref,
+    left_ref,
+    right_ref,
+    source_ref,
+    sums_ref,
+    turn_ref,
+):
+    odd = lax.axis_index("row") % 2
+    cover = cover_ref[...].astype(jnp.float32)
+    cover_narrow = cover.astype(jnp.bfloat16)
+    cover_turned = jnp.concatenate([cover, cover], axis=0).T
+    square = (256, 256)
+    average = jnp.where(
+        row_index(square) // HALF == lane_index(square) // HALF, 1.0 / HALF, 0.0
+    ).astype(jnp.bfloat16)
+    first = block_diagonal(first_ref[...], 4)
+    second = block_diagonal(second_ref[...], 4)
+    focus_gain = jnp.concatenate([focus_gain_ref[...]] * 4, axis=1)
+    dyadic_gain = jnp.concatenate([dyadic_gain_ref[...]] * 4, axis=1)
+    for q in range(4):
+        x = jnp.concatenate(
+            [msa_ref[:, (4 * q + e) * 256 : (4 * q + e + 1) * 256] for e in range(4)], axis=0
+        )
+        mean = jnp.dot(x, average, preferred_element_type=jnp.float32)
+        centred = x.astype(jnp.float32) - mean
+        high, low = parts_of(centred * centred, 2)
+        var = jnp.dot(high, average, preferred_element_type=jnp.float32) + jnp.dot(
+            low, average, preferred_element_type=jnp.float32
+        )
+        normal = centred * lax.rsqrt(var + 1e-05)
+        focus = (normal * focus_gain).astype(jnp.bfloat16)
+        dyadic = (normal * dyadic_gain).astype(jnp.bfloat16)
+        source_ref[q * 256 : (q + 1) * 256, :] = focus
+        left = lax.dot_general(
+            dyadic, first, (((1,), (1,)), ((), ())), preferred_element_type=jnp.float32
+        )
+        pick = ones_where(row_index((64, 512)) == 16 * q + lane_index((64, 512)) // 32)
+        left_cover = jnp.dot(cover_narrow, pick, preferred_element_type=jnp.float32)
+        right = lax.dot_general(
+            second, dyadic, (((1,), (1,)), ((), ())), preferred_element_type=jnp.float32
+        )
+        pick = ones_where(row_index((64, 1024)) == 16 * q + lane_index((64, 1024)) // 64)
+        focus_cover = jnp.dot(cover_narrow, pick, preferred_element_type=jnp.float32)
+        for e in range(4):
+            g = 4 * q + e
+            rows = slice(e * HALF, (e + 1) * HALF)
+            left_ref[(g // 8 + odd) % 2, :, (g % 8) * LANES : (g % 8 + 1) * LANES] = (
+                left[rows] * left_cover[:, e * LANES : (e + 1) * LANES]
+            ).astype(jnp.bfloat16)
+            here = right[:, (e // 2) * LANES : (e // 2 + 1) * LANES]
+            if e % 2:
+                here = pltpu.roll(here, HALF, 1)
+            for j in range(4):
+                turn_ref[pl.ds(4 * g + j, 32, stride=HALF), :] = (
+                    here[j * 32 : (j + 1) * 32] * cover_turned[4 * g + j : 4 * g + j + 1, :]
+                )
+            wide = focus_cover[:, e * 256 : (e + 1) * 256]
+            total = jnp.sum(wide * focus[rows].astype(jnp.float32), 0, keepdims=True)
+            count = jnp.sum(wide, 0, keepdims=True)
+            for k in range(16):
+                sums_ref[k, g : g + 1, :] = total
+                sums_ref[k, 16 + g : 17 + g, :] = count
+    shape = (64, LANES)
+    for h in range(2):
+        pick = ones_where(
+            (row_index(shape) == 32 * h + lane_index(shape)) & (lane_index(shape) < 32)
+        )
+        left_ref[(h + odd) % 2, :, 1024:1152] = jnp.dot(
+            cover_narrow, pick, preferred_element_type=jnp.float32
+        ).astype(jnp.bfloat16)
+    pick = ones_where(row_index(shape) == lane_index(shape) % HALF)
+    right_ref[:, 2048:2176] = jnp.dot(
+        cover_narrow, pick, preferred_element_type=jnp.float32
+    ).astype(jnp.bfloat16)
+    for d in range(16):
+        turned = turn_ref[d * LANES : (d + 1) * LANES, :].T
+        right_ref[:, d * LANES : (d + 1) * LANES] = turned[:HALF].astype(jnp.bfloat16)
+
+
+def attend_kernel(source_ref, cover_ref, sums_ref, asking_ref, lookup_ref, content_ref, part_ref):
+    sums = sums_ref[0]
+    for k in range(1, 16):
+        sums = sums + sums_ref[k]
+    query_mean = (sums[:16] / jnp.maximum(sums[16:], 1.0)).astype(jnp.bfloat16)
+    query = (
+        jnp.dot(query_mean, block_diagonal(asking_ref[...], 4), preferred_element_type=jnp.float32)
+        * 8 ** (-0.5)
+    )
+    shape = (512, 256)
+    spread = jnp.concatenate([jnp.broadcast_to(query[g : g + 1], (32, 256)) for g in range(16)], 0)
+    spread = jnp.where(row_index(shape) % 32 == lane_index(shape) // 8, spread, 0.0)
+    lookup = jnp.concatenate([lookup_ref[...].astype(jnp.float32)] * 8, axis=0)
+    lookup = block_diagonal(lookup.astype(jnp.bfloat16), 4)
+    ask = sum(
+        jnp.dot(part, lookup, preferred_element_type=jnp.float32) for part in parts_of(spread, 3)
+    )
+    ask_parts = parts_of(ask, 3)
+    logits = []
+    for g in range(16):
+        stacked = jnp.concatenate([part[g * 32 : (g + 1) * 32] for part in ask_parts], axis=0)
+        three = lax.dot_general(
+            stacked,
+            source_ref[g * HALF : (g + 1) * HALF, :],
+            (((1,), (1,)), ((), ())),
+            preferred_element_type=jnp.float32,
+        )
+        logits.append(three[:32] + three[32:64] + three[64:])
+    logits = jnp.concatenate(logits, axis=0)
+    cover = cover_ref[...].astype(jnp.float32).T
+    bias = jnp.where(cover > 0, 0.0, -1000000000.0)
+    logits = logits + jnp.broadcast_to(bias[:, None, :], (64, 8, 64)).reshape(512, 64)
+    top = jnp.max(logits, 1, keepdims=True)
+    weights = jnp.exp(logits - top)
+    total = jnp.sum(weights, 1, keepdims=True)
+    weight_parts = parts_of(weights, 3)
+    mixed = []
+    for g in range(16):
+        stacked = jnp.concatenate([part[g * 32 : (g + 1) * 32] for part in weight_parts], axis=0)
+        three = jnp.dot(
+            stacked, source_ref[g * HALF : (g + 1) * HALF, :], preferred_element_type=jnp.float32
+        )
+        mixed.append(three[:32] + three[32:64] + three[64:])
+    mixed = jnp.concatenate(mixed, axis=0)
+    mixed = jnp.where(row_index(shape) // 8 % 4 == lane_index(shape) // HALF, mixed, 0.0)
+    small = (8, LANES)
+    content = lax.dot_general(
+        content_ref[...],
+        ones_where(lane_index(small) == row_index(small) + 8),
+        (((0,), (0,)), ((), ())),
+        preferred_element_type=jnp.float32,
+    ).astype(jnp.bfloat16)
+    content = jnp.concatenate([content] * 4, axis=0)
+    mixed = sum(
+        jnp.dot(part, content, preferred_element_type=jnp.float32) for part in parts_of(mixed, 3)
+    )
+    lane = lane_index((512, LANES))
+    mixed = jnp.where(lane == 0, top, jnp.where(lane == 1, total, mixed))
+    part_ref[...] = mixed.T[:PART_ROWS]
+
+
+def refresh_kernel(part_ref, source_ref, msa_ref, sigmoid_ref, final_ref, out_ref):
+    parts = [part_ref[k * PART_ROWS : k * PART_ROWS + 16, :] for k in range(16)]
+    top = parts[0][0:1]
+    for k in range(1, 16):
+        top = jnp.maximum(top, parts[k][0:1])
+    merged = jnp.zeros((16, 512), jnp.float32)
+    for k in range(16):
+        merged = merged + parts[k] * jnp.exp(parts[k][0:1] - top)
+    mixed = merged[8:] / merged[1:2]
+    shape = (LANES, 1024)
+    spread = ones_where(row_index(shape) == lane_index(shape) // 8)
+    keep = row_index((8, 1024)) == lane_index((8, 1024)) % 8
+    gate_weight = block_diagonal(sigmoid_ref[...], 4)
+    final_weight = block_diagonal(final_ref[...], 4)
+    for q in range(4):
+        stacked = jnp.concatenate(parts_of(mixed[:, q * LANES : (q + 1) * LANES], 3), axis=0)
+        three = jnp.dot(stacked, spread, preferred_element_type=jnp.float32)
+        wide = jnp.where(keep, three[:8] + three[8:16] + three[16:], 0.0)
+        wide = jnp.sum(wide, 0, keepdims=True)
+        wide = jnp.concatenate(
+            [jnp.broadcast_to(wide[:, e * 256 : (e + 1) * 256], (HALF, 256)) for e in range(4)],
+            axis=0,
+        )
+        gate = jax.nn.sigmoid(
+            jnp.dot(
+                source_ref[q * 256 : (q + 1) * 256, :],
+                gate_weight,
+                preferred_element_type=jnp.float32,
+            )
+        )
+        change = jnp.dot(
+            (gate * wide).astype(jnp.bfloat16), final_weight, preferred_element_type=jnp.float32
+        )
+        for e in range(4):
+            lanes = slice((4 * q + e) * 256, (4 * q + e + 1) * 256)
+            out_ref[:, lanes] = (
+                msa_ref[:, lanes].astype(jnp.float32) + change[e * HALF : (e + 1) * HALF]
+            ).astype(jnp.bfloat16)
 
 
 def lane_index(shape):
@@ -44,11 +255,23 @@
     steps = pl.num_programs(0)
     rows = 4
     low = lane_index((LANES, LANES)) < HALF
+    odd = lax.axis_index("row") % 2
+    col = lax.axis_index("col")
+
+    def in_order(ref):
+        blocks = []
+        for block in range(16):
+            turn = (block // 4 - col // 2 + 4) % 4
+            place = jnp.where(turn == 2, 3, jnp.where(turn == 3, 1, jnp.where(turn == 1, 2, 0)))
+            other = (block // 2 + col) % 2
+            start = other * 512 + place * 128 + (block + odd) % 2 * 64
+            blocks.append(ref[pl.ds(pl.multiple_of(start, HALF), HALF), :])
+        return jnp.concatenate(blocks, axis=0)
 
     @pl.when(step == 0)
     def _():
         both = lax.dot_general(
-            left_mask_ref[...],
+            in_order(left_mask_ref),
             right_ref[:, 2048:2176],
             (((0,), (0,)), ((), ())),
             preferred_element_type=jnp.float32,
@@ -56,7 +279,7 @@
         both = jnp.maximum(both[:32], 1.0)
         count_ref[...] = jnp.where(lane_index((16, LANES)) < HALF, both[:16], both[16:])
 
-    left = jnp.concatenate([left_a_ref[...], left_b_ref[...]], axis=1).T
+    left = jnp.concatenate([in_order(left_a_ref), in_order(left_b_ref)], axis=1).T
     for n in range(8):
         outer_ref[:, n * 256 : (n + 1) * 256] = jnp.dot(
             left, right_ref[:, n * 256 : (n + 1) * 256], preferred_element_type=jnp.float32
@@ -200,6 +423,10 @@
 PARAMS = pltpu.CompilerParams(
     vmem_limit_bytes=VMEM_LIMIT, dimension_semantics=("arbitrary",)
 )
+
+
+def cost(us):
+    return pl.CostEstimate(flops=us * 10**9, bytes_accessed=us * 10**6, transcendentals=0)
 
 
 def pair_call(left, right, final, couple, cover, same, table, gain, mapping):
@@ -231,6 +458,7 @@
             pltpu.VMEM((32 * LANES, LANES), jnp.float32),
         ],
         compiler_params=PARAMS,
+        cost_estimate=cost(16),
         name="pair",
     )(left, left, left, right, final, couple, cover, same, table, gain, mapping)
 
@@ -240,6 +468,7 @@
         triangle_kernel,
         out_shape=jax.ShapeDtypeStruct((16, 8, 16, LANES), jnp.bfloat16),
         compiler_params=pltpu.CompilerParams(vmem_limit_bytes=VMEM_LIMIT),
+        cost_estimate=cost(2),
         name="triangle",
     )(taken)
 
@@ -260,25 +489,60 @@
         out_shape=jax.ShapeDtypeStruct((2, 16, HALF, LANES), jnp.float32),
         scratch_shapes=[pltpu.VMEM((LANES * 16, LANES), jnp.float32)],
         compiler_params=PARAMS,
+        cost_estimate=cost(3),
         name="finish",
     )(product, mid, source, gate, final, gain)
 
 
-def spread_left(left, cover):
-    row, n_row, n_col = lax.axis_index("row"), lax.axis_size("row"), lax.axis_size("col")
-    halves = [
-        jnp.concatenate(
-            [
-                left[:, h * 1024 : (h + 1) * 1024],
-                jnp.pad(cover[:, h * 32 : (h + 1) * 32], ((0, 0), (0, LANES - 32))),
-            ],
-            axis=1,
-        )
-        for h in range(2)
+def project_call(msa, cover, focus_gain, dyadic_gain, first, second):
+    return pl.pallas_call(
+        project_kernel,
+        out_shape=[
+            jax.ShapeDtypeStruct((2, 64, 1152), jnp.bfloat16),
+            jax.ShapeDtypeStruct((64, 2176), jnp.bfloat16),
+            jax.ShapeDtypeStruct((1024, 256), jnp.bfloat16),
+            jax.ShapeDtypeStruct((16, 32, 256), jnp.float32),
+        ],
+        scratch_shapes=[pltpu.VMEM((2048, LANES), jnp.float32)],
+        compiler_params=pltpu.CompilerParams(vmem_limit_bytes=VMEM_LIMIT),
+        cost_estimate=cost(4),
+        name="project",
+    )(msa, cover, focus_gain, dyadic_gain, first, second)
+
+
+def attend_call(source, cover, sums, asking, lookup, content):
+    return pl.pallas_call(
+        attend_kernel,
+        out_shape=jax.ShapeDtypeStruct((PART_ROWS, 512), jnp.float32),
+        compiler_params=pltpu.CompilerParams(vmem_limit_bytes=VMEM_LIMIT),
+        cost_estimate=cost(3),
+        name="attend",
+    )(source, cover, sums, asking, lookup, content)
+
+
+def refresh_call(parts, source, msa, gate, final):
+    return pl.pallas_call(
+        refresh_kernel,
+        out_shape=jax.ShapeDtypeStruct((64, 4096), jnp.bfloat16),
+        compiler_params=pltpu.CompilerParams(vmem_limit_bytes=VMEM_LIMIT),
+        cost_estimate=cost(2),
+        name="refresh",
+    )(parts, source, msa, gate, final)
+
+
+def ring_of_four(block, axis, step):
+    half = block.shape[0] // 2
+    back = lax.ppermute(block, axis, step(1))
+    ahead = lax.ppermute(block, axis, step(-1))
+    opposite = [
+        lax.ppermute(back[:half], axis, step(1)),
+        lax.ppermute(ahead[half:], axis, step(-1)),
     ]
-    odd = row % 2 == 1
-    own = jnp.where(odd, halves[1], halves[0])
-    other = jnp.where(odd, halves[0], halves[1])
+    return jnp.concatenate([block, back, ahead] + opposite, axis=0)
+
+
+def spread_left(left):
+    n_row, n_col = lax.axis_size("row"), lax.axis_size("col")
 
     def route(flip):
         return [
@@ -287,10 +551,15 @@
             for c in range(n_col)
         ]
 
-    own = lax.ppermute(own, ("row", "col"), route(0))
-    other = lax.ppermute(other, ("row", "col"), route(1))
-    both = jnp.concatenate([jnp.where(odd, other, own), jnp.where(odd, own, other)], axis=0)
-    return lax.all_gather(both, "col", axis=0, tiled=True)
+    def along(step):
+        return [(c, (c + 2 * step) % n_col) for c in range(n_col)]
+
+    both = jnp.concatenate(
+        [lax.ppermute(left[flip], ("row", "col"), route(flip)) for flip in range(2)], axis=0
+    )
+    gathered = ring_of_four(both, "col", along)
+    swapped = lax.ppermute(gathered, "col", [(c, c ^ 1) for c in range(n_col)])
+    return jnp.concatenate([gathered, swapped], axis=0)
 
 
 def halves_on_lanes(grid):
@@ -320,106 +589,37 @@
     trio_middle_scaling,
     trio_final_factor,
 ):
-    hi = lax.Precision.HIGHEST
     n_row = lax.axis_size("row")
     n_col = lax.axis_size("col")
-    alignments_each_device, vertical_aminos = supplement_align_cover.shape
+    vertical_aminos = supplement_align_cover.shape[1]
     rows_res = couple_tensor.shape[0]
-    align_feature_length = focus_scaling_vector.shape[0]
-    head_dim = focus_lookup_factor.shape[1]
-    heads = focus_asking_factor.shape[1] // head_dim
     width_o = dyadic_first_factor.shape[1]
     width_z = couple_tensor.shape[2]
     width_t = trio_final_factor.shape[0]
-    split_cover_lines = supplement_align_cover.astype(jnp.bfloat16)
-    dispatched, sent_mask = (
-        lax.all_to_all(alignment_tensor, "row", split_axis=1, concat_axis=0, tiled=True),
-        lax.all_to_all(split_cover_lines, "row", split_axis=1, concat_axis=0, tiled=True),
-    )
-    alignments_total, amino_swap = sent_mask.shape
-    align_verticals = dispatched.reshape(alignments_total, amino_swap, align_feature_length).astype(
-        jnp.float32
-    )
-    covered_contents = sent_mask.astype(jnp.float32)
-    focus_source = standardize_features(align_verticals, focus_scaling_vector).astype(jnp.bfloat16)
-    counts = jnp.maximum(jnp.sum(covered_contents, 0), 1.0)
-    query_mean = (
-        jnp.sum(covered_contents[:, :, None] * focus_source.astype(jnp.float32), 0)
-        / counts[:, None]
-    ).astype(jnp.bfloat16)
-    query = (
-        jnp.dot(query_mean, focus_asking_factor, preferred_element_type=jnp.float32)
-        * head_dim ** (-0.5)
-    ).reshape(amino_swap, heads, head_dim)
-    flattened_source = focus_source.reshape(alignments_total * amino_swap, align_feature_length)
-    keys = jnp.dot(
-        flattened_source, focus_lookup_factor, preferred_element_type=jnp.float32
-    ).reshape(alignments_total, amino_swap, head_dim)
-    values = jnp.dot(
-        flattened_source, focus_content_factor, preferred_element_type=jnp.float32
-    ).reshape(alignments_total, amino_swap, head_dim)
-    logits = jnp.einsum("rhd,srd->rhs", query, keys, precision=hi)
-    logits = logits + jnp.where(covered_contents.T[:, None, :] > 0, 0.0, -1000000000.0).astype(
-        jnp.float32
-    )
-    weights = jax.nn.softmax(logits, -1)
-    mixed = jnp.einsum("rhs,srd->rhd", weights, values, precision=hi).reshape(
-        amino_swap, heads * head_dim
-    )
-    gates = jax.nn.sigmoid(
-        jnp.dot(flattened_source, focus_sigmoid_factor, preferred_element_type=jnp.float32)
-    ).reshape(alignments_total, amino_swap, heads * head_dim)
-    sigmoid_scaled_result = (
-        (gates * mixed[None])
-        .astype(jnp.bfloat16)
-        .reshape(alignments_total * amino_swap, heads * head_dim)
-    )
-    refreshed = (
-        align_verticals
-        + jnp.dot(
-            sigmoid_scaled_result, focus_final_factor, preferred_element_type=jnp.float32
-        ).reshape(alignments_total, amino_swap, align_feature_length)
-    ).astype(jnp.bfloat16)
-    refreshed_supplement_align = lax.all_to_all(
-        refreshed.reshape(alignments_total, amino_swap * align_feature_length),
-        "row",
-        split_axis=0,
-        concat_axis=1,
-        tiled=True,
-    )
-    device_align_slice = alignment_tensor.reshape(
-        alignments_each_device, vertical_aminos, align_feature_length
-    ).astype(jnp.float32)
-    device_cover_slice = supplement_align_cover.astype(jnp.float32)
-    product_source = (
-        standardize_features(device_align_slice, dyadic_scaling_vector)
-        .astype(jnp.bfloat16)
-        .reshape(alignments_each_device * vertical_aminos, align_feature_length)
-    )
-    left = (
-        (
-            jnp.dot(
-                product_source, dyadic_first_factor, preferred_element_type=jnp.float32
-            ).reshape(alignments_each_device, vertical_aminos, width_o)
-            * device_cover_slice[:, :, None]
-        )
-        .astype(jnp.bfloat16)
-        .reshape(alignments_each_device, vertical_aminos * width_o)
-    )
-    right = (
-        (
-            jnp.dot(
-                product_source, dyadic_second_factor, preferred_element_type=jnp.float32
-            ).reshape(alignments_each_device, vertical_aminos, width_o)
-            * device_cover_slice[:, :, None]
-        )
-        .astype(jnp.bfloat16)
-        .transpose(0, 2, 1)
-        .reshape(alignments_each_device, vertical_aminos * width_o)
-    )
-    right = jnp.concatenate([right, split_cover_lines, split_cover_lines], axis=1)
-    left_rows = spread_left(left, split_cover_lines)
+    left, right, source, sums = project_call(
+        alignment_tensor,
+        supplement_align_cover,
+        focus_scaling_vector.reshape(1, HALF),
+        dyadic_scaling_vector.reshape(1, HALF),
+        dyadic_first_factor.T,
+        dyadic_second_factor.T,
+    )
     right_all = lax.all_gather(right, "row", axis=0, tiled=True)
+    sums = lax.all_to_all(sums, "row", 0, 0, tiled=True)
+    left, sums = lax.optimization_barrier((left, sums))
+    parts = attend_call(
+        source,
+        supplement_align_cover,
+        sums,
+        focus_asking_factor,
+        focus_lookup_factor.T,
+        focus_content_factor.T,
+    )
+    left_rows, parts = lax.optimization_barrier((spread_left(left), parts))
+    parts = lax.all_gather(parts, "row", axis=0, tiled=True)
+    refreshed_supplement_align = refresh_call(
+        parts, source, alignment_tensor, focus_sigmoid_factor, focus_final_factor
+    )
     chain_rows = lax.dynamic_slice_in_dim(
         amino_strand_label, lax.axis_index("row") * rows_res, rows_res, 0
     )

time: 220 us -> 156 us (0.71)
  blocking collectives: 0 us -> 48.4 us
  local copies, waits for them, and re-layouts: 55.1 us -> 13.7 us
  waiting for transfers between devices: 62.4 us -> 24.1 us
  starting transfers between devices: 48.6 us -> 26.2 us
  matrix products: 11.2 us -> 0 us
  Pallas kernels: 20.6 us -> 28 us
  other arithmetic: 6.02 us -> 0.15 us
    all_to_all x0 -> x2, blocking collectives: none -> 48.4 us  [the longest x1 28.7 us: local(): taken = lax.all_to_all(sides, ('row', 'col'), 0, 0, tiled=True)]
    all_to_all x4 -> x0, starting transfers between devices: 40 us -> none  [the longest x1 21.1 us: local(): lax.all_to_all(split_cover_lines, 'row', split_axis=1, concat_axis=0, til...]
    all_gather x1, waiting for transfers between devices: 26.4 us -> 0.02 us  [local(): right_all = lax.all_gather(right, 'row', axis=0, tiled=True)]
    all_to_all x4 -> x0, waiting for transfers between devices: 21.5 us -> none  [the longest x1 10.3 us: local(): lax.all_to_all(refreshed.reshape(alignments_total, amino_swap * align_fea...]
    ppermute x2 -> x7, starting transfers between devices: 2.31 us -> 21.5 us  [the longest x1 11.3 us: ring_of_four(): back = lax.ppermute(block, axis, step(1))]
    convert_element_type x10 -> x0, local copies, waits for them, and re-layouts: 16 us -> none  [the longest x4 10.5 us: local(): dispatched.reshape(alignments_total, amino_swap, align_feature_length)]
    mul x11 -> x0, local copies, waits for them, and re-layouts: 15.9 us -> none  [the longest x5 5.9 us: standardize_features(): return centred * lax.rsqrt(var + 1e-05) * gain]
    dot_general x9 -> x0, matrix products: 11.2 us -> none  [the longest x1 3.73 us: local(): jnp.dot(flattened_source, focus_sigmoid_factor, preferred_element_type=jn...]
  transfers between devices with their start and end apart: 9 -> 10, of which waited for: 6 -> 4; matrix products, arithmetic and copies ran while one was open for 28% -> 4% of each run, Pallas kernels for 1% -> 14%
where the time goes in v2:
time: 156 us; the launch traced here: 155 us
  blocking collectives  48.4 us (31%)
  Pallas kernels  28 us (18%)
  starting transfers between devices  26.2 us (17%)
  waiting for transfers between devices  24.1 us (15%)
  between operations  14.3 us (9%)
  local copies, waits for them, and re-layouts  13.7 us (9%)
    all_to_all x1, blocking collectives, local(): taken = lax.all_to_all(sides, ('row', 'col'), 0, 0, tiled=True)  28.7 us
    all_to_all x1, blocking collectives, local(): sums = lax.all_to_all(sums, 'row', 0, 0, tiled=True)  19.7 us
    pallas_call x1, Pallas kernels, pair_call(): pl.pallas_call(pair_kernel, grid=(4,), in_specs=[pl.BlockSpec((1024, LANE...  15.2 us
    ppermute x1, starting transfers between devices, ring_of_four(): back = lax.ppermute(block, axis, step(1))  11.3 us
    unnamed x56, local copies, waits for them, and re-layouts  11.2 us
    all_to_all x1, waiting for transfers between devices, local(): lax.all_to_all(product.reshape(n_row * n_col, 16, LANES), ('row', 'col'),...  10.1 us
    ppermute x1, waiting for transfers between devices, ring_of_four(): back = lax.ppermute(block, axis, step(1))  6.28 us
    ppermute x2, waiting for transfers between devices, spread_left(): lax.ppermute(left[flip], ('row', 'col'), route(flip))  6.24 us
  transfers between devices with their start and end apart: 10, of which 4 were waited for; matrix products, arithmetic and copies ran while one was open for 4% of the time, Pallas kernels for 14%

profile of v2, /device:TPU:0, one launch (start us, length us, event | category | flops | bytes accessed | tf_op | source)
XLA Modules:
  0.0 154.9 jit_solution(10741807074721493693)
XLA Ops:
  7.2 1.0 copy-done.1
  8.3 0.8 copy-done.3
  9.0 0.7 copy-done.10
  9.7 0.7 copy-done.11
  10.4 0.7 copy-done.14
  11.1 0.7 copy-done.15
  11.7 3.7 %project.1 = (bf16[2,64,1152]{2,1,0:T(8,128)(2,1)S(1)}, bf16[64,2176]{1,0:T(8,128)(2,1)}, bf16[1024,256]{1,0:T(8,128)(2,1)S(1)}, f32[16,32,256]{2,1,0:T(8,128)S(1)}) custom-call(bf16[64,4096]{1,0:T(8,128)(2,1)S(1)} %copy-done.1, s32[64,64]{1,0:T(8,128)S(1)} %copy-done.3, f32[1,64]{1,0:T(1,128)S(1)} %bitcast.34, f32[1,64]{1,0:T(1,128)S(1)} %bitcast.35, ...), custom_call_target="tpu_custom_call" | custom-call | flops 4000000000 | bytes 4000000 | tf_op jit(solution)/shard_map/project/pallas_call | solution.py:498
  15.5 19.7 %all_to_all.15.sums_ref = f32[16,32,256]{2,1,0:T(8,128)S(1)} all-to-all(f32[16,32,256]{2,1,0:T(8,128)S(1)} %get-tuple-element.14), channel_id=1, replica_groups=mesh['row'=16,'col'=8] {'row'}, dimensions={0} | all-to-all | bytes 1048576 | tf_op jit(solution)/shard_map/all_to_all | solution.py:608
  35.2 0.8 collective-permute-start
  36.4 0.7 constant_dynamic-update-slice_fusion.7
  37.1 6.2 %collective-permute-done.1 = bf16[64,1152]{1,0:T(8,128)(2,1)S(1)} collective-permute-done((bf16[64,1152]{1,0:T(8,128)(2,1)S(1)}, bf16[64,1152]{1,0:T(8,128)(2,1)S(1)}, u32[]{:S(2)}, u32[]{:S(2)}) %collective-permute-start.1) | collective-permute-done | bytes 147488 | tf_op jit(solution)/shard_map/ppermute | solution.py:558
  43.3 0.7 constant_dynamic-update-slice_fusion.6
  44.0 11.3 %collective-permute-start.2 = (bf16[128,1152]{1,0:T(8,128)(2,1)S(1)}, bf16[128,1152]{1,0:T(8,128)(2,1)S(1)}, u32[]{:S(2)}, u32[]{:S(2)}) collective-permute-start(bf16[128,1152]{1,0:T(8,128)(2,1)S(1)} %get-tuple-element.36), channel_id=1, source_target_pairs={{0,2},{1,3},{2,4},{3,5},{4,6},{5,7},{6,0},{7,1},{8,10},{9,11},{10,... | collective-permute-start | bytes 884744 | tf_op jit(solution)/shard_map/ppermute | solution.py:535
  55.3 5.7 %collective-permute-start.3 = (bf16[128,1152]{1,0:T(8,128)(2,1)S(1)}, bf16[128,1152]{1,0:T(8,128)(2,1)S(1)}, u32[]{:S(2)}, u32[]{:S(2)}) collective-permute-start(bf16[128,1152]{1,0:T(8,128)(2,1)S(1)} %get-tuple-element.36), channel_id=1, source_target_pairs={{0,6},{1,7},{2,0},{3,1},{4,2},{5,3},{6,4},{7,5},{8,14},{9,15},{10,... | collective-permute-start | bytes 884744 | tf_op jit(solution)/shard_map/ppermute | solution.py:536
  61.0 6.3 %collective-permute-done.2 = bf16[128,1152]{1,0:T(8,128)(2,1)S(1)} collective-permute-done((bf16[128,1152]{1,0:T(8,128)(2,1)S(1)}, bf16[128,1152]{1,0:T(8,128)(2,1)S(1)}, u32[]{:S(2)}, u32[]{:S(2)}) %collective-permute-start.2) | collective-permute-done | bytes 294944 | tf_op jit(solution)/shard_map/ppermute | solution.py:535
  67.4 3.3 %collective-permute-start.5 = (bf16[64,1152]{1,0:T(8,128)(2,1)S(1)}, bf16[64,1152]{1,0:T(8,128)(2,1)S(1)}, u32[]{:S(2)}, u32[]{:S(2)}) collective-permute-start(bf16[64,1152]{1,0:T(8,128)(2,1)S(1)} %slice.33), channel_id=1, source_target_pairs={{0,6},{1,7},{2,0},{3,1},{4,2},{5,3},{6,4},{7,5},{8,14},{9,15},{10,... | collective-permute-start | bytes 442376 | tf_op jit(solution)/shard_map/ppermute | solution.py:539
  70.7 0.8 constant_dynamic-update-slice_fusion.5
  71.5 0.8 constant_dynamic-update-slice_fusion.4
  72.3 1.4 collective-permute-done.4
  73.7 0.7 constant_dynamic-update-slice_fusion.3
  74.4 0.7 constant_dynamic-update-slice_fusion.2
  75.1 1.5 copy-done.20
  77.6 2.5 %attend.1 = f32[40,512]{1,0:T(8,128)} custom-call(bf16[1024,256]{1,0:T(8,128)(2,1)S(1)} %get-tuple-element.16.source_ref, s32[64,64]{1,0:T(8,128)S(1)} %copy-done.4, f32[16,32,256]{2,1,0:T(8,128)S(1)} %all_to_all.15.sums_ref, bf16[64,64]{1,0:T(8,128)(2,1)S(1)} %copy-done.7, bf16[8,64]{1,0:T(8,128)(2,1)S(1)} %bitcast.32, bf16[8,64]{1,0:T(8,128)(2,1)S(1)} %bitcast.33), custom_call_target="tpu_custom_call" | custom-call | flops 3000000000 | bytes 3000000 | tf_op jit(solution)/shard_map/attend/pallas_call | solution.py:514
  80.1 1.1 constant_dynamic-update-slice_fusion.8.left_a_ref.left_b_ref.left_mask_ref
  81.3 15.2 %pair.1 = (f32[2,16,64,128]{3,2,1,0:T(8,128)S(1)}, bf16[2,16,64,128]{3,2,1,0:T(8,128)(2,1)S(1)}, bf16[128,32,128]{2,1,0:T(8,128)(2,1)S(1)}) custom-call(bf16[1024,1152]{1,0:T(8,128)(2,1)} %constant_dynamic-update-slice_fusion.8.left_a_ref.left_b_ref.left_mask_ref, bf16[1024,1152]{1,0:T(8,128)(2,1)} %constant_dynamic-update-slice_fusion.8.left_a_ref.left_b_ref.left_mask_ref, ...), custom_call_target="tpu_custom_call" | custom-call | flops 16000000000 | bytes 16000000 | tf_op jit(solution)/shard_map/pair/pallas_call | solution.py:433
  96.5 28.7 %all_to_all.16 = bf16[128,32,128]{2,1,0:T(8,128)(2,1)S(1)} all-to-all(bf16[128,32,128]{2,1,0:T(8,128)(2,1)S(1)} %get-tuple-element.21), channel_id=1, replica_groups=mesh['row'=16,'col'=8] {'row','col'}, dimensions={0} | all-to-all | bytes 2097152 | tf_op jit(solution)/shard_map/all_to_all | solution.py:646
  125.3 1.6 %triangle.1 = bf16[16,8,16,128]{3,2,1,0:T(8,128)(2,1)} custom-call(bf16[16,8,32,128]{3,2,1,0:T(8,128)(2,1)S(1)} %bitcast.27), custom_call_target="tpu_custom_call" | custom-call | flops 2000000000 | bytes 2000000 | tf_op jit(solution)/shard_map/triangle/pallas_call | solution.py:467
  126.9 4.6 %all-to-all-start.2 = ((bf16[128,16,128]{2,1,0:T(8,128)(2,1)}), bf16[128,16,128]{2,1,0:T(8,128)(2,1)S(1)}, u32[]{:S(2)}, u32[]{:S(2)}) async-start(bf16[128,16,128]{2,1,0:T(8,128)(2,1)} %bitcast.15), calls=%async_computation.2 | async-start | bytes 1048576 | tf_op jit(solution)/shard_map/all_to_all | solution.py:648
  131.7 1.3 copy-done
  133.0 1.9 %refresh.1 = bf16[64,4096]{1,0:T(8,128)(2,1)} custom-call(f32[640,512]{1,0:T(8,128)S(1)} %copy-done, bf16[1024,256]{1,0:T(8,128)(2,1)S(1)} %get-tuple-element.16.source_ref, bf16[64,4096]{1,0:T(8,128)(2,1)S(1)} %copy-done.2, bf16[64,64]{1,0:T(8,128)(2,1)S(1)} %copy-done.8, bf16[64,64]{1,0:T(8,128)(2,1)S(1)} %copy-done.9), custom_call_target="tpu_custom_call" | custom-call | flops 2000000000 | bytes 2000000 | tf_op jit(solution)/shard_map/refresh/pallas_call | solution.py:524
  135.0 10.1 %all-to-all-done.2.product_ref = bf16[128,16,128]{2,1,0:T(8,128)(2,1)S(1)} async-done(((bf16[128,16,128]{2,1,0:T(8,128)(2,1)}), bf16[128,16,128]{2,1,0:T(8,128)(2,1)S(1)}, u32[]{:S(2)}, u32[]{:S(2)}) %all-to-all-start.2) | async-done | bytes 524320 | tf_op jit(solution)/shard_map/all_to_all | solution.py:648
  145.0 3.0 %finish.1 = f32[2,16,64,128]{3,2,1,0:T(8,128)} custom-call(bf16[128,16,128]{2,1,0:T(8,128)(2,1)S(1)} %all-to-all-done.2.product_ref, f32[2,16,64,128]{3,2,1,0:T(8,128)S(1)} %get-tuple-element.22.mid_ref, bf16[2,16,64,128]{3,2,1,0:T(8,128)(2,1)S(1)} %get-tuple-element.23.source_ref, bf16[128,128]{1,0:T(8,128)(2,1)S(1)} %copy-done.5, ...), custom_call_target="tpu_custom_call" | custom-call | flops 3000000000 | bytes 3000000 | tf_op jit(solution)/shard_map/finish/pallas_call | solution.py:477
  (69 shorter events, 1.9 us)
Async XLA Ops:
  7.2 74.1 %all-gather.5.cloned.1.call-start = ((), (), s32[]{:S(2)}) async-start(), calls=%async_computation.4 | async-start | bytes 4734976 | tf_op jit(solution)/shard_map/all_gather | solution.py:607
  7.2 1.0 copy-start.1
  8.3 0.8 copy-start.3
  9.0 0.7 copy-start.10
  9.7 0.7 copy-start.11
  15.4 116.2 %all-gather.3.cloned.1.call-start = ((), (), s32[]{:S(2)}) async-start(), calls=%async_computation.3 | async-start | bytes 1392640 | tf_op jit(solution)/shard_map/all_gather | solution.py:619
  35.2 41.4 %copy-start.17 = (bf16[1024,128]{1,0:T(8,128)(2,1)S(1)}, bf16[1024,128]{1,0:T(8,128)(2,1)}, u32[]{:S(2)}) copy-start(bf16[1024,128]{1,0:T(8,128)(2,1)} %param.35) | copy-start | bytes 786436
  35.2 1.2 collective-permute-start
  36.0 7.4 %collective-permute-start.1 = (bf16[64,1152]{1,0:T(8,128)(2,1)S(1)}, bf16[64,1152]{1,0:T(8,128)(2,1)S(1)}, u32[]{:S(2)}, u32[]{:S(2)}) collective-permute-start(bf16[64,1152]{1,0:T(8,128)(2,1)S(1)} %get-tuple-element.28), channel_id=1, source_target_pairs={{0,8},{1,24},{2,40},{3,56},{4,72},{5,88},{6,104},{7,120},{8,0},{9,... | collective-permute-start | bytes 442376 | tf_op jit(solution)/shard_map/ppermute | solution.py:558
  44.0 33.0 %copy-start.19 = (s32[32,64]{1,0:T(8,128)S(1)}, s32[32,64]{1,0:T(8,128)}, u32[]{:S(2)}) copy-start(s32[32,64]{1,0:T(8,128)} %param.24) | copy-start | bytes 24580
  44.0 23.2 %collective-permute-start.2 = (bf16[128,1152]{1,0:T(8,128)(2,1)S(1)}, bf16[128,1152]{1,0:T(8,128)(2,1)S(1)}, u32[]{:S(2)}, u32[]{:S(2)}) collective-permute-start(bf16[128,1152]{1,0:T(8,128)(2,1)S(1)} %get-tuple-element.36), channel_id=1, source_target_pairs={{0,2},{1,3},{2,4},{3,5},{4,6},{5,7},{6,0},{7,1},{8,10},{9,11},{10,... | collective-permute-start | bytes 884744 | tf_op jit(solution)/shard_map/ppermute | solution.py:535
  55.3 12.1 %collective-permute-start.3 = (bf16[128,1152]{1,0:T(8,128)(2,1)S(1)}, bf16[128,1152]{1,0:T(8,128)(2,1)S(1)}, u32[]{:S(2)}, u32[]{:S(2)}) collective-permute-start(bf16[128,1152]{1,0:T(8,128)(2,1)S(1)} %get-tuple-element.36), channel_id=1, source_target_pairs={{0,6},{1,7},{2,0},{3,1},{4,2},{5,3},{6,4},{7,5},{8,14},{9,15},{10,... | collective-permute-start | bytes 884744 | tf_op jit(solution)/shard_map/ppermute | solution.py:536
  67.3 9.8 %copy-start.23 = (s32[512]{0:T(512)S(1)}, s32[512]{0:T(512)}, u32[]{:S(2)}) copy-start(s32[512]{0:T(512)} %param.25) | copy-start | bytes 6148
  67.3 9.9 %copy-start.21 = (f32[2,128]{1,0:T(2,128)S(1)}, f32[2,128]{1,0:T(2,128)}, u32[]{:S(2)}) copy-start(f32[2,128]{1,0:T(2,128)} %param.36) | copy-start | bytes 3076
  67.3 10.0 %copy-start.18 = (bf16[128,512]{1,0:T(8,128)(2,1)S(1)}, bf16[128,512]{1,0:T(8,128)(2,1)}, u32[]{:S(2)}) copy-start(bf16[128,512]{1,0:T(8,128)(2,1)} %param.38) | copy-start | bytes 393220
  67.3 6.4 %collective-permute-start.4 = (bf16[64,1152]{1,0:T(8,128)(2,1)S(1)}, bf16[64,1152]{1,0:T(8,128)(2,1)S(1)}, u32[]{:S(2)}, u32[]{:S(2)}) collective-permute-start(bf16[64,1152]{1,0:T(8,128)(2,1)S(1)} %slice.32), channel_id=1, source_target_pairs={{0,2},{1,3},{2,4},{3,5},{4,6},{5,7},{6,0},{7,1},{8,10},{9,11},{10,... | collective-permute-start | bytes 442376 | tf_op jit(solution)/shard_map/ppermute | solution.py:538
  67.4 7.0 %collective-permute-start.5 = (bf16[64,1152]{1,0:T(8,128)(2,1)S(1)}, bf16[64,1152]{1,0:T(8,128)(2,1)S(1)}, u32[]{:S(2)}, u32[]{:S(2)}) collective-permute-start(bf16[64,1152]{1,0:T(8,128)(2,1)S(1)} %slice.33), channel_id=1, source_target_pairs={{0,6},{1,7},{2,0},{3,1},{4,2},{5,3},{6,4},{7,5},{8,14},{9,15},{10,... | collective-permute-start | bytes 442376 | tf_op jit(solution)/shard_map/ppermute | solution.py:539
  70.7 6.9 %copy-start.4 = (s32[64,64]{1,0:T(8,128)S(1)}, s32[64,64]{1,0:T(8,128)}, u32[]{:S(2)}) copy-start(s32[64,64]{1,0:T(8,128)} %cover_ref.3) | copy-start | bytes 49156
  70.7 6.9 %copy-start.7 = (bf16[64,64]{1,0:T(8,128)(2,1)S(1)}, bf16[64,64]{1,0:T(8,128)(2,1)}, u32[]{:S(2)}) copy-start(bf16[64,64]{1,0:T(8,128)(2,1)} %asking_ref.1) | copy-start | bytes 24580
  70.7 6.9 %copy-start.12 = (bf16[64,8]{0,1:T(8,128)(2,1)S(1)}, bf16[64,8]{0,1:T(8,128)(2,1)}, u32[]{:S(2)}) copy-start(bf16[64,8]{0,1:T(8,128)(2,1)} %param.28) | copy-start | bytes 3076
  70.7 6.9 %copy-start.13 = (bf16[64,8]{0,1:T(8,128)(2,1)S(1)}, bf16[64,8]{0,1:T(8,128)(2,1)}, u32[]{:S(2)}) copy-start(bf16[64,8]{0,1:T(8,128)(2,1)} %param.29) | copy-start | bytes 3076
  75.1 1.5 copy-start.20
  76.5 3.6 %collective-permute-start.6 = (bf16[512,1152]{1,0:T(8,128)(2,1)}, bf16[512,1152]{1,0:T(8,128)(2,1)S(1)}, u32[]{:S(2)}, u32[]{:S(2)}) collective-permute-start(bf16[512,1152]{1,0:T(8,128)(2,1)} %get-tuple-element.30), channel_id=1, source_target_pairs={{0,1},{1,0},{2,3},{3,2},{4,5},{5,4},{6,7},{7,6},{8,9},{9,8},{10,11... | collective-permute-start | bytes 3538952 | tf_op jit(solution)/shard_map/ppermute | solution.py:561
  80.1 1.2 copy-start.16
  125.3 6.3 %copy-start.22 = (f32[128]{0:T(128)S(1)}, f32[128]{0:T(128)}, u32[]{:S(2)}) copy-start(f32[128]{0:T(128)} %param.40) | copy-start | bytes 1540
  125.3 6.4 %copy-start.2 = (bf16[64,4096]{1,0:T(8,128)(2,1)S(1)}, bf16[64,4096]{1,0:T(8,128)(2,1)}, u32[]{:S(2)}) copy-start(bf16[64,4096]{1,0:T(8,128)(2,1)} %msa_ref.3) | copy-start | bytes 1572868
  125.3 6.4 %copy-start.8 = (bf16[64,64]{1,0:T(8,128)(2,1)S(1)}, bf16[64,64]{1,0:T(8,128)(2,1)}, u32[]{:S(2)}) copy-start(bf16[64,64]{1,0:T(8,128)(2,1)} %sigmoid_ref.1) | copy-start | bytes 24580
  125.3 6.4 %copy-start.9 = (bf16[64,64]{1,0:T(8,128)(2,1)S(1)}, bf16[64,64]{1,0:T(8,128)(2,1)}, u32[]{:S(2)}) copy-start(bf16[64,64]{1,0:T(8,128)(2,1)} %final_ref.2) | copy-start | bytes 24580
  126.9 18.1 %all-to-all-start.2 = ((bf16[128,16,128]{2,1,0:T(8,128)(2,1)}), bf16[128,16,128]{2,1,0:T(8,128)(2,1)S(1)}, u32[]{:S(2)}, u32[]{:S(2)}) async-start(bf16[128,16,128]{2,1,0:T(8,128)(2,1)} %bitcast.15), calls=%async_computation.2 | async-start | bytes 1048576 | tf_op jit(solution)/shard_map/all_to_all | solution.py:648
  131.7 1.3 copy-start
  133.0 12.0 %copy-start.5 = (bf16[128,128]{1,0:T(8,128)(2,1)S(1)}, bf16[128,128]{1,0:T(8,128)(2,1)}, u32[]{:S(2)}) copy-start(bf16[128,128]{1,0:T(8,128)(2,1)} %gate_ref.1) | copy-start | bytes 98308
  133.0 12.0 %copy-start.6 = (bf16[128,128]{1,0:T(8,128)(2,1)S(1)}, bf16[128,128]{1,0:T(8,128)(2,1)}, u32[]{:S(2)}) copy-start(bf16[128,128]{1,0:T(8,128)(2,1)} %final_ref.3) | copy-start | bytes 98308
  (2 other events, 1.3 us)
Sparse Core Ops, SparseCore 0:
  15.5 65.5 all-gather.4
  83.3 46.7 all-gather.2

commit v3 on v2

--- a/solution.py
+++ b/solution.py
@@ -9,6 +9,7 @@
 HALF = 64
 PART_ROWS = 40
 VMEM_LIMIT = 50 * 1024 * 1024
+ALL_VMEM = 64 * 1024 * 1024 - 8192
 
 
 def row_index(shape):
@@ -106,10 +107,12 @@
                 )
             wide = focus_cover[:, e * 256 : (e + 1) * 256]
             total = jnp.sum(wide * focus[rows].astype(jnp.float32), 0, keepdims=True)
-            count = jnp.sum(wide, 0, keepdims=True)
             for k in range(16):
                 sums_ref[k, g : g + 1, :] = total
-                sums_ref[k, 16 + g : 17 + g, :] = count
+    count = jnp.sum(cover, 0, keepdims=True)
+    for k in range(16):
+        sums_ref[k, 16:, :] = jnp.zeros((8, 256), jnp.float32)
+        sums_ref[k, 16:17, :HALF] = count
     shape = (64, LANES)
     for h in range(2):
         pick = ones_where(
@@ -131,7 +134,15 @@
     sums = sums_ref[0]
     for k in range(1, 16):
         sums = sums + sums_ref[k]
-    query_mean = (sums[:16] / jnp.maximum(sums[16:], 1.0)).astype(jnp.bfloat16)
+    count = jnp.broadcast_to(sums[16:17, :HALF], (16, HALF))
+    shape = (16, HALF)
+    count = jnp.where(lane_index(shape) // 4 == row_index(shape), count, 0.0)
+    shape = (HALF, 256)
+    pick = ones_where(row_index(shape) % 4 == lane_index(shape) // HALF)
+    count = sum(
+        jnp.dot(part, pick, preferred_element_type=jnp.float32) for part in parts_of(count, 2)
+    )
+    query_mean = (sums[:16] / jnp.maximum(count, 1.0)).astype(jnp.bfloat16)
     query = (
         jnp.dot(query_mean, block_diagonal(asking_ref[...], 4), preferred_element_type=jnp.float32)
         * 8 ** (-0.5)
@@ -232,23 +243,30 @@
     return lax.broadcasted_iota(jnp.int32, shape, len(shape) - 1)
 
 
+def prepare_kernel(couple_ref, same_ref, table_ref, base_ref):
+    step = pl.program_id(0)
+    for p in range(4):
+        here = pl.ds(step * 4 + p, 1)
+        base_ref[p] = couple_ref[:, p].reshape(LANES, LANES).T + jnp.where(
+            same_ref[here, :] > 0, table_ref[:, 1:2], table_ref[:, 0:1]
+        )
+
+
 def pair_kernel(
     left_a_ref,
     left_b_ref,
     left_mask_ref,
     right_ref,
     final_ref,
-    couple_ref,
+    base_ref,
     cover_ref,
-    same_ref,
-    table_ref,
     gain_ref,
     mapping_ref,
     mid_ref,
     source_ref,
     sent_ref,
     outer_ref,
-    count_ref,
+    scale_ref,
     sides_ref,
 ):
     step = pl.program_id(0)
@@ -268,6 +286,12 @@
             blocks.append(ref[pl.ds(pl.multiple_of(start, HALF), HALF), :])
         return jnp.concatenate(blocks, axis=0)
 
+    left = jnp.concatenate([in_order(left_a_ref), in_order(left_b_ref)], axis=1).T
+    for n in range(8):
+        outer_ref[:, n * 256 : (n + 1) * 256] = jnp.dot(
+            left, right_ref[:, n * 256 : (n + 1) * 256], preferred_element_type=jnp.float32
+        ).astype(jnp.bfloat16)
+
     @pl.when(step == 0)
     def _():
         both = lax.dot_general(
@@ -276,15 +300,10 @@
             (((0,), (0,)), ((), ())),
             preferred_element_type=jnp.float32,
         )
-        both = jnp.maximum(both[:32], 1.0)
-        count_ref[...] = jnp.where(lane_index((16, LANES)) < HALF, both[:16], both[16:])
-
-    left = jnp.concatenate([in_order(left_a_ref), in_order(left_b_ref)], axis=1).T
-    for n in range(8):
-        outer_ref[:, n * 256 : (n + 1) * 256] = jnp.dot(
-            left, right_ref[:, n * 256 : (n + 1) * 256], preferred_element_type=jnp.float32
-        ).astype(jnp.bfloat16)
-
+        both = 1.0 / jnp.maximum(both[:32], 1.0)
+        scale_ref[...] = jnp.where(lane_index((16, LANES)) < HALF, both[:16], both[16:])
+
+    gain = jnp.broadcast_to(gain_ref[...], (LANES, LANES))
     sources = []
     for p in range(rows):
         halves = []
@@ -303,31 +322,27 @@
         a0, a1 = update[:LANES, :LANES], update[LANES:, :LANES]
         b0, b1 = update[:LANES, LANES:], update[LANES:, LANES:]
         update = jnp.where(low, a0, b1) + pltpu.roll(jnp.where(low, b0, a1), HALF, 1)
-        here = pl.ds(step * rows + p, 1)
-        update = update / count_ref[here, :]
-        update = update + jnp.where(same_ref[here, :] > 0, table_ref[:, 1:2], table_ref[:, 0:1])
-        mid = couple_ref[:, p].reshape(LANES, LANES) + update.T
-        mid_ref[:, p] = mid.reshape(2, HALF, LANES)
-        mean = jnp.mean(mid, -1, keepdims=True)
+        mid = base_ref[p] + update * scale_ref[pl.ds(step * rows + p, 1), :]
+        mid_ref[p] = mid
+        mean = jnp.mean(mid, 0, keepdims=True)
         centred = mid - mean
-        var = jnp.mean(centred * centred, -1, keepdims=True)
-        source = (centred * lax.rsqrt(var + 1e-05) * gain_ref[...]).astype(jnp.bfloat16)
-        source_ref[:, p] = source.reshape(2, HALF, LANES)
+        var = jnp.mean(centred * centred, 0, keepdims=True)
+        source = (centred * lax.rsqrt(var + 1e-05) * gain).astype(jnp.bfloat16)
+        source_ref[p] = source
         sources.append(source)
+    sources = jnp.concatenate(sources, axis=1)
     for half in range(2):
-        proj = lax.dot_general(
+        proj = jnp.dot(
             mapping_ref[half * 256 : (half + 1) * 256, :],
-            jnp.concatenate(sources, axis=0),
-            (((1,), (1,)), ((), ())),
+            sources,
             preferred_element_type=jnp.float32,
         )
         for p in range(rows):
             cover = cover_ref[pl.ds(step * rows + p, 1), :]
             gate = proj[:LANES, p * LANES : (p + 1) * LANES]
             value = proj[LANES:, p * LANES : (p + 1) * LANES]
-            sides_ref[pl.ds(pl.multiple_of((half * 16 + step * rows + p) * LANES, LANES), LANES), :] = (
-                cover * jax.nn.sigmoid(gate) * value
-            )
+            start = pl.multiple_of((half * 16 + step * rows + p) * LANES, LANES)
+            sides_ref[pl.ds(start, LANES), :] = cover * jax.nn.sigmoid(gate) * value
 
     @pl.when(step == steps - 1)
     def _():
@@ -373,9 +388,16 @@
         )
 
 
-def finish_kernel(
-    product_ref, mid_ref, source_ref, gate_ref, final_ref, gain_ref, out_ref, normal_ref
-):
+def gate_kernel(source_ref, weight_ref, gate_ref):
+    sources = jnp.concatenate([source_ref[p] for p in range(4)], axis=1)
+    gate = jax.nn.sigmoid(
+        jnp.dot(weight_ref[...], sources, preferred_element_type=jnp.float32)
+    )
+    for p in range(4):
+        gate_ref[p] = gate[:, p * LANES : (p + 1) * LANES]
+
+
+def finish_kernel(product_ref, mid_ref, gate_ref, final_ref, gain_ref, out_ref, normal_ref):
     step = pl.program_id(0)
     rows = 4
 
@@ -395,29 +417,30 @@
                 product_ref[c].astype(jnp.float32) - mean
             ) * scale
 
+    gain = jnp.broadcast_to(gain_ref[...], (LANES, LANES))
+    centred = jnp.concatenate(
+        [
+            (normal_ref[pl.ds(step * rows + p, LANES, stride=16), :] * gain).astype(jnp.bfloat16)
+            for p in range(rows)
+        ],
+        axis=1,
+    )
+    result = jnp.dot(final_ref[...], centred, preferred_element_type=jnp.float32)
     for p in range(rows):
-        centred = (
-            normal_ref[pl.ds(step * rows + p, LANES, stride=16), :] * gain_ref[...]
-        ).astype(jnp.bfloat16)
-        result = lax.dot_general(
-            centred, final_ref[...], (((0,), (0,)), ((), ())), preferred_element_type=jnp.float32
-        )
-        gate = jax.nn.sigmoid(
-            jnp.dot(
-                source_ref[:, p].reshape(LANES, LANES),
-                gate_ref[...],
-                preferred_element_type=jnp.float32,
-            )
-        )
-        out_ref[:, p] = mid_ref[:, p] + (gate * result).reshape(2, HALF, LANES)
+        out = mid_ref[p] + gate_ref[p] * result[:, p * LANES : (p + 1) * LANES]
+        out_ref[:, p] = out.T.reshape(2, HALF, LANES)
 
 
 def whole(shape):
     return pl.BlockSpec(shape, lambda t: (0,) * len(shape), pipeline_mode=pl.Buffered(1))
 
 
-def by_rows(dtype_rows=4):
-    return pl.BlockSpec((2, dtype_rows, HALF, LANES), lambda t: (0, t, 0, 0))
+def by_rows():
+    return pl.BlockSpec((2, 4, HALF, LANES), lambda t: (0, t, 0, 0))
+
+
+def by_pairs():
+    return pl.BlockSpec((4, LANES, LANES), lambda t: (t, 0, 0))
 
 
 PARAMS = pltpu.CompilerParams(
@@ -429,7 +452,20 @@
     return pl.CostEstimate(flops=us * 10**9, bytes_accessed=us * 10**6, transcendentals=0)
 
 
-def pair_call(left, right, final, couple, cover, same, table, gain, mapping):
+def prepare_call(couple, same, table):
+    return pl.pallas_call(
+        prepare_kernel,
+        grid=(4,),
+        in_specs=[by_rows(), whole((16, LANES)), whole((LANES, 2))],
+        out_specs=by_pairs(),
+        out_shape=jax.ShapeDtypeStruct((16, LANES, LANES), jnp.float32),
+        compiler_params=PARAMS,
+        cost_estimate=cost(3),
+        name="prepare",
+    )(couple, same, table)
+
+
+def pair_call(left, right, final, base, cover, gain, mapping):
     return pl.pallas_call(
         pair_kernel,
         grid=(4,),
@@ -439,17 +475,15 @@
             pl.BlockSpec((1024, LANES), lambda t: (0, 8), pipeline_mode=pl.Buffered(1)),
             whole((1024, 2176)),
             whole((256, 512)),
-            by_rows(),
+            by_pairs(),
             whole((16, LANES)),
-            whole((16, LANES)),
-            whole((LANES, 2)),
-            whole((1, LANES)),
+            whole((LANES, 1)),
             whole((512, LANES)),
         ],
-        out_specs=[by_rows(), by_rows(), whole((LANES, 32, LANES))],
+        out_specs=[by_pairs(), by_pairs(), whole((LANES, 32, LANES))],
         out_shape=[
-            jax.ShapeDtypeStruct((2, 16, HALF, LANES), jnp.float32),
-            jax.ShapeDtypeStruct((2, 16, HALF, LANES), jnp.bfloat16),
+            jax.ShapeDtypeStruct((16, LANES, LANES), jnp.float32),
+            jax.ShapeDtypeStruct((16, LANES, LANES), jnp.bfloat16),
             jax.ShapeDtypeStruct((LANES, 32, LANES), jnp.bfloat16),
         ],
         scratch_shapes=[
@@ -460,7 +494,7 @@
         compiler_params=PARAMS,
         cost_estimate=cost(16),
         name="pair",
-    )(left, left, left, right, final, couple, cover, same, table, gain, mapping)
+    )(left, left, left, right, final, base, cover, gain, mapping)
 
 
 def triangle_call(taken):
@@ -473,15 +507,27 @@
     )(taken)
 
 
-def finish_call(product, mid, source, gate, final, gain):
+def gate_call(source, weight):
+    return pl.pallas_call(
+        gate_kernel,
+        grid=(4,),
+        in_specs=[by_pairs(), whole((LANES, LANES))],
+        out_specs=by_pairs(),
+        out_shape=jax.ShapeDtypeStruct((16, LANES, LANES), jnp.float32),
+        compiler_params=PARAMS,
+        cost_estimate=cost(2),
+        name="gate",
+    )(source, weight)
+
+
+def finish_call(product, mid, gate, final, gain):
     return pl.pallas_call(
         finish_kernel,
         grid=(4,),
         in_specs=[
             whole((LANES, 16, LANES)),
-            by_rows(),
-            by_rows(),
-            whole((LANES, LANES)),
+            by_pairs(),
+            by_pairs(),
             whole((LANES, LANES)),
             whole((LANES, 1)),
         ],
@@ -491,7 +537,7 @@
         compiler_params=PARAMS,
         cost_estimate=cost(3),
         name="finish",
-    )(product, mid, source, gate, final, gain)
+    )(product, mid, gate, final, gain)
 
 
 def project_call(msa, cover, focus_gain, dyadic_gain, first, second):
@@ -501,10 +547,10 @@
             jax.ShapeDtypeStruct((2, 64, 1152), jnp.bfloat16),
             jax.ShapeDtypeStruct((64, 2176), jnp.bfloat16),
             jax.ShapeDtypeStruct((1024, 256), jnp.bfloat16),
-            jax.ShapeDtypeStruct((16, 32, 256), jnp.float32),
+            jax.ShapeDtypeStruct((16, 24, 256), jnp.float32),
         ],
         scratch_shapes=[pltpu.VMEM((2048, LANES), jnp.float32)],
-        compiler_params=pltpu.CompilerParams(vmem_limit_bytes=VMEM_LIMIT),
+        compiler_params=pltpu.CompilerParams(vmem_limit_bytes=ALL_VMEM),
         cost_estimate=cost(4),
         name="project",
     )(msa, cover, focus_gain, dyadic_gain, first, second)
@@ -632,15 +678,18 @@
         .transpose(2, 3, 1, 0)
         .reshape(2 * width_z, 16 * width_o)
     )
+    base = prepare_call(
+        couple_tensor.reshape(2, 16, vertical_aminos, width_z),
+        halves_on_lanes(same),
+        strand_couple_table.T,
+    )
     pair_mid, tri_in, sides = pair_call(
         left_rows,
         right_all,
         final,
-        couple_tensor.reshape(2, 16, vertical_aminos, width_z),
+        base,
         halves_on_lanes(couple_cover_grid.astype(jnp.float32)),
-        halves_on_lanes(same),
-        strand_couple_table.T,
-        trio_source_scaling.reshape(1, width_z),
+        trio_source_scaling.reshape(width_z, 1),
         trio_mapping_factors.T,
     )
     taken = lax.all_to_all(sides, ("row", "col"), 0, 0, tiled=True)
@@ -651,9 +700,8 @@
     refreshed_couple_tensor = finish_call(
         product,
         pair_mid,
-        tri_in,
-        trio_sigmoid_factor,
-        trio_final_factor,
+        gate_call(tri_in, trio_sigmoid_factor.T),
+        trio_final_factor.T,
         trio_middle_scaling.reshape(width_t, 1),
     ).reshape(rows_res, vertical_aminos, width_z)
     return (refreshed_supplement_align, refreshed_couple_tensor)

time: 156 us -> 150 us (0.962)
  blocking collectives: 48.4 us -> 44.6 us
  local copies, waits for them, and re-layouts: 13.7 us -> 11.9 us
    all_gather x1, waiting for transfers between devices: 0.02 us -> 10 us  [local(): parts = lax.all_gather(parts, 'row', axis=0, tiled=True)]
    all_to_all x1, waiting for transfers between devices: 10.1 us -> 0.23 us  [local(): lax.all_to_all(product.reshape(n_row * n_col, 16, LANES), ('row', 'col'),...]
    unnamed x56 -> x54, local copies, waits for them, and re-layouts: 11.2 us -> 6.92 us
    all_to_all x1, blocking collectives: 28.7 us -> 26.4 us  [local(): taken = lax.all_to_all(sides, ('row', 'col'), 0, 0, tiled=True)]
    pallas_call x0 -> x2, Pallas kernels: none -> 2.16 us  [the longest x1 1.39 us: prepare_call(): pl.pallas_call(prepare_kernel, grid=(4,), in_specs=[by_rows(), whole((16,...]
    pallas_call x1, Pallas kernels: 15.2 us -> 13.2 us  [pair_call(): pl.pallas_call(pair_kernel, grid=(4,), in_specs=[pl.BlockSpec((1024, LANE...]
  transfers between devices with their start and end apart: 10 -> 10, of which waited for: 4 -> 5; matrix products, arithmetic and copies ran while one was open for 4% -> 7% of each run, Pallas kernels for 14% -> 14%
where the time goes in v3:
time: 150 us; the launch traced here: 149 us
  blocking collectives  44.6 us (30%)
  Pallas kernels  29.3 us (20%)
  starting transfers between devices  25.9 us (17%)
  waiting for transfers between devices  22.8 us (15%)
  between operations  14.4 us (10%)
  local copies, waits for them, and re-layouts  11.9 us (8%)
    all_to_all x1, blocking collectives, local(): taken = lax.all_to_all(sides, ('row', 'col'), 0, 0, tiled=True)  26.4 us
    all_to_all x1, blocking collectives, local(): sums = lax.all_to_all(sums, 'row', 0, 0, tiled=True)  18.2 us
    pallas_call x1, Pallas kernels, pair_call(): pl.pallas_call(pair_kernel, grid=(4,), in_specs=[pl.BlockSpec((1024, LANE...  13.2 us
    ppermute x1, starting transfers between devices, ring_of_four(): back = lax.ppermute(block, axis, step(1))  11 us
    all_gather x1, waiting for transfers between devices, local(): parts = lax.all_gather(parts, 'row', axis=0, tiled=True)  10 us
    unnamed x54, local copies, waits for them, and re-layouts  6.92 us
    ppermute x2, waiting for transfers between devices, spread_left(): lax.ppermute(left[flip], ('row', 'col'), route(flip))  6.07 us
    ppermute x1, starting transfers between devices, ring_of_four(): ahead = lax.ppermute(block, axis, step(-1))  5.51 us
  transfers between devices with their start and end apart: 10, of which 5 were waited for; matrix products, arithmetic and copies ran while one was open for 7% of the time, Pallas kernels for 14%

profile of v3, /device:TPU:0, one launch (start us, length us, event | category | flops | bytes accessed | tf_op | source)
XLA Modules:
  0.0 149.1 jit_solution(13692493770744260586)
XLA Ops:
  7.2 4.9 %project.1 = (bf16[2,64,1152]{2,1,0:T(8,128)(2,1)}, bf16[64,2176]{1,0:T(8,128)(2,1)}, bf16[1024,256]{1,0:T(8,128)(2,1)}, f32[16,24,256]{2,1,0:T(8,128)}) custom-call(bf16[64,4096]{1,0:T(8,128)(2,1)} %msa_ref.3, s32[64,64]{1,0:T(8,128)} %cover_ref.3, f32[1,64]{1,0:T(1,128)} %bitcast.44, f32[1,64]{1,0:T(1,128)} %bitcast.45, bf16[32,64]{1,0:T(8,128)(2,1)} %bitcast.42, ...), custom_call_target="tpu_custom_call" | custom-call | flops 4000000000 | bytes 4000000 | tf_op jit(solution)/shard_map/project/pallas_call | solution.py:544
  12.2 18.2 %all_to_all.15.sums_ref = f32[16,24,256]{2,1,0:T(8,128)S(1)} all-to-all(f32[16,24,256]{2,1,0:T(8,128)} %get-tuple-element.14), channel_id=1, replica_groups=mesh['row'=16,'col'=8] {'row'}, dimensions={0} | all-to-all | bytes 786432 | tf_op jit(solution)/shard_map/all_to_all | solution.py:654
  30.4 1.0 slice_bitcast_fusion
  31.4 0.7 collective-permute-start
  32.1 0.6 collective-permute-start.1
  32.8 0.8 constant_dynamic-update-slice_fusion.7
  33.5 6.1 %collective-permute-done.1 = bf16[64,1152]{1,0:T(8,128)(2,1)S(1)} collective-permute-done((bf16[64,1152]{1,0:T(8,128)(2,1)S(1)}, bf16[64,1152]{1,0:T(8,128)(2,1)S(1)}, u32[]{:S(2)}, u32[]{:S(2)}) %collective-permute-start.1) | collective-permute-done | bytes 147488 | tf_op jit(solution)/shard_map/ppermute | solution.py:604
  39.6 0.7 constant_dynamic-update-slice_fusion.6
  40.3 11.0 %collective-permute-start.2 = (bf16[128,1152]{1,0:T(8,128)(2,1)S(1)}, bf16[128,1152]{1,0:T(8,128)(2,1)S(1)}, u32[]{:S(2)}, u32[]{:S(2)}) collective-permute-start(bf16[128,1152]{1,0:T(8,128)(2,1)S(1)} %get-tuple-element.36), channel_id=1, source_target_pairs={{0,2},{1,3},{2,4},{3,5},{4,6},{5,7},{6,0},{7,1},{8,10},{9,11},{10,... | collective-permute-start | bytes 884744 | tf_op jit(solution)/shard_map/ppermute | solution.py:581
  51.4 5.5 %collective-permute-start.3 = (bf16[128,1152]{1,0:T(8,128)(2,1)S(1)}, bf16[128,1152]{1,0:T(8,128)(2,1)S(1)}, u32[]{:S(2)}, u32[]{:S(2)}) collective-permute-start(bf16[128,1152]{1,0:T(8,128)(2,1)S(1)} %get-tuple-element.36), channel_id=1, source_target_pairs={{0,6},{1,7},{2,0},{3,1},{4,2},{5,3},{6,4},{7,5},{8,14},{9,15},{10,... | collective-permute-start | bytes 884744 | tf_op jit(solution)/shard_map/ppermute | solution.py:582
  56.9 0.2 copy.30
  57.9 5.2 %collective-permute-done.2 = bf16[128,1152]{1,0:T(8,128)(2,1)S(1)} collective-permute-done((bf16[128,1152]{1,0:T(8,128)(2,1)S(1)}, bf16[128,1152]{1,0:T(8,128)(2,1)S(1)}, u32[]{:S(2)}, u32[]{:S(2)}) %collective-permute-start.2) | collective-permute-done | bytes 294944 | tf_op jit(solution)/shard_map/ppermute | solution.py:581
  63.3 3.3 %collective-permute-start.5 = (bf16[64,1152]{1,0:T(8,128)(2,1)S(1)}, bf16[64,1152]{1,0:T(8,128)(2,1)S(1)}, u32[]{:S(2)}, u32[]{:S(2)}) collective-permute-start(bf16[64,1152]{1,0:T(8,128)(2,1)S(1)} %slice.33), channel_id=1, source_target_pairs={{0,6},{1,7},{2,0},{3,1},{4,2},{5,3},{6,4},{7,5},{8,14},{9,15},{10,... | collective-permute-start | bytes 442376 | tf_op jit(solution)/shard_map/ppermute | solution.py:585
  66.6 0.9 constant_dynamic-update-slice_fusion.5
  67.5 0.9 constant_dynamic-update-slice_fusion.4
  68.4 1.2 collective-permute-done.4
  69.6 0.7 constant_dynamic-update-slice_fusion.3
  70.3 0.7 constant_dynamic-update-slice_fusion.2
  71.3 1.4 prepare.1.base_ref
  72.7 1.0 copy-done.12
  73.7 2.6 %attend.1 = f32[40,512]{1,0:T(8,128)} custom-call(bf16[1024,256]{1,0:T(8,128)(2,1)S(1)} %copy-done.9, s32[64,64]{1,0:T(8,128)S(1)} %copy-done.3, f32[16,24,256]{2,1,0:T(8,128)S(1)} %all_to_all.15.sums_ref, bf16[64,64]{1,0:T(8,128)(2,1)S(1)} %copy-done.4, bf16[8,64]{1,0:T(8,128)(2,1)S(1)} %bitcast.35, bf16[8,64]{1,0:T(8,128)(2,1)S(1)} %bitcast.36), custom_call_target="tpu_custom_call" | custom-call | flops 3000000000 | bytes 3000000 | tf_op jit(solution)/shard_map/attend/pallas_call | solution.py:560
  76.2 2.4 %constant_dynamic-update-slice_fusion.8.left_a_ref.left_b_ref.left_mask_ref = bf16[1024,1152]{1,0:T(8,128)(2,1)} fusion(bf16[1024,1152]{1,0:T(8,128)(2,1)} %get-tuple-element.31, bf16[512,1152]{1,0:T(8,128)(2,1)} %collective-permute-done.6), kind=kLoop, calls=%fused_computation.11 | loop fusion | bytes 2359296 | tf_op jit(solution)/shard_map/concatenate | solution.py:608
  78.7 13.2 %pair.1 = (f32[16,128,128]{2,1,0:T(8,128)S(1)}, bf16[16,128,128]{2,1,0:T(8,128)(2,1)S(1)}, bf16[128,32,128]{2,1,0:T(8,128)(2,1)S(1)}) custom-call(bf16[1024,1152]{1,0:T(8,128)(2,1)} %constant_dynamic-update-slice_fusion.8.left_a_ref.left_b_ref.left_mask_ref, bf16[1024,1152]{1,0:T(8,128)(2,1)} %constant_dynamic-update-slice_fusion.8.left_a_ref.left_b_ref.left_mask_ref, ...), custom_call_target="tpu_custom_call" | custom-call | flops 16000000000 | bytes 16000000 | tf_op jit(solution)/shard_map/pair/pallas_call | solution.py:469
  91.9 26.4 %all_to_all.16 = bf16[128,32,128]{2,1,0:T(8,128)(2,1)S(1)} all-to-all(bf16[128,32,128]{2,1,0:T(8,128)(2,1)S(1)} %get-tuple-element.21), channel_id=1, replica_groups=mesh['row'=16,'col'=8] {'row','col'}, dimensions={0} | all-to-all | bytes 2097152 | tf_op jit(solution)/shard_map/all_to_all | solution.py:695
  118.4 1.6 %triangle.1 = bf16[16,8,16,128]{3,2,1,0:T(8,128)(2,1)} custom-call(bf16[16,8,32,128]{3,2,1,0:T(8,128)(2,1)S(1)} %bitcast.29), custom_call_target="tpu_custom_call" | custom-call | flops 2000000000 | bytes 2000000 | tf_op jit(solution)/shard_map/triangle/pallas_call | solution.py:501
  120.0 4.6 %all-to-all-start.2 = ((bf16[128,16,128]{2,1,0:T(8,128)(2,1)}), bf16[128,16,128]{2,1,0:T(8,128)(2,1)S(1)}, u32[]{:S(2)}, u32[]{:S(2)}) async-start(bf16[128,16,128]{2,1,0:T(8,128)(2,1)} %bitcast.15), calls=%async_computation.2 | async-start | bytes 1048576 | tf_op jit(solution)/shard_map/all_to_all | solution.py:697
  125.0 10.0 %all-gather.3.cloned.1.call-done.part_ref = f32[640,512]{1,0:T(8,128)} async-done(((f32[40,512]{1,0:T(8,128)}), f32[640,512]{1,0:T(8,128)}) %all-gather.3.cloned.1.call-update) | async-done | bytes 1310736 | tf_op jit(solution)/shard_map/all_gather | solution.py:665
  135.0 1.3 copy-done
  136.3 2.0 %refresh.1 = bf16[64,4096]{1,0:T(8,128)(2,1)} custom-call(f32[640,512]{1,0:T(8,128)S(1)} %copy-done, bf16[1024,256]{1,0:T(8,128)(2,1)S(1)} %copy-done.9, bf16[64,4096]{1,0:T(8,128)(2,1)S(1)} %copy-done.2, bf16[64,64]{1,0:T(8,128)(2,1)S(1)} %copy-done.5, bf16[64,64]{1,0:T(8,128)(2,1)S(1)} %copy-done.6), custom_call_target="tpu_custom_call" | custom-call | flops 2000000000 | bytes 2000000 | tf_op jit(solution)/shard_map/refresh/pallas_call | solution.py:570
  138.3 0.8 gate.1.gate_ref
  139.1 0.2 all-to-all-done.2.product_ref
  139.3 2.9 %finish.1 = f32[2,16,64,128]{3,2,1,0:T(8,128)} custom-call(bf16[128,16,128]{2,1,0:T(8,128)(2,1)S(1)} %all-to-all-done.2.product_ref, f32[16,128,128]{2,1,0:T(8,128)S(1)} %get-tuple-element.22.mid_ref, f32[16,128,128]{2,1,0:T(8,128)S(1)} %gate.1.gate_ref, bf16[128,128]{1,0:T(8,128)(2,1)S(1)} %bitcast.32, f32[128,1]{1,0:T(8,128)S(1)} %copy.37.gain_ref), custom_call_target="tpu_custom_call" | custom-call | flops 3000000000 | bytes 3000000 | tf_op jit(solution)/shard_map/finish/pallas_call | solution.py:524
  (71 shorter events, 1.6 us)
Async XLA Ops:
  7.2 71.5 %all-gather.5.cloned.1.call-start = ((), (), s32[]{:S(2)}) async-start(), calls=%async_computation.4 | async-start | bytes 4734976 | tf_op jit(solution)/shard_map/all_gather | solution.py:653
  12.1 44.8 %copy-start.13 = (bf16[1024,128]{1,0:T(8,128)(2,1)S(1)}, bf16[1024,128]{1,0:T(8,128)(2,1)}, u32[]{:S(2)}) copy-start(bf16[1024,128]{1,0:T(8,128)(2,1)} %param.35) | copy-start | bytes 786436
  12.1 45.2 %copy-start.21 = (s32[512]{0:T(512)S(1)}, s32[512]{0:T(512)}, u32[]{:S(2)}) copy-start(s32[512]{0:T(512)} %param.25) | copy-start | bytes 6148
  12.1 45.4 %copy-start.18 = (f32[2,128]{1,0:T(2,128)S(1)}, f32[2,128]{1,0:T(2,128)}, u32[]{:S(2)}) copy-start(f32[2,128]{1,0:T(2,128)} %param.36) | copy-start | bytes 3076
  12.1 45.5 %copy-start.17 = (s32[32,64]{1,0:T(8,128)S(1)}, s32[32,64]{1,0:T(8,128)}, u32[]{:S(2)}) copy-start(s32[32,64]{1,0:T(8,128)} %param.24) | copy-start | bytes 24580
  12.1 45.5 %copy-start.19 = (f32[128]{0:T(128)S(1)}, f32[128]{0:T(128)}, u32[]{:S(2)}) copy-start(f32[128]{0:T(128)} %param.37) | copy-start | bytes 1540
  12.1 45.6 %copy-start.14 = (bf16[128,512]{1,0:T(8,128)(2,1)S(1)}, bf16[128,512]{1,0:T(8,128)(2,1)}, u32[]{:S(2)}) copy-start(bf16[128,512]{1,0:T(8,128)(2,1)} %param.38) | copy-start | bytes 393220
  12.2 122.8 %all-gather.3.cloned.1.call-start = ((), (), s32[]{:S(2)}) async-start(), calls=%async_computation.3 | async-start | bytes 1392640 | tf_op jit(solution)/shard_map/all_gather | solution.py:665
  31.4 1.3 collective-permute-start
  32.1 7.5 %collective-permute-start.1 = (bf16[64,1152]{1,0:T(8,128)(2,1)S(1)}, bf16[64,1152]{1,0:T(8,128)(2,1)S(1)}, u32[]{:S(2)}, u32[]{:S(2)}) collective-permute-start(bf16[64,1152]{1,0:T(8,128)(2,1)S(1)} %get-tuple-element.28), channel_id=1, source_target_pairs={{0,8},{1,24},{2,40},{3,56},{4,72},{5,88},{6,104},{7,120},{8,0},{9,... | collective-permute-start | bytes 442376 | tf_op jit(solution)/shard_map/ppermute | solution.py:604
  40.3 22.8 %collective-permute-start.2 = (bf16[128,1152]{1,0:T(8,128)(2,1)S(1)}, bf16[128,1152]{1,0:T(8,128)(2,1)S(1)}, u32[]{:S(2)}, u32[]{:S(2)}) collective-permute-start(bf16[128,1152]{1,0:T(8,128)(2,1)S(1)} %get-tuple-element.36), channel_id=1, source_target_pairs={{0,2},{1,3},{2,4},{3,5},{4,6},{5,7},{6,0},{7,1},{8,10},{9,11},{10,... | collective-permute-start | bytes 884744 | tf_op jit(solution)/shard_map/ppermute | solution.py:581
  51.4 11.9 %collective-permute-start.3 = (bf16[128,1152]{1,0:T(8,128)(2,1)S(1)}, bf16[128,1152]{1,0:T(8,128)(2,1)S(1)}, u32[]{:S(2)}, u32[]{:S(2)}) collective-permute-start(bf16[128,1152]{1,0:T(8,128)(2,1)S(1)} %get-tuple-element.36), channel_id=1, source_target_pairs={{0,6},{1,7},{2,0},{3,1},{4,2},{5,3},{6,4},{7,5},{8,14},{9,15},{10,... | collective-permute-start | bytes 884744 | tf_op jit(solution)/shard_map/ppermute | solution.py:582
  57.1 14.1 %copy-start.1 = (f32[32,64,128]{2,1,0:T(8,128)S(1)}, f32[32,64,128]{2,1,0:T(8,128)}, u32[]{:S(2)}) copy-start(f32[32,64,128]{2,1,0:T(8,128)} %param.23) | copy-start | bytes 3145732
  63.2 6.4 %collective-permute-start.4 = (bf16[64,1152]{1,0:T(8,128)(2,1)S(1)}, bf16[64,1152]{1,0:T(8,128)(2,1)S(1)}, u32[]{:S(2)}, u32[]{:S(2)}) collective-permute-start(bf16[64,1152]{1,0:T(8,128)(2,1)S(1)} %slice.32), channel_id=1, source_target_pairs={{0,2},{1,3},{2,4},{3,5},{4,6},{5,7},{6,0},{7,1},{8,10},{9,11},{10,... | collective-permute-start | bytes 442376 | tf_op jit(solution)/shard_map/ppermute | solution.py:584
  63.3 7.0 %collective-permute-start.5 = (bf16[64,1152]{1,0:T(8,128)(2,1)S(1)}, bf16[64,1152]{1,0:T(8,128)(2,1)S(1)}, u32[]{:S(2)}, u32[]{:S(2)}) collective-permute-start(bf16[64,1152]{1,0:T(8,128)(2,1)S(1)} %slice.33), channel_id=1, source_target_pairs={{0,6},{1,7},{2,0},{3,1},{4,2},{5,3},{6,4},{7,5},{8,14},{9,15},{10,... | collective-permute-start | bytes 442376 | tf_op jit(solution)/shard_map/ppermute | solution.py:585
  71.1 5.2 %collective-permute-start.6 = (bf16[512,1152]{1,0:T(8,128)(2,1)}, bf16[512,1152]{1,0:T(8,128)(2,1)}, u32[]{:S(2)}, u32[]{:S(2)}) collective-permute-start(bf16[512,1152]{1,0:T(8,128)(2,1)} %get-tuple-element.30), channel_id=1, source_target_pairs={{0,1},{1,0},{2,3},{3,2},{4,5},{5,4},{6,7},{7,6},{8,9},{9,8},{10,11... | collective-permute-start | bytes 3538952 | tf_op jit(solution)/shard_map/ppermute | solution.py:607
  71.2 2.4 %copy-start.3 = (s32[64,64]{1,0:T(8,128)S(1)}, s32[64,64]{1,0:T(8,128)}, u32[]{:S(2)}) copy-start(s32[64,64]{1,0:T(8,128)} %cover_ref.3) | copy-start | bytes 49156
  71.2 2.4 %copy-start.4 = (bf16[64,64]{1,0:T(8,128)(2,1)S(1)}, bf16[64,64]{1,0:T(8,128)(2,1)}, u32[]{:S(2)}) copy-start(bf16[64,64]{1,0:T(8,128)(2,1)} %asking_ref.1) | copy-start | bytes 24580
  71.2 2.4 %copy-start.7 = (bf16[64,8]{0,1:T(8,128)(2,1)S(1)}, bf16[64,8]{0,1:T(8,128)(2,1)}, u32[]{:S(2)}) copy-start(bf16[64,8]{0,1:T(8,128)(2,1)} %param.28) | copy-start | bytes 3076
  71.2 2.4 %copy-start.8 = (bf16[64,8]{0,1:T(8,128)(2,1)S(1)}, bf16[64,8]{0,1:T(8,128)(2,1)}, u32[]{:S(2)}) copy-start(bf16[64,8]{0,1:T(8,128)(2,1)} %param.29) | copy-start | bytes 3076
  71.3 2.4 %copy-start.9 = (bf16[1024,256]{1,0:T(8,128)(2,1)S(1)}, bf16[1024,256]{1,0:T(8,128)(2,1)}, u32[]{:S(2)}) copy-start(bf16[1024,256]{1,0:T(8,128)(2,1)} %get-tuple-element.16.source_ref) | copy-start | bytes 1572868
  72.7 1.0 copy-start.12
  91.9 26.4 %copy-start.10 = (bf16[16,128,128]{2,1,0:T(8,128)(2,1)}, bf16[16,128,128]{2,1,0:T(8,128)(2,1)S(1)}, u32[]{:S(2)}) copy-start(bf16[16,128,128]{2,1,0:T(8,128)(2,1)S(1)} %get-tuple-element.23.source_ref) | copy-start | bytes 1572868
  118.3 6.3 %copy-start.15 = (bf16[128,128]{1,0:T(8,128)(2,1)S(1)}, bf16[128,128]{1,0:T(8,128)(2,1)}, u32[]{:S(2)}) copy-start(bf16[128,128]{1,0:T(8,128)(2,1)} %param.39) | copy-start | bytes 98308
  118.3 6.4 %copy-start.16 = (bf16[128,128]{1,0:T(8,128)(2,1)S(1)}, bf16[128,128]{1,0:T(8,128)(2,1)}, u32[]{:S(2)}) copy-start(bf16[128,128]{1,0:T(8,128)(2,1)} %param.41) | copy-start | bytes 98308
  118.3 6.5 %copy-start.20 = (f32[128]{0:T(128)S(1)}, f32[128]{0:T(128)}, u32[]{:S(2)}) copy-start(f32[128]{0:T(128)} %param.40) | copy-start | bytes 1540
  118.3 16.7 %copy-start.2 = (bf16[64,4096]{1,0:T(8,128)(2,1)S(1)}, bf16[64,4096]{1,0:T(8,128)(2,1)}, u32[]{:S(2)}) copy-start(bf16[64,4096]{1,0:T(8,128)(2,1)} %msa_ref.3) | copy-start | bytes 1572868
  118.3 16.7 %copy-start.5 = (bf16[64,64]{1,0:T(8,128)(2,1)S(1)}, bf16[64,64]{1,0:T(8,128)(2,1)}, u32[]{:S(2)}) copy-start(bf16[64,64]{1,0:T(8,128)(2,1)} %sigmoid_ref.1) | copy-start | bytes 24580
  118.3 16.6 %copy-start.6 = (bf16[64,64]{1,0:T(8,128)(2,1)S(1)}, bf16[64,64]{1,0:T(8,128)(2,1)}, u32[]{:S(2)}) copy-start(bf16[64,64]{1,0:T(8,128)(2,1)} %final_ref.1) | copy-start | bytes 24580
  120.0 19.3 %all-to-all-start.2 = ((bf16[128,16,128]{2,1,0:T(8,128)(2,1)}), bf16[128,16,128]{2,1,0:T(8,128)(2,1)S(1)}, u32[]{:S(2)}, u32[]{:S(2)}) async-start(bf16[128,16,128]{2,1,0:T(8,128)(2,1)} %bitcast.15), calls=%async_computation.2 | async-start | bytes 1048576 | tf_op jit(solution)/shard_map/all_to_all | solution.py:697
  135.0 1.3 copy-start
  136.3 2.0 %copy-start.11 = (bf16[16,128,128]{2,1,0:T(8,128)(2,1)S(1)}, bf16[16,128,128]{2,1,0:T(8,128)(2,1)}, u32[]{:S(2)}) copy-start(bf16[16,128,128]{2,1,0:T(8,128)(2,1)} %copy-done.10) | copy-start | bytes 1572868
Sparse Core Ops, SparseCore 0:
  12.3 65.6 all-gather.4
  80.7 54.2 all-gather.2

commit v4 on v3

--- a/solution.py
+++ b/solution.py
@@ -108,11 +108,12 @@
             wide = focus_cover[:, e * 256 : (e + 1) * 256]
             total = jnp.sum(wide * focus[rows].astype(jnp.float32), 0, keepdims=True)
             for k in range(16):
-                sums_ref[k, g : g + 1, :] = total
+                sums_ref[k, g : g + 1, :] = total[:, :LANES]
+                sums_ref[k, 16 + g : 17 + g, :] = total[:, LANES:]
     count = jnp.sum(cover, 0, keepdims=True)
     for k in range(16):
-        sums_ref[k, 16:, :] = jnp.zeros((8, 256), jnp.float32)
-        sums_ref[k, 16:17, :HALF] = count
+        sums_ref[k, 32:, :] = jnp.zeros((8, LANES), jnp.float32)
+        sums_ref[k, 32:33, :HALF] = count
     shape = (64, LANES)
     for h in range(2):
         pick = ones_where(
@@ -134,7 +135,7 @@
     sums = sums_ref[0]
     for k in range(1, 16):
         sums = sums + sums_ref[k]
-    count = jnp.broadcast_to(sums[16:17, :HALF], (16, HALF))
+    count = jnp.broadcast_to(sums[32:33, :HALF], (16, HALF))
     shape = (16, HALF)
     count = jnp.where(lane_index(shape) // 4 == row_index(shape), count, 0.0)
     shape = (HALF, 256)
@@ -142,7 +143,8 @@
     count = sum(
         jnp.dot(part, pick, preferred_element_type=jnp.float32) for part in parts_of(count, 2)
     )
-    query_mean = (sums[:16] / jnp.maximum(count, 1.0)).astype(jnp.bfloat16)
+    sums = jnp.concatenate([sums[:16], sums[16:32]], axis=1)
+    query_mean = (sums / jnp.maximum(count, 1.0)).astype(jnp.bfloat16)
     query = (
         jnp.dot(query_mean, block_diagonal(asking_ref[...], 4), preferred_element_type=jnp.float32)
         * 8 ** (-0.5)
@@ -253,9 +255,12 @@
 
 
 def pair_kernel(
-    left_a_ref,
-    left_b_ref,
-    left_mask_ref,
+    own_a_ref,
+    own_b_ref,
+    own_mask_ref,
+    other_a_ref,
+    other_b_ref,
+    other_mask_ref,
     right_ref,
     final_ref,
     base_ref,
@@ -275,18 +280,24 @@
     low = lane_index((LANES, LANES)) < HALF
     odd = lax.axis_index("row") % 2
     col = lax.axis_index("col")
-
-    def in_order(ref):
+    z = lax.axis_index("row") // 4
+
+    def in_order(own_ref, other_ref):
         blocks = []
         for block in range(16):
-            turn = (block // 4 - col // 2 + 4) % 4
+            turned = z ^ (block // 4)
+            holder = z ^ jnp.where(
+                turned == 1, 2, jnp.where(turned == 2, 3, jnp.where(turned == 3, 1, 0))
+            )
+            turn = (holder - col // 2 + 4) % 4
             place = jnp.where(turn == 2, 3, jnp.where(turn == 3, 1, jnp.where(turn == 1, 2, 0)))
-            other = (block // 2 + col) % 2
-            start = other * 512 + place * 128 + (block + odd) % 2 * 64
-            blocks.append(ref[pl.ds(pl.multiple_of(start, HALF), HALF), :])
+            start = pl.multiple_of(place * 128 + (block + odd) % 2 * 64, HALF)
+            own = (block // 2 + col) % 2 == 0
+            here = pl.ds(start, HALF)
+            blocks.append(jnp.where(own, own_ref[here, :], other_ref[here, :]))
         return jnp.concatenate(blocks, axis=0)
 
-    left = jnp.concatenate([in_order(left_a_ref), in_order(left_b_ref)], axis=1).T
+    left = jnp.concatenate([in_order(own_a_ref, other_a_ref), in_order(own_b_ref, other_b_ref)], axis=1).T
     for n in range(8):
         outer_ref[:, n * 256 : (n + 1) * 256] = jnp.dot(
             left, right_ref[:, n * 256 : (n + 1) * 256], preferred_element_type=jnp.float32
@@ -295,7 +306,7 @@
     @pl.when(step == 0)
     def _():
         both = lax.dot_general(
-            in_order(left_mask_ref),
+            in_order(own_mask_ref, other_mask_ref),
             right_ref[:, 2048:2176],
             (((0,), (0,)), ((), ())),
             preferred_element_type=jnp.float32,
@@ -465,14 +476,21 @@
     )(couple, same, table)
 
 
-def pair_call(left, right, final, base, cover, gain, mapping):
+def by_left():
+    return [
+        pl.BlockSpec((512, LANES), lambda t: (0, t)),
+        pl.BlockSpec((512, LANES), lambda t: (0, t + 4)),
+        pl.BlockSpec((512, LANES), lambda t: (0, 8), pipeline_mode=pl.Buffered(1)),
+    ]
+
+
+def pair_call(own, other, right, final, base, cover, gain, mapping):
     return pl.pallas_call(
         pair_kernel,
         grid=(4,),
         in_specs=[
-            pl.BlockSpec((1024, LANES), lambda t: (0, t)),
-            pl.BlockSpec((1024, LANES), lambda t: (0, t + 4)),
-            pl.BlockSpec((1024, LANES), lambda t: (0, 8), pipeline_mode=pl.Buffered(1)),
+            *by_left(),
+            *by_left(),
             whole((1024, 2176)),
             whole((256, 512)),
             by_pairs(),
@@ -494,7 +512,7 @@
         compiler_params=PARAMS,
         cost_estimate=cost(16),
         name="pair",
-    )(left, left, left, right, final, base, cover, gain, mapping)
+    )(own, own, own, other, other, other, right, final, base, cover, gain, mapping)
 
 
 def triangle_call(taken):
@@ -547,7 +565,7 @@
             jax.ShapeDtypeStruct((2, 64, 1152), jnp.bfloat16),
             jax.ShapeDtypeStruct((64, 2176), jnp.bfloat16),
             jax.ShapeDtypeStruct((1024, 256), jnp.bfloat16),
-            jax.ShapeDtypeStruct((16, 24, 256), jnp.float32),
+            jax.ShapeDtypeStruct((16, 40, LANES), jnp.float32),
         ],
         scratch_shapes=[pltpu.VMEM((2048, LANES), jnp.float32)],
         compiler_params=pltpu.CompilerParams(vmem_limit_bytes=ALL_VMEM),
@@ -587,25 +605,36 @@
     return jnp.concatenate([block, back, ahead] + opposite, axis=0)
 
 
-def spread_left(left):
+def relay(origin, target):
+    turned = origin ^ target
+    return target ^ (0, 2, 3, 1)[turned]
+
+
+def route_left(left):
     n_row, n_col = lax.axis_size("row"), lax.axis_size("col")
 
     def route(flip):
         return [
-            (r * n_col + c, (2 * c + (r + flip) % 2) * n_col + r // 2)
+            (
+                r * n_col + c,
+                (2 * c + (r + flip) % 2) * n_col + 2 * relay(r // 4, c // 2) + r % 4 // 2,
+            )
             for r in range(n_row)
             for c in range(n_col)
         ]
 
+    return tuple(lax.ppermute(left[flip], ("row", "col"), route(flip)) for flip in range(2))
+
+
+def spread_left(halves):
+    n_col = lax.axis_size("col")
+
     def along(step):
         return [(c, (c + 2 * step) % n_col) for c in range(n_col)]
 
-    both = jnp.concatenate(
-        [lax.ppermute(left[flip], ("row", "col"), route(flip)) for flip in range(2)], axis=0
-    )
-    gathered = ring_of_four(both, "col", along)
+    gathered = ring_of_four(jnp.concatenate(halves, axis=0), "col", along)
     swapped = lax.ppermute(gathered, "col", [(c, c ^ 1) for c in range(n_col)])
-    return jnp.concatenate([gathered, swapped], axis=0)
+    return gathered, swapped
 
 
 def halves_on_lanes(grid):
@@ -651,6 +680,7 @@
         dyadic_second_factor.T,
     )
     right_all = lax.all_gather(right, "row", axis=0, tiled=True)
+    left, sums = lax.optimization_barrier((route_left(left), sums))
     sums = lax.all_to_all(sums, "row", 0, 0, tiled=True)
     left, sums = lax.optimization_barrier((left, sums))
     parts = attend_call(
@@ -661,7 +691,8 @@
         focus_lookup_factor.T,
         focus_content_factor.T,
     )
-    left_rows, parts = lax.optimization_barrier((spread_left(left), parts))
+    left, parts = lax.optimization_barrier((left, parts))
+    left_rows = spread_left(left)
     parts = lax.all_gather(parts, "row", axis=0, tiled=True)
     refreshed_supplement_align = refresh_call(
         parts, source, alignment_tensor, focus_sigmoid_factor, focus_final_factor
@@ -684,7 +715,7 @@
         strand_couple_table.T,
     )
     pair_mid, tri_in, sides = pair_call(
-        left_rows,
+        *left_rows,
         right_all,
         final,
         base,

time: 150 us -> 142 us (0.947)
  starting transfers between devices: 25.9 us -> 14.8 us
  blocking collectives: 44.6 us -> 52.6 us
  local copies, waits for them, and re-layouts: 11.9 us -> 4.89 us
  waiting for transfers between devices: 22.8 us -> 24.3 us
    ppermute x1, starting transfers between devices: 11 us -> 0.86 us  [ring_of_four(): back = lax.ppermute(block, axis, step(1))]
    all_to_all x1, blocking collectives: 18.2 us -> 25.9 us  [local(): sums = lax.all_to_all(sums, 'row', 0, 0, tiled=True)]
    unnamed x54 -> x51, local copies, waits for them, and re-layouts: 6.92 us -> 2.96 us
    ppermute x2, waiting for transfers between devices: 6.07 us -> 3.57 us  [route_left(): lax.ppermute(left[flip], ('row', 'col'), route(flip))]
    concatenate x1, local copies, waits for them, and re-layouts: 2.41 us -> 0.03 us  [spread_left(): gathered = ring_of_four(jnp.concatenate(halves, axis=0), 'col', along)]
    ppermute x1, waiting for transfers between devices: 1.21 us -> 3.56 us  [ring_of_four(): lax.ppermute(back[:half], axis, step(1))]
    ppermute x1, starting transfers between devices: 5.51 us -> 3.34 us  [ring_of_four(): ahead = lax.ppermute(block, axis, step(-1))]
  transfers between devices with their start and end apart: 10 -> 10, of which waited for: 5 -> 6; matrix products, arithmetic and copies ran while one was open for 7% -> 2% of each run, Pallas kernels for 14% -> 15%
where the time goes in v4:
time: 142 us; the launch traced here: 141 us
  blocking collectives  52.6 us (37%)
  Pallas kernels  29.5 us (21%)
  waiting for transfers between devices  24.3 us (17%)
  starting transfers between devices  14.8 us (10%)
  between operations  14.4 us (10%)
  local copies, waits for them, and re-layouts  4.89 us (3%)
    all_to_all x1, blocking collectives, local(): taken = lax.all_to_all(sides, ('row', 'col'), 0, 0, tiled=True)  26.7 us
    all_to_all x1, blocking collectives, local(): sums = lax.all_to_all(sums, 'row', 0, 0, tiled=True)  25.9 us
    pallas_call x1, Pallas kernels, pair_call(): pl.pallas_call(pair_kernel, grid=(4,), in_specs=[*by_left(), *by_left(),...  13.4 us
    all_gather x1, waiting for transfers between devices, local(): parts = lax.all_gather(parts, 'row', axis=0, tiled=True)  8.75 us
    ppermute x1, waiting for transfers between devices, ring_of_four(): back = lax.ppermute(block, axis, step(1))  6.56 us
    pallas_call x1, Pallas kernels, project_call(): pl.pallas_call(project_kernel, out_shape=[jax.ShapeDtypeStruct((2, 64, 11...  4.87 us
    all_to_all x1, starting transfers between devices, local(): lax.all_to_all(product.reshape(n_row * n_col, 16, LANES), ('row', 'col'),...  4.77 us
    ppermute x2, waiting for transfers between devices, route_left(): lax.ppermute(left[flip], ('row', 'col'), route(flip))  3.57 us
  transfers between devices with their start and end apart: 10, of which 6 were waited for; matrix products, arithmetic and copies ran while one was open for 2% of the time, Pallas kernels for 15%

profile of v4, /device:TPU:0, one launch (start us, length us, event | category | flops | bytes accessed | tf_op | source)
XLA Modules:
  0.0 140.6 jit_solution(5487910955293237347)
XLA Ops:
  7.2 4.9 %project.1 = (bf16[2,64,1152]{2,1,0:T(8,128)(2,1)}, bf16[64,2176]{1,0:T(8,128)(2,1)}, bf16[1024,256]{1,0:T(8,128)(2,1)}, f32[16,40,128]{2,1,0:T(8,128)}) custom-call(bf16[64,4096]{1,0:T(8,128)(2,1)} %msa_ref.3, s32[64,64]{1,0:T(8,128)} %cover_ref.3, f32[1,64]{1,0:T(1,128)} %bitcast.44, f32[1,64]{1,0:T(1,128)} %bitcast.45, bf16[32,64]{1,0:T(8,128)(2,1)} %bitcast.42, ...), custom_call_target="tpu_custom_call" | custom-call | flops 4000000000 | bytes 4000000 | tf_op jit(solution)/shard_map/project/pallas_call | solution.py:562
  12.2 1.1 slice_bitcast_fusion
  13.3 0.7 collective-permute-start
  14.0 1.6 %collective-permute-start.1 = (bf16[64,1152]{1,0:T(8,128)(2,1)S(1)}, bf16[64,1152]{1,0:T(8,128)(2,1)S(1)}, u32[]{:S(2)}, u32[]{:S(2)}) collective-permute-start(bf16[64,1152]{1,0:T(8,128)(2,1)S(1)} %get-tuple-element.34), channel_id=1, source_target_pairs={{0,8},{1,24},{2,46},{3,62},{4,74},{5,90},{6,108},{7,124},{8,0},{9,... | collective-permute-start | bytes 442376 | tf_op jit(solution)/shard_map/ppermute | solution.py:626
  15.6 3.6 %collective-permute-done.1 = bf16[64,1152]{1,0:T(8,128)(2,1)S(1)} collective-permute-done((bf16[64,1152]{1,0:T(8,128)(2,1)S(1)}, bf16[64,1152]{1,0:T(8,128)(2,1)S(1)}, u32[]{:S(2)}, u32[]{:S(2)}) %collective-permute-start.1) | collective-permute-done | bytes 147488 | tf_op jit(solution)/shard_map/ppermute | solution.py:626
  19.2 25.9 %all_to_all.15.sums_ref = f32[16,40,128]{2,1,0:T(8,128)S(1)} all-to-all(f32[16,40,128]{2,1,0:T(8,128)} %get-tuple-element.22), channel_id=1, replica_groups=mesh['row'=16,'col'=8] {'row'}, dimensions={0} | all-to-all | bytes 655360 | tf_op jit(solution)/shard_map/all_to_all | solution.py:684
  45.1 2.6 %attend.1 = f32[40,512]{1,0:T(8,128)} custom-call(bf16[1024,256]{1,0:T(8,128)(2,1)S(1)} %copy-done.9, s32[64,64]{1,0:T(8,128)S(1)} %copy-done.3, f32[16,40,128]{2,1,0:T(8,128)S(1)} %all_to_all.15.sums_ref, bf16[64,64]{1,0:T(8,128)(2,1)S(1)} %copy-done.4, bf16[8,64]{1,0:T(8,128)(2,1)S(1)} %bitcast.35, bf16[8,64]{1,0:T(8,128)(2,1)S(1)} %bitcast.36), custom_call_target="tpu_custom_call" | custom-call | flops 3000000000 | bytes 3000000 | tf_op jit(solution)/shard_map/attend/pallas_call | solution.py:578
  47.7 0.9 collective-permute-start.2
  48.6 3.3 %collective-permute-start.3 = (bf16[128,1152]{1,0:T(8,128)(2,1)S(1)}, bf16[128,1152]{1,0:T(8,128)(2,1)S(1)}, u32[]{:S(2)}, u32[]{:S(2)}) collective-permute-start(bf16[128,1152]{1,0:T(8,128)(2,1)S(1)} %get-tuple-element.36), channel_id=1, source_target_pairs={{0,6},{1,7},{2,0},{3,1},{4,2},{5,3},{6,4},{7,5},{8,14},{9,15},{10,... | collective-permute-start | bytes 884744 | tf_op jit(solution)/shard_map/ppermute | solution.py:600
  51.9 0.2 copy.30
  52.2 0.1 copy.33.final_ref
  52.5 0.1 copy.31
  52.7 0.1 copy.34.gain_ref
  52.8 0.1 copy.32
  52.9 6.6 %collective-permute-done.2 = bf16[128,1152]{1,0:T(8,128)(2,1)S(1)} collective-permute-done((bf16[128,1152]{1,0:T(8,128)(2,1)S(1)}, bf16[128,1152]{1,0:T(8,128)(2,1)S(1)}, u32[]{:S(2)}, u32[]{:S(2)}) %collective-permute-start.2) | collective-permute-done | bytes 294944 | tf_op jit(solution)/shard_map/ppermute | solution.py:599
  59.6 3.3 %collective-permute-start.5 = (bf16[64,1152]{1,0:T(8,128)(2,1)S(1)}, bf16[64,1152]{1,0:T(8,128)(2,1)S(1)}, u32[]{:S(2)}, u32[]{:S(2)}) collective-permute-start(bf16[64,1152]{1,0:T(8,128)(2,1)S(1)} %slice.33), channel_id=1, source_target_pairs={{0,6},{1,7},{2,0},{3,1},{4,2},{5,3},{6,4},{7,5},{8,14},{9,15},{10,... | collective-permute-start | bytes 442376 | tf_op jit(solution)/shard_map/ppermute | solution.py:603
  63.0 3.6 %collective-permute-done.4 = bf16[64,1152]{1,0:T(8,128)(2,1)S(1)} collective-permute-done((bf16[64,1152]{1,0:T(8,128)(2,1)S(1)}, bf16[64,1152]{1,0:T(8,128)(2,1)S(1)}, u32[]{:S(2)}, u32[]{:S(2)}) %collective-permute-start.4) | collective-permute-done | bytes 147488 | tf_op jit(solution)/shard_map/ppermute | solution.py:602
  66.9 1.4 prepare.1.base_ref
  68.4 1.0 copy-done.10
  69.3 0.3 collective-permute-done.6.other_a_ref.other_b_ref.other_mask_ref
  69.7 13.4 %pair.1 = (f32[16,128,128]{2,1,0:T(8,128)S(1)}, bf16[16,128,128]{2,1,0:T(8,128)(2,1)S(1)}, bf16[128,32,128]{2,1,0:T(8,128)(2,1)S(1)}) custom-call(bf16[512,1152]{1,0:T(8,128)(2,1)} %copy-done.15, bf16[512,1152]{1,0:T(8,128)(2,1)} %copy-done.15, bf16[512,1152]{1,0:T(8,128)(2,1)} %copy-done.15, ...), custom_call_target="tpu_custom_call" | custom-call | flops 16000000000 | bytes 16000000 | tf_op jit(solution)/shard_map/pair/pallas_call | solution.py:488
  83.1 26.7 %all_to_all.16 = bf16[128,32,128]{2,1,0:T(8,128)(2,1)S(1)} all-to-all(bf16[128,32,128]{2,1,0:T(8,128)(2,1)S(1)} %get-tuple-element.31), channel_id=1, replica_groups=mesh['row'=16,'col'=8] {'row','col'}, dimensions={0} | all-to-all | bytes 2097152 | tf_op jit(solution)/shard_map/all_to_all | solution.py:726
  109.8 1.6 %triangle.1 = bf16[16,8,16,128]{3,2,1,0:T(8,128)(2,1)} custom-call(bf16[16,8,32,128]{3,2,1,0:T(8,128)(2,1)S(1)} %bitcast.29), custom_call_target="tpu_custom_call" | custom-call | flops 2000000000 | bytes 2000000 | tf_op jit(solution)/shard_map/triangle/pallas_call | solution.py:519
  111.4 4.8 %all-to-all-start.2 = ((bf16[128,16,128]{2,1,0:T(8,128)(2,1)}), bf16[128,16,128]{2,1,0:T(8,128)(2,1)S(1)}, u32[]{:S(2)}, u32[]{:S(2)}) async-start(bf16[128,16,128]{2,1,0:T(8,128)(2,1)} %bitcast.15), calls=%async_computation.2 | async-start | bytes 1048576 | tf_op jit(solution)/shard_map/all_to_all | solution.py:728
  116.4 0.1 copy.36
  116.5 0.1 copy.37.gain_ref
  116.6 8.8 %all-gather.3.cloned.1.call-done.part_ref = f32[640,512]{1,0:T(8,128)} async-done(((f32[40,512]{1,0:T(8,128)}), f32[640,512]{1,0:T(8,128)}) %all-gather.3.cloned.1.call-update) | async-done | bytes 1310736 | tf_op jit(solution)/shard_map/all_gather | solution.py:696
  125.4 1.3 copy-done
  126.7 1.9 %refresh.1 = bf16[64,4096]{1,0:T(8,128)(2,1)} custom-call(f32[640,512]{1,0:T(8,128)S(1)} %copy-done, bf16[1024,256]{1,0:T(8,128)(2,1)S(1)} %copy-done.9, bf16[64,4096]{1,0:T(8,128)(2,1)S(1)} %copy-done.2, bf16[64,64]{1,0:T(8,128)(2,1)S(1)} %copy-done.5, bf16[64,64]{1,0:T(8,128)(2,1)S(1)} %copy-done.6), custom_call_target="tpu_custom_call" | custom-call | flops 2000000000 | bytes 2000000 | tf_op jit(solution)/shard_map/refresh/pallas_call | solution.py:588
  128.6 0.8 gate.1.gate_ref
  129.4 1.4 %all-to-all-done.2.product_ref = bf16[128,16,128]{2,1,0:T(8,128)(2,1)S(1)} async-done(((bf16[128,16,128]{2,1,0:T(8,128)(2,1)}), bf16[128,16,128]{2,1,0:T(8,128)(2,1)S(1)}, u32[]{:S(2)}, u32[]{:S(2)}) %all-to-all-start.2) | async-done | bytes 524320 | tf_op jit(solution)/shard_map/all_to_all | solution.py:728
  130.8 2.9 %finish.1 = f32[2,16,64,128]{3,2,1,0:T(8,128)} custom-call(bf16[128,16,128]{2,1,0:T(8,128)(2,1)S(1)} %all-to-all-done.2.product_ref, f32[16,128,128]{2,1,0:T(8,128)S(1)} %get-tuple-element.32.mid_ref, f32[16,128,128]{2,1,0:T(8,128)S(1)} %gate.1.gate_ref, bf16[128,128]{1,0:T(8,128)(2,1)S(1)} %bitcast.32, f32[128,1]{1,0:T(8,128)S(1)} %copy.37.gain_ref), custom_call_target="tpu_custom_call" | custom-call | flops 3000000000 | bytes 3000000 | tf_op jit(solution)/shard_map/finish/pallas_call | solution.py:542
  (68 shorter events, 1.1 us)
Async XLA Ops:
  7.2 62.5 %all-gather.5.cloned.1.call-start = ((), (), s32[]{:S(2)}) async-start(), calls=%async_computation.4 | async-start | bytes 4734976 | tf_op jit(solution)/shard_map/all_gather | solution.py:682
  12.1 33.0 %copy-start.3 = (s32[64,64]{1,0:T(8,128)S(1)}, s32[64,64]{1,0:T(8,128)}, u32[]{:S(2)}) copy-start(s32[64,64]{1,0:T(8,128)} %cover_ref.3) | copy-start | bytes 49156
  12.1 33.0 %copy-start.4 = (bf16[64,64]{1,0:T(8,128)(2,1)S(1)}, bf16[64,64]{1,0:T(8,128)(2,1)}, u32[]{:S(2)}) copy-start(bf16[64,64]{1,0:T(8,128)(2,1)} %asking_ref.1) | copy-start | bytes 24580
  12.1 33.0 %copy-start.7 = (bf16[64,8]{0,1:T(8,128)(2,1)S(1)}, bf16[64,8]{0,1:T(8,128)(2,1)}, u32[]{:S(2)}) copy-start(bf16[64,8]{0,1:T(8,128)(2,1)} %param.28) | copy-start | bytes 3076
  12.1 32.9 %copy-start.8 = (bf16[64,8]{0,1:T(8,128)(2,1)S(1)}, bf16[64,8]{0,1:T(8,128)(2,1)}, u32[]{:S(2)}) copy-start(bf16[64,8]{0,1:T(8,128)(2,1)} %param.29) | copy-start | bytes 3076
  12.1 32.9 %copy-start.9 = (bf16[1024,256]{1,0:T(8,128)(2,1)S(1)}, bf16[1024,256]{1,0:T(8,128)(2,1)}, u32[]{:S(2)}) copy-start(bf16[1024,256]{1,0:T(8,128)(2,1)} %get-tuple-element.25.source_ref) | copy-start | bytes 1572868
  12.1 113.2 %all-gather.3.cloned.1.call-start = ((), (), s32[]{:S(2)}) async-start(), calls=%async_computation.3 | async-start | bytes 1392640 | tf_op jit(solution)/shard_map/all_gather | solution.py:696
  13.3 2.3 %collective-permute-start = (bf16[64,1152]{1,0:T(8,128)(2,1)S(1)}, bf16[64,1152]{1,0:T(8,128)(2,1)S(1)}, u32[]{:S(2)}, u32[]{:S(2)}) collective-permute-start(bf16[64,1152]{1,0:T(8,128)(2,1)S(1)} %get-tuple-element.35), channel_id=1, source_target_pairs={{0,0},{1,16},{2,38},{3,54},{4,66},{5,82},{6,100},{7,116},{8,8},{9,... | collective-permute-start | bytes 442376 | tf_op jit(solution)/shard_map/ppermute | solution.py:626
  14.0 5.2 %collective-permute-start.1 = (bf16[64,1152]{1,0:T(8,128)(2,1)S(1)}, bf16[64,1152]{1,0:T(8,128)(2,1)S(1)}, u32[]{:S(2)}, u32[]{:S(2)}) collective-permute-start(bf16[64,1152]{1,0:T(8,128)(2,1)S(1)} %get-tuple-element.34), channel_id=1, source_target_pairs={{0,8},{1,24},{2,46},{3,62},{4,74},{5,90},{6,108},{7,124},{8,0},{9,... | collective-permute-start | bytes 442376 | tf_op jit(solution)/shard_map/ppermute | solution.py:626
  45.1 6.9 %copy-start.11 = (bf16[1024,128]{1,0:T(8,128)(2,1)S(1)}, bf16[1024,128]{1,0:T(8,128)(2,1)}, u32[]{:S(2)}) copy-start(bf16[1024,128]{1,0:T(8,128)(2,1)} %param.35) | copy-start | bytes 786436
  47.6 4.7 %copy-start.20 = (s32[512]{0:T(512)S(1)}, s32[512]{0:T(512)}, u32[]{:S(2)}) copy-start(s32[512]{0:T(512)} %param.25) | copy-start | bytes 6148
  47.6 4.9 %copy-start.17 = (f32[2,128]{1,0:T(2,128)S(1)}, f32[2,128]{1,0:T(2,128)}, u32[]{:S(2)}) copy-start(f32[2,128]{1,0:T(2,128)} %param.36) | copy-start | bytes 3076
  47.7 5.0 %copy-start.16 = (s32[32,64]{1,0:T(8,128)S(1)}, s32[32,64]{1,0:T(8,128)}, u32[]{:S(2)}) copy-start(s32[32,64]{1,0:T(8,128)} %param.24) | copy-start | bytes 24580
  47.7 5.0 %copy-start.18 = (f32[128]{0:T(128)S(1)}, f32[128]{0:T(128)}, u32[]{:S(2)}) copy-start(f32[128]{0:T(128)} %param.37) | copy-start | bytes 1540
  47.7 5.1 %copy-start.12 = (bf16[128,512]{1,0:T(8,128)(2,1)S(1)}, bf16[128,512]{1,0:T(8,128)(2,1)}, u32[]{:S(2)}) copy-start(bf16[128,512]{1,0:T(8,128)(2,1)} %param.38) | copy-start | bytes 393220
  47.7 11.8 %collective-permute-start.2 = (bf16[128,1152]{1,0:T(8,128)(2,1)S(1)}, bf16[128,1152]{1,0:T(8,128)(2,1)S(1)}, u32[]{:S(2)}, u32[]{:S(2)}) collective-permute-start(bf16[128,1152]{1,0:T(8,128)(2,1)S(1)} %get-tuple-element.36), channel_id=1, source_target_pairs={{0,2},{1,3},{2,4},{3,5},{4,6},{5,7},{6,0},{7,1},{8,10},{9,11},{10,... | collective-permute-start | bytes 884744 | tf_op jit(solution)/shard_map/ppermute | solution.py:599
  48.6 11.0 %collective-permute-start.3 = (bf16[128,1152]{1,0:T(8,128)(2,1)S(1)}, bf16[128,1152]{1,0:T(8,128)(2,1)S(1)}, u32[]{:S(2)}, u32[]{:S(2)}) collective-permute-start(bf16[128,1152]{1,0:T(8,128)(2,1)S(1)} %get-tuple-element.36), channel_id=1, source_target_pairs={{0,6},{1,7},{2,0},{3,1},{4,2},{5,3},{6,4},{7,5},{8,14},{9,15},{10,... | collective-permute-start | bytes 884744 | tf_op jit(solution)/shard_map/ppermute | solution.py:600
  52.9 14.0 %copy-start.1 = (f32[32,64,128]{2,1,0:T(8,128)S(1)}, f32[32,64,128]{2,1,0:T(8,128)}, u32[]{:S(2)}) copy-start(f32[32,64,128]{2,1,0:T(8,128)} %param.23) | copy-start | bytes 3145732
  59.5 7.0 %collective-permute-start.4 = (bf16[64,1152]{1,0:T(8,128)(2,1)S(1)}, bf16[64,1152]{1,0:T(8,128)(2,1)S(1)}, u32[]{:S(2)}, u32[]{:S(2)}) collective-permute-start(bf16[64,1152]{1,0:T(8,128)(2,1)S(1)} %slice.32), channel_id=1, source_target_pairs={{0,2},{1,3},{2,4},{3,5},{4,6},{5,7},{6,0},{7,1},{8,10},{9,11},{10,... | collective-permute-start | bytes 442376 | tf_op jit(solution)/shard_map/ppermute | solution.py:602
  59.6 6.9 %collective-permute-start.5 = (bf16[64,1152]{1,0:T(8,128)(2,1)S(1)}, bf16[64,1152]{1,0:T(8,128)(2,1)S(1)}, u32[]{:S(2)}, u32[]{:S(2)}) collective-permute-start(bf16[64,1152]{1,0:T(8,128)(2,1)S(1)} %slice.33), channel_id=1, source_target_pairs={{0,6},{1,7},{2,0},{3,1},{4,2},{5,3},{6,4},{7,5},{8,14},{9,15},{10,... | collective-permute-start | bytes 442376 | tf_op jit(solution)/shard_map/ppermute | solution.py:603
  66.6 1.7 %copy-start.15 = (bf16[512,1152]{1,0:T(8,128)(2,1)}, bf16[512,1152]{1,0:T(8,128)(2,1)S(1)}, u32[]{:S(2)}) copy-start(bf16[512,1152]{1,0:T(8,128)(2,1)S(1)} %constant_dynamic-update-slice_fusion.2.own_a_ref.own_b_ref.own_mask_ref) | copy-start | bytes 3538948
  66.6 3.1 %collective-permute-start.6 = (bf16[512,1152]{1,0:T(8,128)(2,1)S(1)}, bf16[512,1152]{1,0:T(8,128)(2,1)}, u32[]{:S(2)}, u32[]{:S(2)}) collective-permute-start(bf16[512,1152]{1,0:T(8,128)(2,1)S(1)} %constant_dynamic-update-slice_fusion.2.own_a_ref.own_b_ref.own_mask_ref), channel_id=1, source_target_pairs={{0,1},{1,0},{2,3},{3,2},{4,5},{5,4},{6,7},{7,6},{8,9},{9,8},{10,11... | collective-permute-start | bytes 3538952 | tf_op jit(solution)/shard_map/ppermute | solution.py:636
  68.3 1.0 copy-start.10
  109.8 6.4 %copy-start.13 = (bf16[128,128]{1,0:T(8,128)(2,1)S(1)}, bf16[128,128]{1,0:T(8,128)(2,1)}, u32[]{:S(2)}) copy-start(bf16[128,128]{1,0:T(8,128)(2,1)} %param.39) | copy-start | bytes 98308
  109.8 6.5 %copy-start.14 = (bf16[128,128]{1,0:T(8,128)(2,1)S(1)}, bf16[128,128]{1,0:T(8,128)(2,1)}, u32[]{:S(2)}) copy-start(bf16[128,128]{1,0:T(8,128)(2,1)} %param.41) | copy-start | bytes 98308
  111.4 5.0 %copy-start.19 = (f32[128]{0:T(128)S(1)}, f32[128]{0:T(128)}, u32[]{:S(2)}) copy-start(f32[128]{0:T(128)} %param.40) | copy-start | bytes 1540
  111.4 13.9 %copy-start.2 = (bf16[64,4096]{1,0:T(8,128)(2,1)S(1)}, bf16[64,4096]{1,0:T(8,128)(2,1)}, u32[]{:S(2)}) copy-start(bf16[64,4096]{1,0:T(8,128)(2,1)} %msa_ref.3) | copy-start | bytes 1572868
  111.4 13.9 %copy-start.5 = (bf16[64,64]{1,0:T(8,128)(2,1)S(1)}, bf16[64,64]{1,0:T(8,128)(2,1)}, u32[]{:S(2)}) copy-start(bf16[64,64]{1,0:T(8,128)(2,1)} %sigmoid_ref.1) | copy-start | bytes 24580
  111.4 13.9 %copy-start.6 = (bf16[64,64]{1,0:T(8,128)(2,1)S(1)}, bf16[64,64]{1,0:T(8,128)(2,1)}, u32[]{:S(2)}) copy-start(bf16[64,64]{1,0:T(8,128)(2,1)} %final_ref.1) | copy-start | bytes 24580
  111.4 19.4 %all-to-all-start.2 = ((bf16[128,16,128]{2,1,0:T(8,128)(2,1)}), bf16[128,16,128]{2,1,0:T(8,128)(2,1)S(1)}, u32[]{:S(2)}, u32[]{:S(2)}) async-start(bf16[128,16,128]{2,1,0:T(8,128)(2,1)} %bitcast.15), calls=%async_computation.2 | async-start | bytes 1048576 | tf_op jit(solution)/shard_map/all_to_all | solution.py:728
  125.4 1.3 copy-start
Sparse Core Ops, SparseCore 0:
  12.3 56.9 all-gather.4
  72.0 53.3 all-gather.2

commit v5 on v4

--- a/solution.py
+++ b/solution.py
@@ -276,7 +276,7 @@
 ):
     step = pl.program_id(0)
     steps = pl.num_programs(0)
-    rows = 4
+    rows = 8
     low = lane_index((LANES, LANES)) < HALF
     odd = lax.axis_index("row") % 2
     col = lax.axis_index("col")
@@ -318,7 +318,7 @@
     sources = []
     for p in range(rows):
         halves = []
-        for top in (p * 32, 128 + p * 32):
+        for top in (p * 32, 256 + p * 32):
             halves.append(
                 jnp.concatenate(
                     [outer_ref[top : top + 32, d * LANES : (d + 1) * LANES] for d in range(16)],
@@ -410,7 +410,7 @@
 
 def finish_kernel(product_ref, mid_ref, gate_ref, final_ref, gain_ref, out_ref, normal_ref):
     step = pl.program_id(0)
-    rows = 4
+    rows = 8
 
     @pl.when(step == 0)
     def _():
@@ -446,12 +446,12 @@
     return pl.BlockSpec(shape, lambda t: (0,) * len(shape), pipeline_mode=pl.Buffered(1))
 
 
-def by_rows():
-    return pl.BlockSpec((2, 4, HALF, LANES), lambda t: (0, t, 0, 0))
-
-
-def by_pairs():
-    return pl.BlockSpec((4, LANES, LANES), lambda t: (t, 0, 0))
+def by_rows(rows=4):
+    return pl.BlockSpec((2, rows, HALF, LANES), lambda t: (0, t, 0, 0))
+
+
+def by_pairs(rows=4):
+    return pl.BlockSpec((rows, LANES, LANES), lambda t: (t, 0, 0))
 
 
 PARAMS = pltpu.CompilerParams(
@@ -478,8 +478,8 @@
 
 def by_left():
     return [
-        pl.BlockSpec((512, LANES), lambda t: (0, t)),
-        pl.BlockSpec((512, LANES), lambda t: (0, t + 4)),
+        pl.BlockSpec((512, 256), lambda t: (0, t)),
+        pl.BlockSpec((512, 256), lambda t: (0, t + 2)),
         pl.BlockSpec((512, LANES), lambda t: (0, 8), pipeline_mode=pl.Buffered(1)),
     ]
 
@@ -487,25 +487,25 @@
 def pair_call(own, other, right, final, base, cover, gain, mapping):
     return pl.pallas_call(
         pair_kernel,
-        grid=(4,),
+        grid=(2,),
         in_specs=[
             *by_left(),
             *by_left(),
             whole((1024, 2176)),
             whole((256, 512)),
-            by_pairs(),
+            by_pairs(8),
             whole((16, LANES)),
             whole((LANES, 1)),
             whole((512, LANES)),
         ],
-        out_specs=[by_pairs(), by_pairs(), whole((LANES, 32, LANES))],
+        out_specs=[by_pairs(8), by_pairs(8), whole((LANES, 32, LANES))],
         out_shape=[
             jax.ShapeDtypeStruct((16, LANES, LANES), jnp.float32),
             jax.ShapeDtypeStruct((16, LANES, LANES), jnp.bfloat16),
             jax.ShapeDtypeStruct((LANES, 32, LANES), jnp.bfloat16),
         ],
         scratch_shapes=[
-            pltpu.VMEM((256, 2048), jnp.bfloat16),
+            pltpu.VMEM((512, 2048), jnp.bfloat16),
             pltpu.VMEM((16, LANES), jnp.float32),
             pltpu.VMEM((32 * LANES, LANES), jnp.float32),
         ],
@@ -541,15 +541,15 @@
 def finish_call(product, mid, gate, final, gain):
     return pl.pallas_call(
         finish_kernel,
-        grid=(4,),
+        grid=(2,),
         in_specs=[
             whole((LANES, 16, LANES)),
-            by_pairs(),
-            by_pairs(),
+            by_pairs(8),
+            by_pairs(8),
             whole((LANES, LANES)),
             whole((LANES, 1)),
         ],
-        out_specs=by_rows(),
+        out_specs=by_rows(8),
         out_shape=jax.ShapeDtypeStruct((2, 16, HALF, LANES), jnp.float32),
         scratch_shapes=[pltpu.VMEM((LANES * 16, LANES), jnp.float32)],
         compiler_params=PARAMS,

time: 142 us -> 141 us (level)
  Pallas kernels: 29.5 us -> 27.2 us
  waiting for transfers between devices: 24.3 us -> 25.8 us
    all_gather x1, waiting for transfers between devices: 8.75 us -> 11.6 us  [local(): parts = lax.all_gather(parts, 'row', axis=0, tiled=True)]
    pallas_call x2, Pallas kernels: 16.3 us -> 14.1 us  [the longest x1 11.9 us: pair_call(): pl.pallas_call(pair_kernel, grid=(2,), in_specs=[*by_left(), *by_left(),...]
  transfers between devices with their start and end apart: 10 -> 10, of which waited for: 6 -> 6; matrix products, arithmetic and copies ran while one was open for 2% -> 2% of each run, Pallas kernels for 15% -> 14%
where the time goes in v5:
time: 141 us; the launch traced here: 140 us
  blocking collectives  52.7 us (37%)
  Pallas kernels  27.2 us (19%)
  waiting for transfers between devices  25.8 us (18%)
  starting transfers between devices  14.8 us (10%)
  between operations  14.4 us (10%)
  local copies, waits for them, and re-layouts  4.89 us (3%)
    all_to_all x1, blocking collectives, local(): taken = lax.all_to_all(sides, ('row', 'col'), 0, 0, tiled=True)  26.9 us
    all_to_all x1, blocking collectives, local(): sums = lax.all_to_all(sums, 'row', 0, 0, tiled=True)  25.9 us
    pallas_call x1, Pallas kernels, pair_call(): pl.pallas_call(pair_kernel, grid=(2,), in_specs=[*by_left(), *by_left(),...  11.9 us
    all_gather x1, waiting for transfers between devices, local(): parts = lax.all_gather(parts, 'row', axis=0, tiled=True)  11.6 us
    ppermute x1, waiting for transfers between devices, ring_of_four(): back = lax.ppermute(block, axis, step(1))  6.56 us
    pallas_call x1, Pallas kernels, project_call(): pl.pallas_call(project_kernel, out_shape=[jax.ShapeDtypeStruct((2, 64, 11...  4.87 us
    all_to_all x1, starting transfers between devices, local(): lax.all_to_all(product.reshape(n_row * n_col, 16, LANES), ('row', 'col'),...  4.77 us
    ppermute x2, waiting for transfers between devices, route_left(): lax.ppermute(left[flip], ('row', 'col'), route(flip))  3.57 us
  transfers between devices with their start and end apart: 10, of which 6 were waited for; matrix products, arithmetic and copies ran while one was open for 2% of the time, Pallas kernels for 14%

profile of v5, /device:TPU:0, one launch (start us, length us, event | category | flops | bytes accessed | tf_op | source)
XLA Modules:
  0.0 140.0 jit_solution(3950465909965304515)
XLA Ops:
  7.2 4.9 %project.1 = (bf16[2,64,1152]{2,1,0:T(8,128)(2,1)}, bf16[64,2176]{1,0:T(8,128)(2,1)}, bf16[1024,256]{1,0:T(8,128)(2,1)}, f32[16,40,128]{2,1,0:T(8,128)}) custom-call(bf16[64,4096]{1,0:T(8,128)(2,1)} %msa_ref.3, s32[64,64]{1,0:T(8,128)} %cover_ref.3, f32[1,64]{1,0:T(1,128)} %bitcast.44, f32[1,64]{1,0:T(1,128)} %bitcast.45, bf16[32,64]{1,0:T(8,128)(2,1)} %bitcast.42, ...), custom_call_target="tpu_custom_call" | custom-call | flops 4000000000 | bytes 4000000 | tf_op jit(solution)/shard_map/project/pallas_call | solution.py:562
  12.2 1.1 slice_bitcast_fusion
  13.3 0.7 collective-permute-start
  14.0 1.6 %collective-permute-start.1 = (bf16[64,1152]{1,0:T(8,128)(2,1)S(1)}, bf16[64,1152]{1,0:T(8,128)(2,1)S(1)}, u32[]{:S(2)}, u32[]{:S(2)}) collective-permute-start(bf16[64,1152]{1,0:T(8,128)(2,1)S(1)} %get-tuple-element.34), channel_id=1, source_target_pairs={{0,8},{1,24},{2,46},{3,62},{4,74},{5,90},{6,108},{7,124},{8,0},{9,... | collective-permute-start | bytes 442376 | tf_op jit(solution)/shard_map/ppermute | solution.py:626
  15.6 3.6 %collective-permute-done.1 = bf16[64,1152]{1,0:T(8,128)(2,1)S(1)} collective-permute-done((bf16[64,1152]{1,0:T(8,128)(2,1)S(1)}, bf16[64,1152]{1,0:T(8,128)(2,1)S(1)}, u32[]{:S(2)}, u32[]{:S(2)}) %collective-permute-start.1) | collective-permute-done | bytes 147488 | tf_op jit(solution)/shard_map/ppermute | solution.py:626
  19.2 25.9 %all_to_all.15.sums_ref = f32[16,40,128]{2,1,0:T(8,128)S(1)} all-to-all(f32[16,40,128]{2,1,0:T(8,128)} %get-tuple-element.22), channel_id=1, replica_groups=mesh['row'=16,'col'=8] {'row'}, dimensions={0} | all-to-all | bytes 655360 | tf_op jit(solution)/shard_map/all_to_all | solution.py:684
  45.1 2.6 %attend.1 = f32[40,512]{1,0:T(8,128)} custom-call(bf16[1024,256]{1,0:T(8,128)(2,1)S(1)} %copy-done.9, s32[64,64]{1,0:T(8,128)S(1)} %copy-done.3, f32[16,40,128]{2,1,0:T(8,128)S(1)} %all_to_all.15.sums_ref, bf16[64,64]{1,0:T(8,128)(2,1)S(1)} %copy-done.4, bf16[8,64]{1,0:T(8,128)(2,1)S(1)} %bitcast.35, bf16[8,64]{1,0:T(8,128)(2,1)S(1)} %bitcast.36), custom_call_target="tpu_custom_call" | custom-call | flops 3000000000 | bytes 3000000 | tf_op jit(solution)/shard_map/attend/pallas_call | solution.py:578
  47.7 0.9 collective-permute-start.2
  48.6 3.3 %collective-permute-start.3 = (bf16[128,1152]{1,0:T(8,128)(2,1)S(1)}, bf16[128,1152]{1,0:T(8,128)(2,1)S(1)}, u32[]{:S(2)}, u32[]{:S(2)}) collective-permute-start(bf16[128,1152]{1,0:T(8,128)(2,1)S(1)} %get-tuple-element.36), channel_id=1, source_target_pairs={{0,6},{1,7},{2,0},{3,1},{4,2},{5,3},{6,4},{7,5},{8,14},{9,15},{10,... | collective-permute-start | bytes 884744 | tf_op jit(solution)/shard_map/ppermute | solution.py:600
  51.9 0.2 copy.30
  52.2 0.1 copy.33.final_ref
  52.5 0.1 copy.31
  52.7 0.1 copy.34.gain_ref
  52.8 0.1 copy.32
  52.9 6.6 %collective-permute-done.2 = bf16[128,1152]{1,0:T(8,128)(2,1)S(1)} collective-permute-done((bf16[128,1152]{1,0:T(8,128)(2,1)S(1)}, bf16[128,1152]{1,0:T(8,128)(2,1)S(1)}, u32[]{:S(2)}, u32[]{:S(2)}) %collective-permute-start.2) | collective-permute-done | bytes 294944 | tf_op jit(solution)/shard_map/ppermute | solution.py:599
  59.6 3.3 %collective-permute-start.5 = (bf16[64,1152]{1,0:T(8,128)(2,1)S(1)}, bf16[64,1152]{1,0:T(8,128)(2,1)S(1)}, u32[]{:S(2)}, u32[]{:S(2)}) collective-permute-start(bf16[64,1152]{1,0:T(8,128)(2,1)S(1)} %slice.33), channel_id=1, source_target_pairs={{0,6},{1,7},{2,0},{3,1},{4,2},{5,3},{6,4},{7,5},{8,14},{9,15},{10,... | collective-permute-start | bytes 442376 | tf_op jit(solution)/shard_map/ppermute | solution.py:603
  63.0 3.6 %collective-permute-done.4 = bf16[64,1152]{1,0:T(8,128)(2,1)S(1)} collective-permute-done((bf16[64,1152]{1,0:T(8,128)(2,1)S(1)}, bf16[64,1152]{1,0:T(8,128)(2,1)S(1)}, u32[]{:S(2)}, u32[]{:S(2)}) %collective-permute-start.4) | collective-permute-done | bytes 147488 | tf_op jit(solution)/shard_map/ppermute | solution.py:602
  66.9 1.4 prepare.1.base_ref
  68.4 1.0 copy-done.10
  69.3 0.3 collective-permute-done.6.other_a_ref.other_b_ref.other_mask_ref
  69.7 11.9 %pair.1 = (f32[16,128,128]{2,1,0:T(8,128)S(1)}, bf16[16,128,128]{2,1,0:T(8,128)(2,1)S(1)}, bf16[128,32,128]{2,1,0:T(8,128)(2,1)S(1)}) custom-call(bf16[512,1152]{1,0:T(8,128)(2,1)} %copy-done.15, bf16[512,1152]{1,0:T(8,128)(2,1)} %copy-done.15, bf16[512,1152]{1,0:T(8,128)(2,1)} %copy-done.15, ...), custom_call_target="tpu_custom_call" | custom-call | flops 16000000000 | bytes 16000000 | tf_op jit(solution)/shard_map/pair/pallas_call | solution.py:488
  81.6 26.9 %all_to_all.16 = bf16[128,32,128]{2,1,0:T(8,128)(2,1)S(1)} all-to-all(bf16[128,32,128]{2,1,0:T(8,128)(2,1)S(1)} %get-tuple-element.31), channel_id=1, replica_groups=mesh['row'=16,'col'=8] {'row','col'}, dimensions={0} | all-to-all | bytes 2097152 | tf_op jit(solution)/shard_map/all_to_all | solution.py:726
  108.4 1.6 %triangle.1 = bf16[16,8,16,128]{3,2,1,0:T(8,128)(2,1)} custom-call(bf16[16,8,32,128]{3,2,1,0:T(8,128)(2,1)S(1)} %bitcast.29), custom_call_target="tpu_custom_call" | custom-call | flops 2000000000 | bytes 2000000 | tf_op jit(solution)/shard_map/triangle/pallas_call | solution.py:519
  110.1 4.8 %all-to-all-start.2 = ((bf16[128,16,128]{2,1,0:T(8,128)(2,1)}), bf16[128,16,128]{2,1,0:T(8,128)(2,1)S(1)}, u32[]{:S(2)}, u32[]{:S(2)}) async-start(bf16[128,16,128]{2,1,0:T(8,128)(2,1)} %bitcast.15), calls=%async_computation.2 | async-start | bytes 1048576 | tf_op jit(solution)/shard_map/all_to_all | solution.py:728
  115.0 0.1 copy.36
  115.1 0.1 copy.37.gain_ref
  115.2 11.6 %all-gather.3.cloned.1.call-done.part_ref = f32[640,512]{1,0:T(8,128)} async-done(((f32[40,512]{1,0:T(8,128)}), f32[640,512]{1,0:T(8,128)}) %all-gather.3.cloned.1.call-update) | async-done | bytes 1310736 | tf_op jit(solution)/shard_map/all_gather | solution.py:696
  126.8 1.3 copy-done
  128.1 1.9 %refresh.1 = bf16[64,4096]{1,0:T(8,128)(2,1)} custom-call(f32[640,512]{1,0:T(8,128)S(1)} %copy-done, bf16[1024,256]{1,0:T(8,128)(2,1)S(1)} %copy-done.9, bf16[64,4096]{1,0:T(8,128)(2,1)S(1)} %copy-done.2, bf16[64,64]{1,0:T(8,128)(2,1)S(1)} %copy-done.5, bf16[64,64]{1,0:T(8,128)(2,1)S(1)} %copy-done.6), custom_call_target="tpu_custom_call" | custom-call | flops 2000000000 | bytes 2000000 | tf_op jit(solution)/shard_map/refresh/pallas_call | solution.py:588
  130.1 0.8 gate.1.gate_ref
  130.8 0.2 all-to-all-done.2.product_ref
  131.0 2.2 %finish.1 = f32[2,16,64,128]{3,2,1,0:T(8,128)} custom-call(bf16[128,16,128]{2,1,0:T(8,128)(2,1)S(1)} %all-to-all-done.2.product_ref, f32[16,128,128]{2,1,0:T(8,128)S(1)} %get-tuple-element.32.mid_ref, f32[16,128,128]{2,1,0:T(8,128)S(1)} %gate.1.gate_ref, bf16[128,128]{1,0:T(8,128)(2,1)S(1)} %bitcast.32, f32[128,1]{1,0:T(8,128)S(1)} %copy.37.gain_ref), custom_call_target="tpu_custom_call" | custom-call | flops 3000000000 | bytes 3000000 | tf_op jit(solution)/shard_map/finish/pallas_call | solution.py:542
  (68 shorter events, 1.1 us)
Async XLA Ops:
  7.2 62.5 %all-gather.5.cloned.1.call-start = ((), (), s32[]{:S(2)}) async-start(), calls=%async_computation.4 | async-start | bytes 4734976 | tf_op jit(solution)/shard_map/all_gather | solution.py:682
  12.1 33.0 %copy-start.3 = (s32[64,64]{1,0:T(8,128)S(1)}, s32[64,64]{1,0:T(8,128)}, u32[]{:S(2)}) copy-start(s32[64,64]{1,0:T(8,128)} %cover_ref.3) | copy-start | bytes 49156
  12.1 33.0 %copy-start.4 = (bf16[64,64]{1,0:T(8,128)(2,1)S(1)}, bf16[64,64]{1,0:T(8,128)(2,1)}, u32[]{:S(2)}) copy-start(bf16[64,64]{1,0:T(8,128)(2,1)} %asking_ref.1) | copy-start | bytes 24580
  12.1 33.0 %copy-start.7 = (bf16[64,8]{0,1:T(8,128)(2,1)S(1)}, bf16[64,8]{0,1:T(8,128)(2,1)}, u32[]{:S(2)}) copy-start(bf16[64,8]{0,1:T(8,128)(2,1)} %param.28) | copy-start | bytes 3076
  12.1 33.0 %copy-start.8 = (bf16[64,8]{0,1:T(8,128)(2,1)S(1)}, bf16[64,8]{0,1:T(8,128)(2,1)}, u32[]{:S(2)}) copy-start(bf16[64,8]{0,1:T(8,128)(2,1)} %param.29) | copy-start | bytes 3076
  12.1 32.9 %copy-start.9 = (bf16[1024,256]{1,0:T(8,128)(2,1)S(1)}, bf16[1024,256]{1,0:T(8,128)(2,1)}, u32[]{:S(2)}) copy-start(bf16[1024,256]{1,0:T(8,128)(2,1)} %get-tuple-element.25.source_ref) | copy-start | bytes 1572868
  12.1 114.6 %all-gather.3.cloned.1.call-start = ((), (), s32[]{:S(2)}) async-start(), calls=%async_computation.3 | async-start | bytes 1392640 | tf_op jit(solution)/shard_map/all_gather | solution.py:696
  13.3 2.3 %collective-permute-start = (bf16[64,1152]{1,0:T(8,128)(2,1)S(1)}, bf16[64,1152]{1,0:T(8,128)(2,1)S(1)}, u32[]{:S(2)}, u32[]{:S(2)}) collective-permute-start(bf16[64,1152]{1,0:T(8,128)(2,1)S(1)} %get-tuple-element.35), channel_id=1, source_target_pairs={{0,0},{1,16},{2,38},{3,54},{4,66},{5,82},{6,100},{7,116},{8,8},{9,... | collective-permute-start | bytes 442376 | tf_op jit(solution)/shard_map/ppermute | solution.py:626
  14.0 5.2 %collective-permute-start.1 = (bf16[64,1152]{1,0:T(8,128)(2,1)S(1)}, bf16[64,1152]{1,0:T(8,128)(2,1)S(1)}, u32[]{:S(2)}, u32[]{:S(2)}) collective-permute-start(bf16[64,1152]{1,0:T(8,128)(2,1)S(1)} %get-tuple-element.34), channel_id=1, source_target_pairs={{0,8},{1,24},{2,46},{3,62},{4,74},{5,90},{6,108},{7,124},{8,0},{9,... | collective-permute-start | bytes 442376 | tf_op jit(solution)/shard_map/ppermute | solution.py:626
  45.1 6.9 %copy-start.11 = (bf16[1024,128]{1,0:T(8,128)(2,1)S(1)}, bf16[1024,128]{1,0:T(8,128)(2,1)}, u32[]{:S(2)}) copy-start(bf16[1024,128]{1,0:T(8,128)(2,1)} %param.35) | copy-start | bytes 786436
  47.6 4.7 %copy-start.20 = (s32[512]{0:T(512)S(1)}, s32[512]{0:T(512)}, u32[]{:S(2)}) copy-start(s32[512]{0:T(512)} %param.25) | copy-start | bytes 6148
  47.7 4.9 %copy-start.17 = (f32[2,128]{1,0:T(2,128)S(1)}, f32[2,128]{1,0:T(2,128)}, u32[]{:S(2)}) copy-start(f32[2,128]{1,0:T(2,128)} %param.36) | copy-start | bytes 3076
  47.7 5.0 %copy-start.16 = (s32[32,64]{1,0:T(8,128)S(1)}, s32[32,64]{1,0:T(8,128)}, u32[]{:S(2)}) copy-start(s32[32,64]{1,0:T(8,128)} %param.24) | copy-start | bytes 24580
  47.7 5.0 %copy-start.18 = (f32[128]{0:T(128)S(1)}, f32[128]{0:T(128)}, u32[]{:S(2)}) copy-start(f32[128]{0:T(128)} %param.37) | copy-start | bytes 1540
  47.7 5.1 %copy-start.12 = (bf16[128,512]{1,0:T(8,128)(2,1)S(1)}, bf16[128,512]{1,0:T(8,128)(2,1)}, u32[]{:S(2)}) copy-start(bf16[128,512]{1,0:T(8,128)(2,1)} %param.38) | copy-start | bytes 393220
  47.7 11.8 %collective-permute-start.2 = (bf16[128,1152]{1,0:T(8,128)(2,1)S(1)}, bf16[128,1152]{1,0:T(8,128)(2,1)S(1)}, u32[]{:S(2)}, u32[]{:S(2)}) collective-permute-start(bf16[128,1152]{1,0:T(8,128)(2,1)S(1)} %get-tuple-element.36), channel_id=1, source_target_pairs={{0,2},{1,3},{2,4},{3,5},{4,6},{5,7},{6,0},{7,1},{8,10},{9,11},{10,... | collective-permute-start | bytes 884744 | tf_op jit(solution)/shard_map/ppermute | solution.py:599
  48.6 11.0 %collective-permute-start.3 = (bf16[128,1152]{1,0:T(8,128)(2,1)S(1)}, bf16[128,1152]{1,0:T(8,128)(2,1)S(1)}, u32[]{:S(2)}, u32[]{:S(2)}) collective-permute-start(bf16[128,1152]{1,0:T(8,128)(2,1)S(1)} %get-tuple-element.36), channel_id=1, source_target_pairs={{0,6},{1,7},{2,0},{3,1},{4,2},{5,3},{6,4},{7,5},{8,14},{9,15},{10,... | collective-permute-start | bytes 884744 | tf_op jit(solution)/shard_map/ppermute | solution.py:600
  52.9 14.0 %copy-start.1 = (f32[32,64,128]{2,1,0:T(8,128)S(1)}, f32[32,64,128]{2,1,0:T(8,128)}, u32[]{:S(2)}) copy-start(f32[32,64,128]{2,1,0:T(8,128)} %param.23) | copy-start | bytes 3145732
  59.5 7.0 %collective-permute-start.4 = (bf16[64,1152]{1,0:T(8,128)(2,1)S(1)}, bf16[64,1152]{1,0:T(8,128)(2,1)S(1)}, u32[]{:S(2)}, u32[]{:S(2)}) collective-permute-start(bf16[64,1152]{1,0:T(8,128)(2,1)S(1)} %slice.32), channel_id=1, source_target_pairs={{0,2},{1,3},{2,4},{3,5},{4,6},{5,7},{6,0},{7,1},{8,10},{9,11},{10,... | collective-permute-start | bytes 442376 | tf_op jit(solution)/shard_map/ppermute | solution.py:602
  59.6 6.9 %collective-permute-start.5 = (bf16[64,1152]{1,0:T(8,128)(2,1)S(1)}, bf16[64,1152]{1,0:T(8,128)(2,1)S(1)}, u32[]{:S(2)}, u32[]{:S(2)}) collective-permute-start(bf16[64,1152]{1,0:T(8,128)(2,1)S(1)} %slice.33), channel_id=1, source_target_pairs={{0,6},{1,7},{2,0},{3,1},{4,2},{5,3},{6,4},{7,5},{8,14},{9,15},{10,... | collective-permute-start | bytes 442376 | tf_op jit(solution)/shard_map/ppermute | solution.py:603
  66.6 1.7 %copy-start.15 = (bf16[512,1152]{1,0:T(8,128)(2,1)}, bf16[512,1152]{1,0:T(8,128)(2,1)S(1)}, u32[]{:S(2)}) copy-start(bf16[512,1152]{1,0:T(8,128)(2,1)S(1)} %constant_dynamic-update-slice_fusion.2.own_a_ref.own_b_ref.own_mask_ref) | copy-start | bytes 3538948
  66.6 3.1 %collective-permute-start.6 = (bf16[512,1152]{1,0:T(8,128)(2,1)S(1)}, bf16[512,1152]{1,0:T(8,128)(2,1)}, u32[]{:S(2)}, u32[]{:S(2)}) collective-permute-start(bf16[512,1152]{1,0:T(8,128)(2,1)S(1)} %constant_dynamic-update-slice_fusion.2.own_a_ref.own_b_ref.own_mask_ref), channel_id=1, source_target_pairs={{0,1},{1,0},{2,3},{3,2},{4,5},{5,4},{6,7},{7,6},{8,9},{9,8},{10,11... | collective-permute-start | bytes 3538952 | tf_op jit(solution)/shard_map/ppermute | solution.py:636
  68.3 1.0 copy-start.10
  108.4 6.4 %copy-start.13 = (bf16[128,128]{1,0:T(8,128)(2,1)S(1)}, bf16[128,128]{1,0:T(8,128)(2,1)}, u32[]{:S(2)}) copy-start(bf16[128,128]{1,0:T(8,128)(2,1)} %param.39) | copy-start | bytes 98308
  108.4 6.5 %copy-start.14 = (bf16[128,128]{1,0:T(8,128)(2,1)S(1)}, bf16[128,128]{1,0:T(8,128)(2,1)}, u32[]{:S(2)}) copy-start(bf16[128,128]{1,0:T(8,128)(2,1)} %param.41) | copy-start | bytes 98308
  110.0 5.0 %copy-start.19 = (f32[128]{0:T(128)S(1)}, f32[128]{0:T(128)}, u32[]{:S(2)}) copy-start(f32[128]{0:T(128)} %param.40) | copy-start | bytes 1540
  110.0 16.7 %copy-start.2 = (bf16[64,4096]{1,0:T(8,128)(2,1)S(1)}, bf16[64,4096]{1,0:T(8,128)(2,1)}, u32[]{:S(2)}) copy-start(bf16[64,4096]{1,0:T(8,128)(2,1)} %msa_ref.3) | copy-start | bytes 1572868
  110.0 16.7 %copy-start.5 = (bf16[64,64]{1,0:T(8,128)(2,1)S(1)}, bf16[64,64]{1,0:T(8,128)(2,1)}, u32[]{:S(2)}) copy-start(bf16[64,64]{1,0:T(8,128)(2,1)} %sigmoid_ref.1) | copy-start | bytes 24580
  110.0 16.7 %copy-start.6 = (bf16[64,64]{1,0:T(8,128)(2,1)S(1)}, bf16[64,64]{1,0:T(8,128)(2,1)}, u32[]{:S(2)}) copy-start(bf16[64,64]{1,0:T(8,128)(2,1)} %final_ref.1) | copy-start | bytes 24580
  110.1 20.9 %all-to-all-start.2 = ((bf16[128,16,128]{2,1,0:T(8,128)(2,1)}), bf16[128,16,128]{2,1,0:T(8,128)(2,1)S(1)}, u32[]{:S(2)}, u32[]{:S(2)}) async-start(bf16[128,16,128]{2,1,0:T(8,128)(2,1)} %bitcast.15), calls=%async_computation.2 | async-start | bytes 1048576 | tf_op jit(solution)/shard_map/all_to_all | solution.py:728
  126.8 1.3 copy-start
Sparse Core Ops, SparseCore 0:
  12.3 56.9 all-gather.4
  72.0 54.7 all-gather.2

commit v6 on v5

--- a/solution.py
+++ b/solution.py
@@ -107,11 +107,11 @@
                 )
             wide = focus_cover[:, e * 256 : (e + 1) * 256]
             total = jnp.sum(wide * focus[rows].astype(jnp.float32), 0, keepdims=True)
-            for k in range(16):
+            for k in range(4):
                 sums_ref[k, g : g + 1, :] = total[:, :LANES]
                 sums_ref[k, 16 + g : 17 + g, :] = total[:, LANES:]
     count = jnp.sum(cover, 0, keepdims=True)
-    for k in range(16):
+    for k in range(4):
         sums_ref[k, 32:, :] = jnp.zeros((8, LANES), jnp.float32)
         sums_ref[k, 32:33, :HALF] = count
     shape = (64, LANES)
@@ -133,7 +133,7 @@
 
 def attend_kernel(source_ref, cover_ref, sums_ref, asking_ref, lookup_ref, content_ref, part_ref):
     sums = sums_ref[0]
-    for k in range(1, 16):
+    for k in range(1, 4):
         sums = sums + sums_ref[k]
     count = jnp.broadcast_to(sums[32:33, :HALF], (16, HALF))
     shape = (16, HALF)
@@ -565,7 +565,7 @@
             jax.ShapeDtypeStruct((2, 64, 1152), jnp.bfloat16),
             jax.ShapeDtypeStruct((64, 2176), jnp.bfloat16),
             jax.ShapeDtypeStruct((1024, 256), jnp.bfloat16),
-            jax.ShapeDtypeStruct((16, 40, LANES), jnp.float32),
+            jax.ShapeDtypeStruct((4, 40, LANES), jnp.float32),
         ],
         scratch_shapes=[pltpu.VMEM((2048, LANES), jnp.float32)],
         compiler_params=pltpu.CompilerParams(vmem_limit_bytes=ALL_VMEM),
@@ -681,7 +681,11 @@
     )
     right_all = lax.all_gather(right, "row", axis=0, tiled=True)
     left, sums = lax.optimization_barrier((route_left(left), sums))
-    sums = lax.all_to_all(sums, "row", 0, 0, tiled=True)
+    near = [[4 * z + x for x in range(4)] for z in range(4)]
+    far = [[4 * z + x for z in range(4)] for x in range(4)]
+    sums = lax.all_to_all(sums, "row", 0, 0, tiled=True, axis_index_groups=near)
+    sums = jnp.broadcast_to(jnp.sum(sums, 0, keepdims=True), sums.shape)
+    sums = lax.all_to_all(sums, "row", 0, 0, tiled=True, axis_index_groups=far)
     left, sums = lax.optimization_barrier((left, sums))
     parts = attend_call(
         source,

time: 141 us -> 140 us (level)
  waiting for transfers between devices: 25.8 us -> 22.4 us
  blocking collectives: 52.7 us -> 55.1 us
    all_to_all x1 -> x2, blocking collectives: 25.9 us -> 29.7 us  [the longest x1 15.9 us: local(): sums = lax.all_to_all(sums, 'row', 0, 0, tiled=True, axis_index_groups=far)]
    all_gather x1, waiting for transfers between devices: 11.6 us -> 9.55 us  [local(): parts = lax.all_gather(parts, 'row', axis=0, tiled=True)]
    all_to_all x1, blocking collectives: 26.9 us -> 25.4 us  [local(): taken = lax.all_to_all(sides, ('row', 'col'), 0, 0, tiled=True)]
  transfers between devices with their start and end apart: 10 -> 10, of which waited for: 6 -> 6; matrix products, arithmetic and copies ran while one was open for 2% -> 2% of each run, Pallas kernels for 14% -> 15%
where the time goes in v6:
time: 140 us; the launch traced here: 139 us
  blocking collectives  55.1 us (39%)
  Pallas kernels  27.2 us (19%)
  waiting for transfers between devices  22.4 us (16%)
  starting transfers between devices  14.6 us (10%)
  between operations  14.4 us (10%)
  local copies, waits for them, and re-layouts  4.9 us (4%)
    all_to_all x1, blocking collectives, local(): taken = lax.all_to_all(sides, ('row', 'col'), 0, 0, tiled=True)  25.4 us
    all_to_all x1, blocking collectives, local(): sums = lax.all_to_all(sums, 'row', 0, 0, tiled=True, axis_index_groups=far)  15.9 us
    all_to_all x1, blocking collectives, local(): sums = lax.all_to_all(sums, 'row', 0, 0, tiled=True, axis_index_groups=near)  13.7 us
    pallas_call x1, Pallas kernels, pair_call(): pl.pallas_call(pair_kernel, grid=(2,), in_specs=[*by_left(), *by_left(),...  11.9 us
    all_gather x1, waiting for transfers between devices, local(): parts = lax.all_gather(parts, 'row', axis=0, tiled=True)  9.55 us
    ppermute x1, waiting for transfers between devices, ring_of_four(): back = lax.ppermute(block, axis, step(1))  5.3 us
    pallas_call x1, Pallas kernels, project_call(): pl.pallas_call(project_kernel, out_shape=[jax.ShapeDtypeStruct((2, 64, 11...  4.85 us
    all_to_all x1, starting transfers between devices, local(): lax.all_to_all(product.reshape(n_row * n_col, 16, LANES), ('row', 'col'),...  4.77 us
  transfers between devices with their start and end apart: 10, of which 6 were waited for; matrix products, arithmetic and copies ran while one was open for 2% of the time, Pallas kernels for 15%

profile of v6, /device:TPU:0, one launch (start us, length us, event | category | flops | bytes accessed | tf_op | source)
XLA Modules:
  0.0 138.7 jit_solution(17268544006355359328)
XLA Ops:
  7.2 4.8 %project.1 = (bf16[2,64,1152]{2,1,0:T(8,128)(2,1)}, bf16[64,2176]{1,0:T(8,128)(2,1)}, bf16[1024,256]{1,0:T(8,128)(2,1)}, f32[4,40,128]{2,1,0:T(8,128)}) custom-call(bf16[64,4096]{1,0:T(8,128)(2,1)} %msa_ref.3, s32[64,64]{1,0:T(8,128)} %cover_ref.3, f32[1,64]{1,0:T(1,128)} %bitcast.44, f32[1,64]{1,0:T(1,128)} %bitcast.45, bf16[32,64]{1,0:T(8,128)(2,1)} %bitcast.42, ...), custom_call_target="tpu_custom_call" | custom-call | flops 4000000000 | bytes 4000000 | tf_op jit(solution)/shard_map/project/pallas_call | solution.py:562
  12.2 1.1 slice_bitcast_fusion
  13.3 0.7 collective-permute-start
  13.9 1.6 %collective-permute-start.1 = (bf16[64,1152]{1,0:T(8,128)(2,1)S(1)}, bf16[64,1152]{1,0:T(8,128)(2,1)S(1)}, u32[]{:S(2)}, u32[]{:S(2)}) collective-permute-start(bf16[64,1152]{1,0:T(8,128)(2,1)S(1)} %get-tuple-element.34), channel_id=1, source_target_pairs={{0,8},{1,24},{2,46},{3,62},{4,74},{5,90},{6,108},{7,124},{8,0},{9,... | collective-permute-start | bytes 442376 | tf_op jit(solution)/shard_map/ppermute | solution.py:626
  15.6 3.6 %collective-permute-done.1 = bf16[64,1152]{1,0:T(8,128)(2,1)S(1)} collective-permute-done((bf16[64,1152]{1,0:T(8,128)(2,1)S(1)}, bf16[64,1152]{1,0:T(8,128)(2,1)S(1)}, u32[]{:S(2)}, u32[]{:S(2)}) %collective-permute-start.1) | collective-permute-done | bytes 147488 | tf_op jit(solution)/shard_map/ppermute | solution.py:626
  19.2 13.7 %all_to_all.20 = f32[4,40,128]{2,1,0:T(8,128)S(1)} all-to-all(f32[4,40,128]{2,1,0:T(8,128)} %get-tuple-element.22), channel_id=1, replica_groups={{0,8,16,24},{32,40,48,56},{64,72,80,88},{96,104,112,120},{1,9,17,25},{3..., dimensions={0} | all-to-all | bytes 163840 | tf_op jit(solution)/shard_map/all_to_all | solution.py:686
  32.9 15.9 %all_to_all.21.sums_ref = f32[4,40,128]{2,1,0:T(8,128)S(1)} all-to-all(f32[4,40,128]{2,1,0:T(8,128)S(1)} %broadcast_in_dim.2), channel_id=1, replica_groups={{0,32,64,96},{8,40,72,104},{16,48,80,112},{24,56,88,120},{1,33,65,97},{..., dimensions={0} | all-to-all | bytes 163840 | tf_op jit(solution)/shard_map/all_to_all | solution.py:688
  48.9 2.6 %attend.1 = f32[40,512]{1,0:T(8,128)} custom-call(bf16[1024,256]{1,0:T(8,128)(2,1)S(1)} %copy-done.9, s32[64,64]{1,0:T(8,128)S(1)} %copy-done.3, f32[4,40,128]{2,1,0:T(8,128)S(1)} %all_to_all.21.sums_ref, bf16[64,64]{1,0:T(8,128)(2,1)S(1)} %copy-done.4, bf16[8,64]{1,0:T(8,128)(2,1)S(1)} %bitcast.35, bf16[8,64]{1,0:T(8,128)(2,1)S(1)} %bitcast.36), custom_call_target="tpu_custom_call" | custom-call | flops 3000000000 | bytes 3000000 | tf_op jit(solution)/shard_map/attend/pallas_call | solution.py:578
  51.6 1.1 collective-permute-start.2
  52.7 2.8 %collective-permute-start.3 = (bf16[128,1152]{1,0:T(8,128)(2,1)S(1)}, bf16[128,1152]{1,0:T(8,128)(2,1)S(1)}, u32[]{:S(2)}, u32[]{:S(2)}) collective-permute-start(bf16[128,1152]{1,0:T(8,128)(2,1)S(1)} %get-tuple-element.36), channel_id=1, source_target_pairs={{0,6},{1,7},{2,0},{3,1},{4,2},{5,3},{6,4},{7,5},{8,14},{9,15},{10,... | collective-permute-start | bytes 884744 | tf_op jit(solution)/shard_map/ppermute | solution.py:600
  55.5 0.2 copy.30
  55.8 0.1 copy.33.final_ref
  56.3 0.1 copy.34.gain_ref
  56.4 0.1 copy.32
  56.5 5.3 %collective-permute-done.2 = bf16[128,1152]{1,0:T(8,128)(2,1)S(1)} collective-permute-done((bf16[128,1152]{1,0:T(8,128)(2,1)S(1)}, bf16[128,1152]{1,0:T(8,128)(2,1)S(1)}, u32[]{:S(2)}, u32[]{:S(2)}) %collective-permute-start.2) | collective-permute-done | bytes 294944 | tf_op jit(solution)/shard_map/ppermute | solution.py:599
  62.0 3.3 %collective-permute-start.5 = (bf16[64,1152]{1,0:T(8,128)(2,1)S(1)}, bf16[64,1152]{1,0:T(8,128)(2,1)S(1)}, u32[]{:S(2)}, u32[]{:S(2)}) collective-permute-start(bf16[64,1152]{1,0:T(8,128)(2,1)S(1)} %slice.33), channel_id=1, source_target_pairs={{0,6},{1,7},{2,0},{3,1},{4,2},{5,3},{6,4},{7,5},{8,14},{9,15},{10,... | collective-permute-start | bytes 442376 | tf_op jit(solution)/shard_map/ppermute | solution.py:603
  65.3 3.0 %collective-permute-done.4 = bf16[64,1152]{1,0:T(8,128)(2,1)S(1)} collective-permute-done((bf16[64,1152]{1,0:T(8,128)(2,1)S(1)}, bf16[64,1152]{1,0:T(8,128)(2,1)S(1)}, u32[]{:S(2)}, u32[]{:S(2)}) %collective-permute-start.4) | collective-permute-done | bytes 147488 | tf_op jit(solution)/shard_map/ppermute | solution.py:602
  68.7 1.4 prepare.1.base_ref
  70.1 1.0 copy-done.10
  71.1 0.3 collective-permute-done.6.other_a_ref.other_b_ref.other_mask_ref
  71.4 11.9 %pair.1 = (f32[16,128,128]{2,1,0:T(8,128)S(1)}, bf16[16,128,128]{2,1,0:T(8,128)(2,1)S(1)}, bf16[128,32,128]{2,1,0:T(8,128)(2,1)S(1)}) custom-call(bf16[512,1152]{1,0:T(8,128)(2,1)} %copy-done.15, bf16[512,1152]{1,0:T(8,128)(2,1)} %copy-done.15, bf16[512,1152]{1,0:T(8,128)(2,1)} %copy-done.15, ...), custom_call_target="tpu_custom_call" | custom-call | flops 16000000000 | bytes 16000000 | tf_op jit(solution)/shard_map/pair/pallas_call | solution.py:488
  83.3 25.4 %all_to_all.22 = bf16[128,32,128]{2,1,0:T(8,128)(2,1)S(1)} all-to-all(bf16[128,32,128]{2,1,0:T(8,128)(2,1)S(1)} %get-tuple-element.31), channel_id=1, replica_groups=mesh['row'=16,'col'=8] {'row','col'}, dimensions={0} | all-to-all | bytes 2097152 | tf_op jit(solution)/shard_map/all_to_all | solution.py:730
  108.7 1.6 %triangle.1 = bf16[16,8,16,128]{3,2,1,0:T(8,128)(2,1)} custom-call(bf16[16,8,32,128]{3,2,1,0:T(8,128)(2,1)S(1)} %bitcast.29), custom_call_target="tpu_custom_call" | custom-call | flops 2000000000 | bytes 2000000 | tf_op jit(solution)/shard_map/triangle/pallas_call | solution.py:519
  110.3 4.8 %all-to-all-start.3 = ((bf16[128,16,128]{2,1,0:T(8,128)(2,1)}), bf16[128,16,128]{2,1,0:T(8,128)(2,1)S(1)}, u32[]{:S(2)}, u32[]{:S(2)}) async-start(bf16[128,16,128]{2,1,0:T(8,128)(2,1)} %bitcast.15), calls=%async_computation.3 | async-start | bytes 1048576 | tf_op jit(solution)/shard_map/all_to_all | solution.py:732
  115.2 0.1 copy.36
  115.3 0.1 copy.37.gain_ref
  115.5 9.6 %all-gather.3.cloned.1.call-done.part_ref = f32[640,512]{1,0:T(8,128)} async-done(((f32[40,512]{1,0:T(8,128)}), f32[640,512]{1,0:T(8,128)}) %all-gather.3.cloned.1.call-update) | async-done | bytes 1310736 | tf_op jit(solution)/shard_map/all_gather | solution.py:700
  125.0 1.3 copy-done
  126.3 1.9 %refresh.1 = bf16[64,4096]{1,0:T(8,128)(2,1)} custom-call(f32[640,512]{1,0:T(8,128)S(1)} %copy-done, bf16[1024,256]{1,0:T(8,128)(2,1)S(1)} %copy-done.9, bf16[64,4096]{1,0:T(8,128)(2,1)S(1)} %copy-done.2, bf16[64,64]{1,0:T(8,128)(2,1)S(1)} %copy-done.5, bf16[64,64]{1,0:T(8,128)(2,1)S(1)} %copy-done.6), custom_call_target="tpu_custom_call" | custom-call | flops 2000000000 | bytes 2000000 | tf_op jit(solution)/shard_map/refresh/pallas_call | solution.py:588
  128.3 0.8 gate.1.gate_ref
  129.1 0.6 all-to-all-done.3.product_ref
  129.7 2.2 %finish.1 = f32[2,16,64,128]{3,2,1,0:T(8,128)} custom-call(bf16[128,16,128]{2,1,0:T(8,128)(2,1)S(1)} %all-to-all-done.3.product_ref, f32[16,128,128]{2,1,0:T(8,128)S(1)} %get-tuple-element.32.mid_ref, f32[16,128,128]{2,1,0:T(8,128)S(1)} %gate.1.gate_ref, bf16[128,128]{1,0:T(8,128)(2,1)S(1)} %bitcast.32, f32[128,1]{1,0:T(8,128)S(1)} %copy.37.gain_ref), custom_call_target="tpu_custom_call" | custom-call | flops 3000000000 | bytes 3000000 | tf_op jit(solution)/shard_map/finish/pallas_call | solution.py:542
  (71 shorter events, 1.2 us)
Async XLA Ops:
  7.2 64.2 %all-gather.5.cloned.1.call-start = ((), (), s32[]{:S(2)}) async-start(), calls=%async_computation.5 | async-start | bytes 4734976 | tf_op jit(solution)/shard_map/all_gather | solution.py:682
  12.1 36.8 %copy-start.3 = (s32[64,64]{1,0:T(8,128)S(1)}, s32[64,64]{1,0:T(8,128)}, u32[]{:S(2)}) copy-start(s32[64,64]{1,0:T(8,128)} %cover_ref.3) | copy-start | bytes 49156
  12.1 36.8 %copy-start.4 = (bf16[64,64]{1,0:T(8,128)(2,1)S(1)}, bf16[64,64]{1,0:T(8,128)(2,1)}, u32[]{:S(2)}) copy-start(bf16[64,64]{1,0:T(8,128)(2,1)} %asking_ref.1) | copy-start | bytes 24580
  12.1 36.8 %copy-start.7 = (bf16[64,8]{0,1:T(8,128)(2,1)S(1)}, bf16[64,8]{0,1:T(8,128)(2,1)}, u32[]{:S(2)}) copy-start(bf16[64,8]{0,1:T(8,128)(2,1)} %param.28) | copy-start | bytes 3076
  12.1 36.8 %copy-start.8 = (bf16[64,8]{0,1:T(8,128)(2,1)S(1)}, bf16[64,8]{0,1:T(8,128)(2,1)}, u32[]{:S(2)}) copy-start(bf16[64,8]{0,1:T(8,128)(2,1)} %param.29) | copy-start | bytes 3076
  12.1 36.8 %copy-start.9 = (bf16[1024,256]{1,0:T(8,128)(2,1)S(1)}, bf16[1024,256]{1,0:T(8,128)(2,1)}, u32[]{:S(2)}) copy-start(bf16[1024,256]{1,0:T(8,128)(2,1)} %get-tuple-element.25.source_ref) | copy-start | bytes 1572868
  12.1 112.9 %all-gather.3.cloned.1.call-start = ((), (), s32[]{:S(2)}) async-start(), calls=%async_computation.4 | async-start | bytes 1392640 | tf_op jit(solution)/shard_map/all_gather | solution.py:700
  13.3 2.3 %collective-permute-start = (bf16[64,1152]{1,0:T(8,128)(2,1)S(1)}, bf16[64,1152]{1,0:T(8,128)(2,1)S(1)}, u32[]{:S(2)}, u32[]{:S(2)}) collective-permute-start(bf16[64,1152]{1,0:T(8,128)(2,1)S(1)} %get-tuple-element.35), channel_id=1, source_target_pairs={{0,0},{1,16},{2,38},{3,54},{4,66},{5,82},{6,100},{7,116},{8,8},{9,... | collective-permute-start | bytes 442376 | tf_op jit(solution)/shard_map/ppermute | solution.py:626
  13.9 5.2 %collective-permute-start.1 = (bf16[64,1152]{1,0:T(8,128)(2,1)S(1)}, bf16[64,1152]{1,0:T(8,128)(2,1)S(1)}, u32[]{:S(2)}, u32[]{:S(2)}) collective-permute-start(bf16[64,1152]{1,0:T(8,128)(2,1)S(1)} %get-tuple-element.34), channel_id=1, source_target_pairs={{0,8},{1,24},{2,46},{3,62},{4,74},{5,90},{6,108},{7,124},{8,0},{9,... | collective-permute-start | bytes 442376 | tf_op jit(solution)/shard_map/ppermute | solution.py:626
  48.9 6.7 %copy-start.11 = (bf16[1024,128]{1,0:T(8,128)(2,1)S(1)}, bf16[1024,128]{1,0:T(8,128)(2,1)}, u32[]{:S(2)}) copy-start(bf16[1024,128]{1,0:T(8,128)(2,1)} %param.35) | copy-start | bytes 786436
  51.5 4.5 %copy-start.20 = (s32[512]{0:T(512)S(1)}, s32[512]{0:T(512)}, u32[]{:S(2)}) copy-start(s32[512]{0:T(512)} %param.25) | copy-start | bytes 6148
  51.5 4.7 %copy-start.17 = (f32[2,128]{1,0:T(2,128)S(1)}, f32[2,128]{1,0:T(2,128)}, u32[]{:S(2)}) copy-start(f32[2,128]{1,0:T(2,128)} %param.36) | copy-start | bytes 3076
  51.5 4.8 %copy-start.16 = (s32[32,64]{1,0:T(8,128)S(1)}, s32[32,64]{1,0:T(8,128)}, u32[]{:S(2)}) copy-start(s32[32,64]{1,0:T(8,128)} %param.24) | copy-start | bytes 24580
  51.5 4.8 %copy-start.18 = (f32[128]{0:T(128)S(1)}, f32[128]{0:T(128)}, u32[]{:S(2)}) copy-start(f32[128]{0:T(128)} %param.37) | copy-start | bytes 1540
  51.5 4.9 %copy-start.12 = (bf16[128,512]{1,0:T(8,128)(2,1)S(1)}, bf16[128,512]{1,0:T(8,128)(2,1)}, u32[]{:S(2)}) copy-start(bf16[128,512]{1,0:T(8,128)(2,1)} %param.38) | copy-start | bytes 393220
  51.6 10.3 %collective-permute-start.2 = (bf16[128,1152]{1,0:T(8,128)(2,1)S(1)}, bf16[128,1152]{1,0:T(8,128)(2,1)S(1)}, u32[]{:S(2)}, u32[]{:S(2)}) collective-permute-start(bf16[128,1152]{1,0:T(8,128)(2,1)S(1)} %get-tuple-element.36), channel_id=1, source_target_pairs={{0,2},{1,3},{2,4},{3,5},{4,6},{5,7},{6,0},{7,1},{8,10},{9,11},{10,... | collective-permute-start | bytes 884744 | tf_op jit(solution)/shard_map/ppermute | solution.py:599
  52.7 9.2 %collective-permute-start.3 = (bf16[128,1152]{1,0:T(8,128)(2,1)S(1)}, bf16[128,1152]{1,0:T(8,128)(2,1)S(1)}, u32[]{:S(2)}, u32[]{:S(2)}) collective-permute-start(bf16[128,1152]{1,0:T(8,128)(2,1)S(1)} %get-tuple-element.36), channel_id=1, source_target_pairs={{0,6},{1,7},{2,0},{3,1},{4,2},{5,3},{6,4},{7,5},{8,14},{9,15},{10,... | collective-permute-start | bytes 884744 | tf_op jit(solution)/shard_map/ppermute | solution.py:600
  56.5 12.2 %copy-start.1 = (f32[32,64,128]{2,1,0:T(8,128)S(1)}, f32[32,64,128]{2,1,0:T(8,128)}, u32[]{:S(2)}) copy-start(f32[32,64,128]{2,1,0:T(8,128)} %param.23) | copy-start | bytes 3145732
  61.9 6.4 %collective-permute-start.4 = (bf16[64,1152]{1,0:T(8,128)(2,1)S(1)}, bf16[64,1152]{1,0:T(8,128)(2,1)S(1)}, u32[]{:S(2)}, u32[]{:S(2)}) collective-permute-start(bf16[64,1152]{1,0:T(8,128)(2,1)S(1)} %slice.32), channel_id=1, source_target_pairs={{0,2},{1,3},{2,4},{3,5},{4,6},{5,7},{6,0},{7,1},{8,10},{9,11},{10,... | collective-permute-start | bytes 442376 | tf_op jit(solution)/shard_map/ppermute | solution.py:602
  62.0 6.3 %collective-permute-start.5 = (bf16[64,1152]{1,0:T(8,128)(2,1)S(1)}, bf16[64,1152]{1,0:T(8,128)(2,1)S(1)}, u32[]{:S(2)}, u32[]{:S(2)}) collective-permute-start(bf16[64,1152]{1,0:T(8,128)(2,1)S(1)} %slice.33), channel_id=1, source_target_pairs={{0,6},{1,7},{2,0},{3,1},{4,2},{5,3},{6,4},{7,5},{8,14},{9,15},{10,... | collective-permute-start | bytes 442376 | tf_op jit(solution)/shard_map/ppermute | solution.py:603
  68.3 1.7 %copy-start.15 = (bf16[512,1152]{1,0:T(8,128)(2,1)}, bf16[512,1152]{1,0:T(8,128)(2,1)S(1)}, u32[]{:S(2)}) copy-start(bf16[512,1152]{1,0:T(8,128)(2,1)S(1)} %constant_dynamic-update-slice_fusion.2.own_a_ref.own_b_ref.own_mask_ref) | copy-start | bytes 3538948
  68.3 3.1 %collective-permute-start.6 = (bf16[512,1152]{1,0:T(8,128)(2,1)S(1)}, bf16[512,1152]{1,0:T(8,128)(2,1)}, u32[]{:S(2)}, u32[]{:S(2)}) collective-permute-start(bf16[512,1152]{1,0:T(8,128)(2,1)S(1)} %constant_dynamic-update-slice_fusion.2.own_a_ref.own_b_ref.own_mask_ref), channel_id=1, source_target_pairs={{0,1},{1,0},{2,3},{3,2},{4,5},{5,4},{6,7},{7,6},{8,9},{9,8},{10,11... | collective-permute-start | bytes 3538952 | tf_op jit(solution)/shard_map/ppermute | solution.py:636
  70.1 1.0 copy-start.10
  108.7 6.4 %copy-start.13 = (bf16[128,128]{1,0:T(8,128)(2,1)S(1)}, bf16[128,128]{1,0:T(8,128)(2,1)}, u32[]{:S(2)}) copy-start(bf16[128,128]{1,0:T(8,128)(2,1)} %param.39) | copy-start | bytes 98308
  108.7 6.5 %copy-start.14 = (bf16[128,128]{1,0:T(8,128)(2,1)S(1)}, bf16[128,128]{1,0:T(8,128)(2,1)}, u32[]{:S(2)}) copy-start(bf16[128,128]{1,0:T(8,128)(2,1)} %param.41) | copy-start | bytes 98308
  110.3 5.0 %copy-start.19 = (f32[128]{0:T(128)S(1)}, f32[128]{0:T(128)}, u32[]{:S(2)}) copy-start(f32[128]{0:T(128)} %param.40) | copy-start | bytes 1540
  110.3 14.7 %copy-start.2 = (bf16[64,4096]{1,0:T(8,128)(2,1)S(1)}, bf16[64,4096]{1,0:T(8,128)(2,1)}, u32[]{:S(2)}) copy-start(bf16[64,4096]{1,0:T(8,128)(2,1)} %msa_ref.3) | copy-start | bytes 1572868
  110.3 14.7 %copy-start.5 = (bf16[64,64]{1,0:T(8,128)(2,1)S(1)}, bf16[64,64]{1,0:T(8,128)(2,1)}, u32[]{:S(2)}) copy-start(bf16[64,64]{1,0:T(8,128)(2,1)} %sigmoid_ref.1) | copy-start | bytes 24580
  110.3 14.7 %copy-start.6 = (bf16[64,64]{1,0:T(8,128)(2,1)S(1)}, bf16[64,64]{1,0:T(8,128)(2,1)}, u32[]{:S(2)}) copy-start(bf16[64,64]{1,0:T(8,128)(2,1)} %final_ref.1) | copy-start | bytes 24580
  110.3 19.4 %all-to-all-start.3 = ((bf16[128,16,128]{2,1,0:T(8,128)(2,1)}), bf16[128,16,128]{2,1,0:T(8,128)(2,1)S(1)}, u32[]{:S(2)}, u32[]{:S(2)}) async-start(bf16[128,16,128]{2,1,0:T(8,128)(2,1)} %bitcast.15), calls=%async_computation.3 | async-start | bytes 1048576 | tf_op jit(solution)/shard_map/all_to_all | solution.py:732
  125.0 1.3 copy-start
Sparse Core Ops, SparseCore 0:
  12.2 55.9 all-gather.4
  71.2 53.7 all-gather.2
